TPU v7x, 512 devices: a whole 4x4x16 slice. The times are simulated.
512 devices in a mesh: gx: 64 (over x, z), gz: 8 (over y, core).
Axes of the slice: x: 4, y: 4, z: 16, core: 2. Of those that a mesh axis runs over, the one named last changes fastest.
Arguments:
- velocity: float32 [2048, 64, 1024], P('gx', None, 'gz'), may hold values from -6 to 6
- register: float32 [2048, 64, 1024], P('gx', None, 'gz'), may hold values from -6 to 6
- eddy_viscosity: bfloat16 [2048, 64, 1024], P('gx', None, 'gz'), may hold values from 0.019897461 to 0.19921875
- courant: float32 [2048], P('gx'), may hold values from 200 to 20000
- inflow: float32 [64, 1024], P(None, 'gz'), may hold values from 0.5 to 1.5
Outputs:
- new_velocity: float32 [2048, 64, 1024], P('gx', None, 'gz')
- new_register: float32 [2048, 64, 1024], P('gx', None, 'gz')
All inputs are finite; a program needn't handle non-finite values.
Results may differ from a plain program's by a relative error of at most 0.0017.
The roundings to bfloat16 on the way count: a program that leaves them out, or rounds other values in their place, can miss the bound.
Values may be sent and summed in bfloat16 or wider, within the bound.
No kernel may reach another device: no remote copies, remote signals or barrier semaphores. Data moves between devices by JAX's collectives and lax.ppermute only.
A program may use at most 64 MiB of HBM per device.

v0:
```python
import math

import jax
import jax.numpy as jnp
import numpy as np
from jax import lax
from jax.experimental import pallas as pl
from jax.experimental.pallas import tpu as pltpu
from jax.sharding import PartitionSpec as P

coef_zero = -49.0 / 18.0
coef_one = 1.5
coef_two = -3.0 / 20.0
coef_three = 1.0 / 90.0
decay = -5.0 / 9.0
weight = 15.0 / 16.0

STATIONS, NY, WIDTH, PARTS = 32, 64, 128, 8
LENGTH = WIDTH * PARTS
ROWS = STATIONS * NY // PARTS
VMEM_LIMIT = 16 * 1024 * 1024
F32, BF16 = jnp.float32, jnp.bfloat16
PAYLOAD = NY + 16

GROUPS = (
    [[x * 16 + h * 4 + l for l in range(4)] for x in range(4) for h in range(4)],
    [[x * 16 + h * 4 + l for h in range(4)] for x in range(4) for l in range(4)],
    [[x * 16 + z for x in range(4)] for z in range(16)],
)


def span_tables():
    position = np.arange(LENGTH, dtype=np.int64)
    product = position[:, None] * position[None, 1 : LENGTH // 2 + 1] % LENGTH
    angle = product.astype(np.float32) * np.float32(2.0 * math.pi / LENGTH)
    table = np.concatenate([np.cos(angle), np.sin(angle)], axis=1).astype(BF16)
    wave = np.arange(1, LENGTH // 2 + 1).astype(np.float32) * np.float32(2.0 * math.pi / LENGTH)
    factor = -(wave * wave) / np.float32(LENGTH)
    twice = np.where(np.arange(1, LENGTH // 2 + 1) < LENGTH // 2, 2.0, 1.0).astype(np.float32)
    factor = np.concatenate([factor * twice] * 2)[None, :].astype(np.float32)
    return table, factor


def stencil_kernel(keep, take, velocity, register, eddy, low, high, base, offset):
    def plane(i):
        if i < 0:
            return low[i + 3].astype(F32)
        if i >= STATIONS:
            return high[i - STATIONS].astype(F32)
        return velocity[i]

    running = jnp.zeros((NY, WIDTH), F32)
    for i in range(STATIONS):
        here = velocity[i]
        total = (2.0 * coef_zero) * here
        for shift, coef in ((1, coef_one), (2, coef_two), (3, coef_three)):
            along = plane(i - shift) + plane(i + shift)
            across = pltpu.roll(here, shift, 0) + pltpu.roll(here, NY - shift, 0)
            total = total + coef * (along + across)
        part = decay * register[i] + eddy[i].astype(F32) * total
        base[i] = part
        running = keep[i] * running + take[i] * (here + weight * part)
    offset[...] = running


def span_kernel(lines, table, factor, out, scaled):
    whole = jnp.concatenate([lines[b] for b in range(PARTS)], axis=1)
    step = 256
    for n in range(LENGTH // step):
        cut = slice(n * step, (n + 1) * step)
        part = jnp.dot(whole, table[:, cut], preferred_element_type=F32)
        scaled[:, cut] = (part * factor[:, cut]).astype(BF16)
    for n in range(LENGTH // step):
        part = lax.dot_general(
            scaled[...],
            table[n * step : (n + 1) * step, :],
            (((1,), (1,)), ((), ())),
            preferred_element_type=F32,
        ).astype(BF16)
        for b in range(step // WIDTH):
            out[n * step // WIDTH + b] = part[:, b * WIDTH : (b + 1) * WIDTH]


def store_payload(out, plane, gain):
    upper = gain.astype(BF16).astype(F32)
    tail = jnp.concatenate([upper, gain - upper], axis=0).astype(BF16)
    plane = plane.astype(BF16)
    for m in range(4):
        out[m, 0:NY] = plane
        out[m, NY:PAYLOAD] = tail


def offset_kernel(keep, take, second, eddy, base_offset, out):
    running = jnp.zeros((NY, WIDTH), F32)
    gain = jnp.ones((8, WIDTH), F32)
    for i in range(STATIONS):
        term = eddy[i].astype(F32) * second[i].astype(F32)
        running = keep[i] * running + (take[i] * weight) * term
        gain = gain * keep[i]
    store_payload(out, running + base_offset[...], gain)


def local_kernel(keep, take, velocity, base, eddy, second, _, register, local):
    running = jnp.zeros((NY, WIDTH), F32)
    for i in range(STATIONS):
        new = base[i] + eddy[i].astype(F32) * second[i].astype(F32)
        register[i] = new
        running = keep[i] * running + take[i] * (velocity[i] + weight * new)
        local[i] = running


def fold(place, received):
    total = jnp.zeros((NY, WIDTH), F32)
    gain = jnp.ones((8, WIDTH), F32)
    before, gain_before = total, gain
    for m in range(4):
        reached = place == m
        before = jnp.where(reached, total, before)
        gain_before = jnp.where(reached, gain, gain_before)
        tail = received[m, NY:PAYLOAD].astype(F32)
        one = tail[0:8] + tail[8:16]
        total = total * one[0:1] + received[m, 0:NY].astype(F32)
        gain = gain * one
    return before, gain_before, total, gain


def fold_kernel(place, received, before, gain_before, out):
    one, two, total, gain = fold(place[0], received)
    before[...] = one
    gain_before[...] = two
    store_payload(out, total, gain)


def final_kernel(place, keep, received, before1, gain1, before2, gain2, inflow, local, out, entering):
    step = pl.program_id(0)
    count = out.shape[0]

    @pl.when(step == 0)
    def _():
        before, gain, _, _ = fold(place[0], received)
        value = before + gain[0:1] * inflow[...]
        value = before2[...] + gain2[0:1] * value
        entering[...] = before1[...] + gain1[0:1] * value

    running = entering[...]
    for i in range(count):
        running = running * keep[step * count + i]
        out[i] = local[i] + running
    entering[...] = running


SMEM = pl.BlockSpec(memory_space=pltpu.SMEM)
VMEM = pl.BlockSpec(memory_space=pltpu.VMEM)
ANY = pl.BlockSpec(memory_space=pl.ANY)
CUBE = jax.ShapeDtypeStruct((STATIONS, NY, WIDTH), F32)
PLANE = jax.ShapeDtypeStruct((NY, WIDTH), F32)
GAIN = jax.ShapeDtypeStruct((8, WIDTH), F32)
SLOTS = jax.ShapeDtypeStruct((4, PAYLOAD, WIDTH), BF16)


def call(kernel, name, in_specs, out_shape, flops, bytes_accessed, scratch=()):
    many = isinstance(out_shape, tuple)
    return pl.pallas_call(
        kernel,
        name=name,
        in_specs=in_specs,
        out_specs=tuple(VMEM for _ in out_shape) if many else VMEM,
        out_shape=out_shape,
        scratch_shapes=scratch,
        compiler_params=pltpu.CompilerParams(vmem_limit_bytes=VMEM_LIMIT),
        cost_estimate=pl.CostEstimate(flops=flops, bytes_accessed=bytes_accessed, transcendentals=0),
    )


def body(velocity, register, eddy_viscosity, courant, inflow):
    table, factor = span_tables()
    place = lax.axis_index("gx")
    places = [jnp.reshape(p, (1,)) for p in (place % 4, place // 4 % 4, place // 16)]
    keep = courant / (1.0 + courant)
    take = 1.0 / (1.0 + courant)

    rounded = velocity.astype(BF16)
    lines = lax.all_to_all(rounded.reshape(PARTS, ROWS, WIDTH), "gz", 0, 0, tiled=True)

    count = lax.axis_size("gx")
    forward = [(i, i + 1) for i in range(count - 1)]
    backward = [(b, a) for a, b in forward]
    low = lax.ppermute(rounded[STATIONS - 3 :], "gx", forward)
    high = lax.ppermute(rounded[:3], "gx", backward)
    base, base_offset = call(
        stencil_kernel, "stencil", [SMEM, SMEM] + [VMEM] * 5, (CUBE, PLANE), 8_000_000, 4_000_000
    )(keep, take, velocity, register, eddy_viscosity, low, high)

    derived = call(
        span_kernel,
        "span",
        [VMEM, VMEM, VMEM],
        jax.ShapeDtypeStruct((PARTS, ROWS, WIDTH), BF16),
        4 * ROWS * LENGTH * LENGTH,
        3_200_000,
        (pltpu.VMEM((ROWS, LENGTH), BF16),),
    )(lines, jnp.asarray(table), jnp.asarray(factor))
    second = lax.all_to_all(derived, "gz", 0, 0, tiled=True).reshape(STATIONS, NY, WIDTH)

    payload = call(offset_kernel, "offset", [SMEM, SMEM] + [VMEM] * 3, SLOTS, 1_500_000, 1_100_000)(
        keep, take, second, eddy_viscosity, base_offset
    )
    new_register, local = call(
        local_kernel, "local", [SMEM, SMEM] + [VMEM] * 4 + [ANY], (CUBE, CUBE), 3_000_000, 5_000_000
    )(keep, take, velocity, base, eddy_viscosity, second, payload)

    found = []
    for level in range(3):
        payload = lax.all_to_all(payload, "gx", 0, 0, axis_index_groups=GROUPS[level], tiled=True)
        if level < 2:
            before, gain, payload = call(
                fold_kernel, "fold", [SMEM, VMEM], (PLANE, GAIN, SLOTS), 200_000, 300_000
            )(places[level], payload)
            found += [before, gain]

    chunk = 8
    whole = lambda *shape: pl.BlockSpec(shape, lambda i: (0,) * len(shape))
    cube = pl.BlockSpec((chunk, NY, WIDTH), lambda i: (i, 0, 0))
    new_velocity = pl.pallas_call(
        final_kernel,
        name="final",
        grid=(STATIONS // chunk,),
        in_specs=[SMEM, SMEM, whole(4, PAYLOAD, WIDTH)]
        + [whole(NY, WIDTH), whole(8, WIDTH)] * 2
        + [whole(NY, WIDTH), cube],
        out_specs=cube,
        out_shape=CUBE,
        scratch_shapes=[pltpu.VMEM((NY, WIDTH), F32)],
        compiler_params=pltpu.CompilerParams(vmem_limit_bytes=VMEM_LIMIT),
        cost_estimate=pl.CostEstimate(flops=800_000, bytes_accessed=2_300_000, transcendentals=0),
    )(places[2], keep, payload, *found, inflow, local)
    return new_velocity, new_register


def solution(mesh):
    return jax.shard_map(
        body,
        mesh=mesh,
        in_specs=(
            P("gx", None, "gz"),
            P("gx", None, "gz"),
            P("gx", None, "gz"),
            P("gx"),
            P(None, "gz"),
        ),
        out_specs=(P("gx", None, "gz"), P("gx", None, "gz")),
        check_vma=False,
    )
```

profile of v0, /device:TPU:8, one launch (start us, length us, event | category | flops | bytes accessed | tf_op | source)
XLA Modules:
  0.0 89.7 jit_solution(6849061899219238368)
XLA Ops:
  0.6 0.0 copy-start.10
  0.6 0.0 copy-start.9
  0.7 1.5 %convert_element_type.3 = bf16[32,64,128]{2,1,0:T(8,128)(2,1)S(1)} convert(f32[32,64,128]{2,1,0:T(8,128)} %velocity.3) | non-fusion elementwise | flops 262144 | bytes 1572864 | tf_op jit(solution)/shard_map/convert_element_type | solution.py:182
  2.1 0.0 copy-start.11
  2.1 0.8 copy-done.11
  2.9 17.2 %all_to_all.25.lines = bf16[8,256,128]{2,1,0:T(8,128)(2,1)S(1)} all-to-all(bf16[8,256,128]{2,1,0:T(8,128)(2,1)S(1)} %bitcast.7), channel_id=1, replica_groups=mesh['gx'=64,'gz'=8] {'gz'}, dimensions={0} | all-to-all | bytes 1048576 | tf_op jit(solution)/shard_map/all_to_all | solution.py:183
  20.1 0.0 copy-start.1
  20.1 0.0 copy-start.2
  20.1 1.3 %span.1 = bf16[8,256,128]{2,1,0:T(8,128)(2,1)S(1)} custom-call(bf16[8,256,128]{2,1,0:T(8,128)(2,1)S(1)} %all_to_all.25.lines, bf16[1024,1024]{1,0:T(8,128)(2,1)S(1)} %copy-done.9, f32[1,1024]{1,0:T(1,128)S(1)} %copy-done.10), custom_call_target="tpu_custom_call" | custom-call | flops 1073741824 | bytes 3200000 | tf_op jit(solution)/shard_map/span/pallas_call | solution.py:194
  21.4 0.0 copy-start.7
  21.4 0.8 copy-done.7
  22.2 4.9 %all-to-all-start.1 = ((bf16[8,256,128]{2,1,0:T(8,128)(2,1)}), bf16[8,256,128]{2,1,0:T(8,128)(2,1)S(1)}, u32[]{:S(2)}, u32[]{:S(2)}) async-start(bf16[8,256,128]{2,1,0:T(8,128)(2,1)} %copy-done.7), calls=%async_computation.1 | async-start | bytes 1048576 | tf_op jit(solution)/shard_map/all_to_all | solution.py:203
  27.0 0.8 fusion
  27.9 1.3 %collective-permute-start.1 = (bf16[3,64,128]{2,1,0:T(8,128)(2,1)S(1)}, bf16[3,64,128]{2,1,0:T(8,128)(2,1)S(1)}, u32[]{:S(2)}, u32[]{:S(2)}) collective-permute-start(bf16[3,64,128]{2,1,0:T(8,128)(2,1)S(1)} %get-tuple-element.22), channel_id=1, source_target_pairs={{8,0},{16,8},{24,16},{32,24},{40,32},{48,40},{56,48},{64,56},{72,6... | collective-permute-start | bytes 147464 | tf_op jit(solution)/shard_map/ppermute | solution.py:189
  29.2 4.5 %collective-permute-start = (bf16[3,64,128]{2,1,0:T(8,128)(2,1)S(1)}, bf16[3,64,128]{2,1,0:T(8,128)(2,1)S(1)}, u32[]{:S(2)}, u32[]{:S(2)}) collective-permute-start(bf16[3,64,128]{2,1,0:T(8,128)(2,1)S(1)} %get-tuple-element.23), channel_id=1, source_target_pairs={{0,8},{8,16},{16,24},{24,32},{32,40},{40,48},{48,56},{56,64},{64,7... | collective-permute-start | bytes 147464 | tf_op jit(solution)/shard_map/ppermute | solution.py:188
  33.7 0.1 collective-permute-done.1.high
  33.8 1.6 %collective-permute-done.low = bf16[3,64,128]{2,1,0:T(8,128)(2,1)S(1)} collective-permute-done((bf16[3,64,128]{2,1,0:T(8,128)(2,1)S(1)}, bf16[3,64,128]{2,1,0:T(8,128)(2,1)S(1)}, u32[]{:S(2)}, u32[]{:S(2)}) %collective-permute-start) | collective-permute-done | bytes 49184 | tf_op jit(solution)/shard_map/ppermute | solution.py:188
  35.5 1.8 %stencil.1 = (f32[32,64,128]{2,1,0:T(8,128)S(1)}, f32[64,128]{1,0:T(8,128)S(1)}) custom-call(f32[32]{0:T(128)S(1)} %get-tuple-element.25.keep, f32[32]{0:T(128)S(1)} %get-tuple-element.24.take, f32[32,64,128]{2,1,0:T(8,128)S(1)} %copy-done, f32[32,64,128]{2,1,0:T(8,128)S(1)} %copy-done.2, bf16[32,64,128]{2,1,0:T(8,128)(2,1)S(1)} %copy-done.1, ...), custom_call_target="tpu_custom_call" | custom-call | flops 8000000 | bytes 4000000 | tf_op jit(solution)/shard_map/stencil/pallas_call | solution.py:190
  37.3 1.0 %copy-done.3 = f32[32,64,128]{2,1,0:T(8,128)} copy-done((f32[32,64,128]{2,1,0:T(8,128)}, f32[32,64,128]{2,1,0:T(8,128)S(1)}, u32[]{:S(2)}) %copy-start.3) | copy-done | bytes 1048600
  38.3 1.4 %offset.1._ = bf16[4,80,128]{2,1,0:T(8,128)(2,1)} custom-call(f32[32]{0:T(128)S(1)} %get-tuple-element.25.keep, f32[32]{0:T(128)S(1)} %get-tuple-element.24.take, bf16[32,64,128]{2,1,0:T(8,128)(2,1)S(1)} %bitcast.5, bf16[32,64,128]{2,1,0:T(8,128)(2,1)S(1)} %copy-done.1, f32[64,128]{1,0:T(8,128)S(1)} %get-tuple-element.12.base_offset), custom_call_target="tpu_custom_call" | custom-call | flops 1500000 | bytes 1100000 | tf_op jit(solution)/shard_map/offset/pallas_call | solution.py:205
  39.7 3.7 %all-to-all-start.2 = ((bf16[4,80,128]{2,1,0:T(8,128)(2,1)}), bf16[4,80,128]{2,1,0:T(8,128)(2,1)S(1)}, u32[]{:S(2)}, u32[]{:S(2)}) async-start(bf16[4,80,128]{2,1,0:T(8,128)(2,1)} %offset.1._), calls=%async_computation.2 | async-start | bytes 163840 | tf_op jit(solution)/shard_map/all_to_all | solution.py:214
  43.4 5.8 %all-to-all-done.2.received = bf16[4,80,128]{2,1,0:T(8,128)(2,1)S(1)} async-done(((bf16[4,80,128]{2,1,0:T(8,128)(2,1)}), bf16[4,80,128]{2,1,0:T(8,128)(2,1)S(1)}, u32[]{:S(2)}, u32[]{:S(2)}) %all-to-all-start.2) | async-done | bytes 81952 | tf_op jit(solution)/shard_map/all_to_all | solution.py:214
  49.2 0.7 fold.2
  49.9 12.9 %all-to-all-start.3 = ((bf16[4,80,128]{2,1,0:T(8,128)(2,1)}), bf16[4,80,128]{2,1,0:T(8,128)(2,1)S(1)}, u32[]{:S(2)}, u32[]{:S(2)}) async-start(bf16[4,80,128]{2,1,0:T(8,128)(2,1)} %get-tuple-element.13), calls=%async_computation.3 | async-start | bytes 163840 | tf_op jit(solution)/shard_map/all_to_all | solution.py:214
  62.8 12.9 %all-to-all-done.3.received = bf16[4,80,128]{2,1,0:T(8,128)(2,1)S(1)} async-done(((bf16[4,80,128]{2,1,0:T(8,128)(2,1)}), bf16[4,80,128]{2,1,0:T(8,128)(2,1)S(1)}, u32[]{:S(2)}, u32[]{:S(2)}) %all-to-all-start.3) | async-done | bytes 81952 | tf_op jit(solution)/shard_map/all_to_all | solution.py:214
  75.7 0.7 fold.3
  76.3 4.3 %all-to-all-start.4 = ((bf16[4,80,128]{2,1,0:T(8,128)(2,1)}), bf16[4,80,128]{2,1,0:T(8,128)(2,1)S(1)}, u32[]{:S(2)}, u32[]{:S(2)}) async-start(bf16[4,80,128]{2,1,0:T(8,128)(2,1)} %get-tuple-element.14), calls=%async_computation.4 | async-start | bytes 163840 | tf_op jit(solution)/shard_map/all_to_all | solution.py:214
  80.6 1.8 %local.1 = (f32[32,64,128]{2,1,0:T(8,128)}, f32[32,64,128]{2,1,0:T(8,128)S(1)}) custom-call(f32[32]{0:T(128)S(1)} %get-tuple-element.25.keep, f32[32]{0:T(128)S(1)} %get-tuple-element.24.take, f32[32,64,128]{2,1,0:T(8,128)S(1)} %copy-done, f32[32,64,128]{2,1,0:T(8,128)S(1)} %copy-done.4, bf16[32,64,128]{2,1,0:T(8,128)(2,1)S(1)} %copy-done.1, ...), custom_call_target="tpu_custom_call" | custom-call | flops 3000000 | bytes 5000000 | tf_op jit(solution)/shard_map/local/pallas_call | solution.py:208
  82.4 1.0 %copy-done.5 = f32[32,64,128]{2,1,0:T(8,128)} copy-done((f32[32,64,128]{2,1,0:T(8,128)}, f32[32,64,128]{2,1,0:T(8,128)S(1)}, u32[]{:S(2)}) %copy-start.5) | copy-done | bytes 1048600
  83.4 2.9 %all-to-all-done.4.received = bf16[4,80,128]{2,1,0:T(8,128)(2,1)S(1)} async-done(((bf16[4,80,128]{2,1,0:T(8,128)(2,1)}), bf16[4,80,128]{2,1,0:T(8,128)(2,1)S(1)}, u32[]{:S(2)}, u32[]{:S(2)}) %all-to-all-start.4) | async-done | bytes 81952 | tf_op jit(solution)/shard_map/all_to_all | solution.py:214
  86.3 1.2 %copy-done.6 = f32[32,64,128]{2,1,0:T(8,128)S(1)} copy-done((f32[32,64,128]{2,1,0:T(8,128)S(1)}, f32[32,64,128]{2,1,0:T(8,128)}, u32[]{:S(2)}) %copy-start.6) | copy-done | bytes 1048600
  87.6 2.1 %final.1 = f32[32,64,128]{2,1,0:T(8,128)} custom-call(s32[1]{0:T(128)} %bitcast.place, f32[32]{0:T(128)S(1)} %get-tuple-element.25.keep, bf16[4,80,128]{2,1,0:T(8,128)(2,1)S(1)} %all-to-all-done.4.received, f32[64,128]{1,0:T(8,128)S(1)} %get-tuple-element.15.before1, f32[8,128]{1,0:T(8,128)S(1)} %get-tuple-element.16.gain1, ...), custom_call_target="tpu_custom_call" | custom-call | flops 800000 | bytes 2300000 | tf_op jit(solution)/shard_map/final/pallas_call | solution.py:224
  (17 shorter events, 0.0 us)
Async XLA Ops:
  0.6 19.4 %copy-start.10 = (f32[1,1024]{1,0:T(1,128)S(1)}, f32[1,1024]{1,0:T(1,128)}, u32[]{:S(2)}) copy-start(f32[1,1024]{1,0:T(1,128)} %constant.53.clone.factor) | copy-start | bytes 12292
  0.6 19.4 %copy-start.9 = (bf16[1024,1024]{1,0:T(8,128)(2,1)S(1)}, bf16[1024,1024]{1,0:T(8,128)(2,1)}, u32[]{:S(2)}) copy-start(bf16[1024,1024]{1,0:T(8,128)(2,1)} %constant.52.clone.table) | copy-start | bytes 6291460
  2.1 0.8 copy-start.11
  20.1 13.6 %copy-start.12 = (f32[32]{0:T(128)S(1)}, f32[32]{0:T(128)}, u32[]{:S(2)}) copy-start(f32[32]{0:T(128)} %param.10) | copy-start | bytes 388
  20.1 15.4 %copy-start = (f32[32,64,128]{2,1,0:T(8,128)S(1)}, f32[32,64,128]{2,1,0:T(8,128)}, u32[]{:S(2)}) copy-start(f32[32,64,128]{2,1,0:T(8,128)} %velocity.3) | copy-start | bytes 3145732
  20.1 15.4 %copy-start.1 = (bf16[32,64,128]{2,1,0:T(8,128)(2,1)S(1)}, bf16[32,64,128]{2,1,0:T(8,128)(2,1)}, u32[]{:S(2)}) copy-start(bf16[32,64,128]{2,1,0:T(8,128)(2,1)} %eddy.5) | copy-start | bytes 1572868
  20.1 15.4 %copy-start.2 = (f32[32,64,128]{2,1,0:T(8,128)S(1)}, f32[32,64,128]{2,1,0:T(8,128)}, u32[]{:S(2)}) copy-start(f32[32,64,128]{2,1,0:T(8,128)} %register.1) | copy-start | bytes 3145732
  21.4 0.8 copy-start.7
  22.2 16.1 %all-to-all-start.1 = ((bf16[8,256,128]{2,1,0:T(8,128)(2,1)}), bf16[8,256,128]{2,1,0:T(8,128)(2,1)S(1)}, u32[]{:S(2)}, u32[]{:S(2)}) async-start(bf16[8,256,128]{2,1,0:T(8,128)(2,1)} %copy-done.7), calls=%async_computation.1 | async-start | bytes 1048576 | tf_op jit(solution)/shard_map/all_to_all | solution.py:203
  27.9 6.0 %collective-permute-start.1 = (bf16[3,64,128]{2,1,0:T(8,128)(2,1)S(1)}, bf16[3,64,128]{2,1,0:T(8,128)(2,1)S(1)}, u32[]{:S(2)}, u32[]{:S(2)}) collective-permute-start(bf16[3,64,128]{2,1,0:T(8,128)(2,1)S(1)} %get-tuple-element.22), channel_id=1, source_target_pairs={{8,0},{16,8},{24,16},{32,24},{40,32},{48,40},{56,48},{64,56},{72,6... | collective-permute-start | bytes 147464 | tf_op jit(solution)/shard_map/ppermute | solution.py:189
  29.2 6.3 %collective-permute-start = (bf16[3,64,128]{2,1,0:T(8,128)(2,1)S(1)}, bf16[3,64,128]{2,1,0:T(8,128)(2,1)S(1)}, u32[]{:S(2)}, u32[]{:S(2)}) collective-permute-start(bf16[3,64,128]{2,1,0:T(8,128)(2,1)S(1)} %get-tuple-element.23), channel_id=1, source_target_pairs={{0,8},{8,16},{16,24},{24,32},{32,40},{40,48},{48,56},{56,64},{64,7... | collective-permute-start | bytes 147464 | tf_op jit(solution)/shard_map/ppermute | solution.py:188
  37.3 1.0 %copy-start.3 = (f32[32,64,128]{2,1,0:T(8,128)}, f32[32,64,128]{2,1,0:T(8,128)S(1)}, u32[]{:S(2)}) copy-start(f32[32,64,128]{2,1,0:T(8,128)S(1)} %get-tuple-element.19.base) | copy-start | bytes 3145732
  38.3 42.3 %copy-start.4 = (f32[32,64,128]{2,1,0:T(8,128)S(1)}, f32[32,64,128]{2,1,0:T(8,128)}, u32[]{:S(2)}) copy-start(f32[32,64,128]{2,1,0:T(8,128)} %copy-done.3) | copy-start | bytes 3145732
  39.7 46.6 %copy-start.8 = (f32[64,128]{1,0:T(8,128)S(1)}, f32[64,128]{1,0:T(8,128)}, u32[]{:S(2)}) copy-start(f32[64,128]{1,0:T(8,128)} %inflow.1) | copy-start | bytes 98308
  39.7 9.5 %all-to-all-start.2 = ((bf16[4,80,128]{2,1,0:T(8,128)(2,1)}), bf16[4,80,128]{2,1,0:T(8,128)(2,1)S(1)}, u32[]{:S(2)}, u32[]{:S(2)}) async-start(bf16[4,80,128]{2,1,0:T(8,128)(2,1)} %offset.1._), calls=%async_computation.2 | async-start | bytes 163840 | tf_op jit(solution)/shard_map/all_to_all | solution.py:214
  49.9 25.8 %all-to-all-start.3 = ((bf16[4,80,128]{2,1,0:T(8,128)(2,1)}), bf16[4,80,128]{2,1,0:T(8,128)(2,1)S(1)}, u32[]{:S(2)}, u32[]{:S(2)}) async-start(bf16[4,80,128]{2,1,0:T(8,128)(2,1)} %get-tuple-element.13), calls=%async_computation.3 | async-start | bytes 163840 | tf_op jit(solution)/shard_map/all_to_all | solution.py:214
  76.3 10.0 %all-to-all-start.4 = ((bf16[4,80,128]{2,1,0:T(8,128)(2,1)}), bf16[4,80,128]{2,1,0:T(8,128)(2,1)S(1)}, u32[]{:S(2)}, u32[]{:S(2)}) async-start(bf16[4,80,128]{2,1,0:T(8,128)(2,1)} %get-tuple-element.14), calls=%async_computation.4 | async-start | bytes 163840 | tf_op jit(solution)/shard_map/all_to_all | solution.py:214
  82.4 1.0 %copy-start.5 = (f32[32,64,128]{2,1,0:T(8,128)}, f32[32,64,128]{2,1,0:T(8,128)S(1)}, u32[]{:S(2)}) copy-start(f32[32,64,128]{2,1,0:T(8,128)S(1)} %get-tuple-element.20.local) | copy-start | bytes 3145732
  86.3 1.2 %copy-start.6 = (f32[32,64,128]{2,1,0:T(8,128)S(1)}, f32[32,64,128]{2,1,0:T(8,128)}, u32[]{:S(2)}) copy-start(f32[32,64,128]{2,1,0:T(8,128)} %copy-done.5) | copy-start | bytes 3145732
where the time goes:
time: 90.4 us; the launch traced here: 89.7 us
  starting transfers between devices  31.6 us (35%)
  waiting for transfers between devices  23.4 us (26%)
  blocking collectives  17.2 us (19%)
  Pallas kernels  9.78 us (11%)
  local copies, waits for them, and re-layouts  5.6 us (6%)
  other arithmetic  1.46 us (2%)
    all_to_all x3, waiting for transfers between devices, body(): lax.all_to_all(payload, 'gx', 0, 0, axis_index_groups=GROUPS[level], tile...  21.6 us
    all_to_all x3, starting transfers between devices, body(): lax.all_to_all(payload, 'gx', 0, 0, axis_index_groups=GROUPS[level], tile...  20.9 us
    all_to_all x1, blocking collectives, body(): lax.all_to_all(rounded.reshape(PARTS, ROWS, WIDTH), 'gz', 0, 0, tiled=True)  17.2 us
    all_to_all x1, starting transfers between devices, body(): lax.all_to_all(derived, 'gz', 0, 0, tiled=True).reshape(STATIONS, NY, WIDTH)  4.86 us
    unnamed x26, local copies, waits for them, and re-layouts  4.78 us
    ppermute x1, starting transfers between devices, body(): low = lax.ppermute(rounded[STATIONS - 3:], 'gx', forward)  4.55 us
    pallas_call x1, Pallas kernels, body(): pl.pallas_call(final_kernel, name='final', grid=(STATIONS // chunk,), in_...  2.13 us
    pallas_call x1, Pallas kernels, body(): call(stencil_kernel, 'stencil', [SMEM, SMEM] + [VMEM] * 5, (CUBE, PLANE),...  1.84 us
  transfers between devices with their start and end apart: 6, of which 5 were waited for; matrix products, arithmetic and copies ran while one was open for 1% of the time, Pallas kernels for 4%

commit v1 on v0

--- a/solution.py
+++ b/solution.py
@@ -16,9 +16,11 @@
 weight = 15.0 / 16.0
 
 STATIONS, NY, WIDTH, PARTS = 32, 64, 128, 8
+CUTS = 4
 LENGTH = WIDTH * PARTS
 ROWS = STATIONS * NY // PARTS
-VMEM_LIMIT = 16 * 1024 * 1024
+MIB = 1024 * 1024
+LARGE = 62
 F32, BF16 = jnp.float32, jnp.bfloat16
 PAYLOAD = NY + 16
 
@@ -39,6 +41,28 @@
     twice = np.where(np.arange(1, LENGTH // 2 + 1) < LENGTH // 2, 2.0, 1.0).astype(np.float32)
     factor = np.concatenate([factor * twice] * 2)[None, :].astype(np.float32)
     return table, factor
+
+
+def round_kernel(velocity, rounded, first, last, wide, narrow, in_sem, out_sem):
+    step = STATIONS // CUTS
+    cuts = [pl.ds(c * step, step) for c in range(CUTS)]
+    order = [0, CUTS - 1, *range(1, CUTS - 1)]
+    loads = {c: pltpu.make_async_copy(velocity.at[cuts[c]], wide.at[cuts[c]], in_sem.at[c]) for c in order}
+    stores = {c: pltpu.make_async_copy(narrow.at[cuts[c]], rounded.at[cuts[c]], out_sem.at[c]) for c in order}
+    for c in order:
+        loads[c].start()
+    for c in order:
+        loads[c].wait()
+        for i in range(c * step, (c + 1) * step):
+            plane = wide[i].astype(BF16)
+            narrow[i] = plane
+            if i < 3:
+                first[i] = plane
+            if i >= STATIONS - 3:
+                last[i - STATIONS + 3] = plane
+        stores[c].start()
+    for c in order:
+        stores[c].wait()
 
 
 def stencil_kernel(keep, take, velocity, register, eddy, low, high, base, offset):
@@ -63,13 +87,26 @@
     offset[...] = running
 
 
-def span_kernel(lines, table, factor, out, scaled):
-    whole = jnp.concatenate([lines[b] for b in range(PARTS)], axis=1)
+def span_kernel(lines, far_table, factor, _buffer, out, whole, table, scaled, held, line_sem, load_sem, sem):
     step = 256
+    slabs = [pl.ds(n * step, step) for n in range(LENGTH // step)]
+    loads = [
+        pltpu.make_async_copy(far_table.at[:, cut], table.at[:, cut], load_sem.at[n]) for n, cut in enumerate(slabs)
+    ]
+    arrive = [
+        pltpu.make_async_copy(lines.at[b], whole.at[:, pl.ds(b * WIDTH, WIDTH)], line_sem.at[b]) for b in range(PARTS)
+    ]
+    for copy in [*arrive, *loads]:
+        copy.start()
+    for copy in arrive:
+        copy.wait()
     for n in range(LENGTH // step):
+        loads[n].wait()
         cut = slice(n * step, (n + 1) * step)
-        part = jnp.dot(whole, table[:, cut], preferred_element_type=F32)
+        part = jnp.dot(whole[...], table[:, cut], preferred_element_type=F32)
         scaled[:, cut] = (part * factor[:, cut]).astype(BF16)
+    blocks = [pl.ds(n * step // WIDTH, step // WIDTH) for n in range(LENGTH // step)]
+    copies = [pltpu.make_async_copy(held.at[b], out.at[b], sem.at[n]) for n, b in enumerate(blocks)]
     for n in range(LENGTH // step):
         part = lax.dot_general(
             scaled[...],
@@ -78,7 +115,10 @@
             preferred_element_type=F32,
         ).astype(BF16)
         for b in range(step // WIDTH):
-            out[n * step // WIDTH + b] = part[:, b * WIDTH : (b + 1) * WIDTH]
+            held[n * step // WIDTH + b] = part[:, b * WIDTH : (b + 1) * WIDTH]
+        copies[n].start()
+    for copy in copies:
+        copy.wait()
 
 
 def store_payload(out, plane, gain):
@@ -100,13 +140,28 @@
     store_payload(out, running + base_offset[...], gain)
 
 
-def local_kernel(keep, take, velocity, base, eddy, second, _, register, local):
+def local_kernel(keep, take, velocity, base, eddy, second, _, register, local, new_held, held, sem):
+    step = STATIONS // CUTS
+    cuts = [pl.ds(c * step, step) for c in range(CUTS)]
+    copies = [
+        (
+            pltpu.make_async_copy(new_held.at[cuts[c]], register.at[cuts[c]], sem.at[0, c]),
+            pltpu.make_async_copy(held.at[cuts[c]], local.at[cuts[c]], sem.at[1, c]),
+        )
+        for c in range(CUTS)
+    ]
     running = jnp.zeros((NY, WIDTH), F32)
-    for i in range(STATIONS):
-        new = base[i] + eddy[i].astype(F32) * second[i].astype(F32)
-        register[i] = new
-        running = keep[i] * running + take[i] * (velocity[i] + weight * new)
-        local[i] = running
+    for c in range(CUTS):
+        for i in range(c * step, (c + 1) * step):
+            new = base[i] + eddy[i].astype(F32) * second[i].astype(F32)
+            new_held[i] = new
+            running = keep[i] * running + take[i] * (velocity[i] + weight * new)
+            held[i] = running
+        for copy in copies[c]:
+            copy.start()
+    for pair in copies:
+        for copy in pair:
+            copy.wait()
 
 
 def fold(place, received):
@@ -131,43 +186,51 @@
     store_payload(out, total, gain)
 
 
-def final_kernel(place, keep, received, before1, gain1, before2, gain2, inflow, local, out, entering):
-    step = pl.program_id(0)
-    count = out.shape[0]
-
-    @pl.when(step == 0)
-    def _():
-        before, gain, _, _ = fold(place[0], received)
-        value = before + gain[0:1] * inflow[...]
-        value = before2[...] + gain2[0:1] * value
-        entering[...] = before1[...] + gain1[0:1] * value
-
-    running = entering[...]
-    for i in range(count):
-        running = running * keep[step * count + i]
-        out[i] = local[i] + running
-    entering[...] = running
+def final_kernel(
+    place, keep, received, before1, gain1, before2, gain2, inflow, local, out, held, done, in_sem, out_sem
+):
+    step = STATIONS // CUTS
+    cuts = [pl.ds(c * step, step) for c in range(CUTS)]
+    loads = [pltpu.make_async_copy(local.at[cuts[c]], held.at[cuts[c]], in_sem.at[c]) for c in range(CUTS)]
+    stores = [pltpu.make_async_copy(done.at[cuts[c]], out.at[cuts[c]], out_sem.at[c]) for c in range(CUTS)]
+    for load in loads:
+        load.start()
+    before, gain, _, _ = fold(place[0], received)
+    value = before + gain[0:1] * inflow[...]
+    value = before2[...] + gain2[0:1] * value
+    running = before1[...] + gain1[0:1] * value
+    for c in range(CUTS):
+        loads[c].wait()
+        for i in range(c * step, (c + 1) * step):
+            running = running * keep[i]
+            done[i] = held[i] + running
+        stores[c].start()
+    for store in stores:
+        store.wait()
 
 
 SMEM = pl.BlockSpec(memory_space=pltpu.SMEM)
 VMEM = pl.BlockSpec(memory_space=pltpu.VMEM)
 ANY = pl.BlockSpec(memory_space=pl.ANY)
+HBM = pl.BlockSpec(memory_space=pltpu.HBM)
 CUBE = jax.ShapeDtypeStruct((STATIONS, NY, WIDTH), F32)
 PLANE = jax.ShapeDtypeStruct((NY, WIDTH), F32)
 GAIN = jax.ShapeDtypeStruct((8, WIDTH), F32)
+EDGE = jax.ShapeDtypeStruct((3, NY, WIDTH), BF16)
+DMA = pltpu.SemaphoreType.DMA
 SLOTS = jax.ShapeDtypeStruct((4, PAYLOAD, WIDTH), BF16)
 
 
-def call(kernel, name, in_specs, out_shape, flops, bytes_accessed, scratch=()):
-    many = isinstance(out_shape, tuple)
+def call(kernel, name, in_specs, out_specs, out_shape, flops, bytes_accessed, scratch=(), limit=16, alias=None):
     return pl.pallas_call(
         kernel,
         name=name,
         in_specs=in_specs,
-        out_specs=tuple(VMEM for _ in out_shape) if many else VMEM,
+        out_specs=out_specs,
         out_shape=out_shape,
         scratch_shapes=scratch,
-        compiler_params=pltpu.CompilerParams(vmem_limit_bytes=VMEM_LIMIT),
+        input_output_aliases=alias or {},
+        compiler_params=pltpu.CompilerParams(vmem_limit_bytes=int(limit * MIB)),
         cost_estimate=pl.CostEstimate(flops=flops, bytes_accessed=bytes_accessed, transcendentals=0),
     )
 
@@ -179,34 +242,64 @@
     keep = courant / (1.0 + courant)
     take = 1.0 / (1.0 + courant)
 
-    rounded = velocity.astype(BF16)
-    lines = lax.all_to_all(rounded.reshape(PARTS, ROWS, WIDTH), "gz", 0, 0, tiled=True)
+    rounded, first, last = call(
+        round_kernel,
+        "round",
+        [HBM],
+        (HBM, VMEM, VMEM),
+        (jax.ShapeDtypeStruct(CUBE.shape, BF16), EDGE, EDGE),
+        300_000,
+        1_600_000,
+        (pltpu.VMEM(CUBE.shape, F32), pltpu.VMEM(CUBE.shape, BF16), DMA((CUTS,)), DMA((CUTS,))),
+        LARGE,
+    )(velocity)
+    rounded = rounded.reshape(PARTS, ROWS, WIDTH)
+    lines = lax.all_to_all(rounded, "gz", 0, 0, tiled=True)
 
     count = lax.axis_size("gx")
     forward = [(i, i + 1) for i in range(count - 1)]
     backward = [(b, a) for a, b in forward]
-    low = lax.ppermute(rounded[STATIONS - 3 :], "gx", forward)
-    high = lax.ppermute(rounded[:3], "gx", backward)
+    low = lax.ppermute(last, "gx", forward)
+    high = lax.ppermute(first, "gx", backward)
+    lines, low, high = lax.optimization_barrier((lines, low, high))
     base, base_offset = call(
-        stencil_kernel, "stencil", [SMEM, SMEM] + [VMEM] * 5, (CUBE, PLANE), 8_000_000, 4_000_000
+        stencil_kernel, "stencil", [SMEM, SMEM] + [VMEM] * 5, (VMEM, VMEM), (CUBE, PLANE), 8_000_000, 4_000_000
     )(keep, take, velocity, register, eddy_viscosity, low, high)
 
     derived = call(
         span_kernel,
         "span",
-        [VMEM, VMEM, VMEM],
+        [HBM, HBM, VMEM, HBM],
+        HBM,
         jax.ShapeDtypeStruct((PARTS, ROWS, WIDTH), BF16),
         4 * ROWS * LENGTH * LENGTH,
         3_200_000,
-        (pltpu.VMEM((ROWS, LENGTH), BF16),),
-    )(lines, jnp.asarray(table), jnp.asarray(factor))
+        (
+            pltpu.VMEM((ROWS, LENGTH), BF16),
+            pltpu.VMEM((LENGTH, LENGTH), BF16),
+            pltpu.VMEM((ROWS, LENGTH), BF16),
+            pltpu.VMEM((PARTS, ROWS, WIDTH), BF16),
+            DMA((PARTS,)),
+            DMA((LENGTH // 256,)),
+            DMA((LENGTH // 256,)),
+        ),
+        LARGE,
+        {3: 0},
+    )(lines, jnp.asarray(table), jnp.asarray(factor), rounded)
     second = lax.all_to_all(derived, "gz", 0, 0, tiled=True).reshape(STATIONS, NY, WIDTH)
 
-    payload = call(offset_kernel, "offset", [SMEM, SMEM] + [VMEM] * 3, SLOTS, 1_500_000, 1_100_000)(
+    payload = call(offset_kernel, "offset", [SMEM, SMEM] + [VMEM] * 3, VMEM, SLOTS, 1_500_000, 1_100_000)(
         keep, take, second, eddy_viscosity, base_offset
     )
     new_register, local = call(
-        local_kernel, "local", [SMEM, SMEM] + [VMEM] * 4 + [ANY], (CUBE, CUBE), 3_000_000, 5_000_000
+        local_kernel,
+        "local",
+        [SMEM, SMEM] + [VMEM] * 4 + [ANY],
+        (HBM, HBM),
+        (CUBE, CUBE),
+        3_000_000,
+        5_000_000,
+        (pltpu.VMEM(CUBE.shape, F32), pltpu.VMEM(CUBE.shape, F32), DMA((2, CUTS))),
     )(keep, take, velocity, base, eddy_viscosity, second, payload)
 
     found = []
@@ -214,25 +307,20 @@
         payload = lax.all_to_all(payload, "gx", 0, 0, axis_index_groups=GROUPS[level], tiled=True)
         if level < 2:
             before, gain, payload = call(
-                fold_kernel, "fold", [SMEM, VMEM], (PLANE, GAIN, SLOTS), 200_000, 300_000
+                fold_kernel, "fold", [SMEM, VMEM], (VMEM,) * 3, (PLANE, GAIN, SLOTS), 200_000, 300_000
             )(places[level], payload)
             found += [before, gain]
 
-    chunk = 8
-    whole = lambda *shape: pl.BlockSpec(shape, lambda i: (0,) * len(shape))
-    cube = pl.BlockSpec((chunk, NY, WIDTH), lambda i: (i, 0, 0))
-    new_velocity = pl.pallas_call(
+    new_velocity = call(
         final_kernel,
-        name="final",
-        grid=(STATIONS // chunk,),
-        in_specs=[SMEM, SMEM, whole(4, PAYLOAD, WIDTH)]
-        + [whole(NY, WIDTH), whole(8, WIDTH)] * 2
-        + [whole(NY, WIDTH), cube],
-        out_specs=cube,
-        out_shape=CUBE,
-        scratch_shapes=[pltpu.VMEM((NY, WIDTH), F32)],
-        compiler_params=pltpu.CompilerParams(vmem_limit_bytes=VMEM_LIMIT),
-        cost_estimate=pl.CostEstimate(flops=800_000, bytes_accessed=2_300_000, transcendentals=0),
+        "final",
+        [SMEM, SMEM] + [VMEM] * 6 + [HBM],
+        HBM,
+        CUBE,
+        800_000,
+        2_300_000,
+        (pltpu.VMEM(CUBE.shape, F32), pltpu.VMEM(CUBE.shape, F32), DMA((CUTS,)), DMA((CUTS,))),
+        alias={8: 0},
     )(places[2], keep, payload, *found, inflow, local)
     return new_velocity, new_register
 

time: 90.4 us -> 91.5 us (1.012)
  the two profiles are of different devices: /device:TPU:8 before, /device:TPU:32 now
where the time goes in v1:
time: 91.5 us; the launch traced here: 90.6 us
  starting transfers between devices  40.5 us (44%)
  waiting for transfers between devices  29.1 us (32%)
  Pallas kernels  16.9 us (18%)
  local copies, waits for them, and re-layouts  3.43 us (4%)
    all_to_all x3, starting transfers between devices, body(): lax.all_to_all(payload, 'gx', 0, 0, axis_index_groups=GROUPS[level], tile...  22.8 us
    all_to_all x3, waiting for transfers between devices, body(): lax.all_to_all(payload, 'gx', 0, 0, axis_index_groups=GROUPS[level], tile...  20.8 us
    all_to_all x1, waiting for transfers between devices, body(): lax.all_to_all(derived, 'gz', 0, 0, tiled=True).reshape(STATIONS, NY, WIDTH)  6.26 us
    pallas_call x1, Pallas kernels, body(): call(span_kernel, 'span', [HBM, HBM, VMEM, HBM], HBM, jax.ShapeDtypeStruc...  5.26 us
    ppermute x1, starting transfers between devices, body(): high = lax.ppermute(first, 'gx', backward)  4.7 us
    all_to_all x1, starting transfers between devices, body(): lax.all_to_all(derived, 'gz', 0, 0, tiled=True).reshape(STATIONS, NY, WIDTH)  4.68 us
    all_to_all x1, starting transfers between devices, body(): lines = lax.all_to_all(rounded, 'gz', 0, 0, tiled=True)  4.48 us
    ppermute x1, starting transfers between devices, body(): low = lax.ppermute(last, 'gx', forward)  3.81 us
  transfers between devices with their start and end apart: 7, of which 6 were waited for; matrix products, arithmetic and copies ran while one was open for 0% of the time, Pallas kernels for 4%

profile of v1, /device:TPU:32, one launch (start us, length us, event | category | flops | bytes accessed | tf_op | source)
XLA Modules:
  0.0 90.6 jit_solution(10026901348943486190)
XLA Ops:
  0.6 2.6 %round.1 = (bf16[32,64,128]{2,1,0:T(8,128)(2,1)}, bf16[3,64,128]{2,1,0:T(8,128)(2,1)}, bf16[3,64,128]{2,1,0:T(8,128)(2,1)}) custom-call(f32[32,64,128]{2,1,0:T(8,128)} %velocity.5), custom_call_target="tpu_custom_call" | custom-call | flops 300000 | bytes 1600000 | tf_op jit(solution)/shard_map/round/pallas_call | solution.py:245
  3.2 4.5 %all-to-all-start = ((bf16[8,256,128]{2,1,0:T(8,128)(2,1)}), bf16[8,256,128]{2,1,0:T(8,128)(2,1)}, u32[]{:S(2)}, u32[]{:S(2)}) async-start(bf16[8,256,128]{2,1,0:T(8,128)(2,1)} %bitcast.7), calls=%async_computation | async-start | bytes 1048576 | tf_op jit(solution)/shard_map/all_to_all | solution.py:257
  7.7 3.8 %collective-permute-start = (bf16[3,64,128]{2,1,0:T(8,128)(2,1)}, bf16[3,64,128]{2,1,0:T(8,128)(2,1)S(1)}, u32[]{:S(2)}, u32[]{:S(2)}) collective-permute-start(bf16[3,64,128]{2,1,0:T(8,128)(2,1)} %get-tuple-element.19), channel_id=1, source_target_pairs={{0,8},{8,16},{16,24},{24,32},{32,40},{40,48},{48,56},{56,64},{64,7... | collective-permute-start | bytes 147464 | tf_op jit(solution)/shard_map/ppermute | solution.py:262
  11.5 0.0 copy-start.6
  11.5 0.0 copy-start
  11.5 0.0 copy-start.1
  11.5 4.7 %collective-permute-start.1 = (bf16[3,64,128]{2,1,0:T(8,128)(2,1)}, bf16[3,64,128]{2,1,0:T(8,128)(2,1)S(1)}, u32[]{:S(2)}, u32[]{:S(2)}) collective-permute-start(bf16[3,64,128]{2,1,0:T(8,128)(2,1)} %get-tuple-element.20), channel_id=1, source_target_pairs={{8,0},{16,8},{24,16},{32,24},{40,32},{48,40},{56,48},{64,56},{72,6... | collective-permute-start | bytes 147464 | tf_op jit(solution)/shard_map/ppermute | solution.py:263
  16.2 0.4 collective-permute-done.low
  16.6 1.7 %collective-permute-done.1.high = bf16[3,64,128]{2,1,0:T(8,128)(2,1)S(1)} collective-permute-done((bf16[3,64,128]{2,1,0:T(8,128)(2,1)}, bf16[3,64,128]{2,1,0:T(8,128)(2,1)S(1)}, u32[]{:S(2)}, u32[]{:S(2)}) %collective-permute-start.1) | collective-permute-done | bytes 49184 | tf_op jit(solution)/shard_map/ppermute | solution.py:263
  18.3 0.0 all-to-all-done.lines
  18.3 5.3 %span.1 = bf16[8,256,128]{2,1,0:T(8,128)(2,1)} custom-call(bf16[8,256,128]{2,1,0:T(8,128)(2,1)} %all-to-all-done.lines, bf16[1024,1024]{1,0:T(8,128)(2,1)} %constant.52.clone.far_table, f32[1,1024]{1,0:T(1,128)} %constant.53.clone.factor, bf16[8,256,128]{2,1,0:T(8,128)(2,1)} %bitcast.8), custom_call_target="tpu_custom_call", output_to_operand_aliasing={{}: (3, {})} | custom-call | flops 1073741824 | bytes 3200000 | tf_op jit(solution)/shard_map/span/pallas_call | solution.py:269
  23.6 4.7 %all-to-all-start.1 = ((bf16[8,256,128]{2,1,0:T(8,128)(2,1)}), bf16[8,256,128]{2,1,0:T(8,128)(2,1)S(1)}, u32[]{:S(2)}, u32[]{:S(2)}) async-start(bf16[8,256,128]{2,1,0:T(8,128)(2,1)} %span.1), calls=%async_computation.1 | async-start | bytes 1048576 | tf_op jit(solution)/shard_map/all_to_all | solution.py:289
  28.2 0.0 copy-done.6
  28.3 0.0 copy-done
  28.3 0.0 copy-start.2
  28.3 1.2 %copy-done.2 = f32[32,64,128]{2,1,0:T(8,128)S(1)} copy-done((f32[32,64,128]{2,1,0:T(8,128)S(1)}, f32[32,64,128]{2,1,0:T(8,128)}, u32[]{:S(2)}) %copy-start.2) | copy-done | bytes 1048600
  29.5 1.8 %stencil.1 = (f32[32,64,128]{2,1,0:T(8,128)S(1)}, f32[64,128]{1,0:T(8,128)S(1)}) custom-call(f32[32]{0:T(128)S(1)} %get-tuple-element.35.keep, f32[32]{0:T(128)S(1)} %get-tuple-element.34.take, f32[32,64,128]{2,1,0:T(8,128)S(1)} %copy-done, f32[32,64,128]{2,1,0:T(8,128)S(1)} %copy-done.2, bf16[32,64,128]{2,1,0:T(8,128)(2,1)S(1)} %copy-done.1, ...), custom_call_target="tpu_custom_call" | custom-call | flops 8000000 | bytes 4000000 | tf_op jit(solution)/shard_map/stencil/pallas_call | solution.py:265
  31.4 0.0 copy-start.3
  31.4 1.0 %copy-done.3 = f32[32,64,128]{2,1,0:T(8,128)} copy-done((f32[32,64,128]{2,1,0:T(8,128)}, f32[32,64,128]{2,1,0:T(8,128)S(1)}, u32[]{:S(2)}) %copy-start.3) | copy-done | bytes 1048600
  32.3 6.3 %all-to-all-done.1 = bf16[8,256,128]{2,1,0:T(8,128)(2,1)S(1)} async-done(((bf16[8,256,128]{2,1,0:T(8,128)(2,1)}), bf16[8,256,128]{2,1,0:T(8,128)(2,1)S(1)}, u32[]{:S(2)}, u32[]{:S(2)}) %all-to-all-start.1) | async-done | bytes 524320 | tf_op jit(solution)/shard_map/all_to_all | solution.py:289
  38.6 1.4 %offset.1._ = bf16[4,80,128]{2,1,0:T(8,128)(2,1)} custom-call(f32[32]{0:T(128)S(1)} %get-tuple-element.35.keep, f32[32]{0:T(128)S(1)} %get-tuple-element.34.take, bf16[32,64,128]{2,1,0:T(8,128)(2,1)S(1)} %bitcast.5, bf16[32,64,128]{2,1,0:T(8,128)(2,1)S(1)} %copy-done.1, f32[64,128]{1,0:T(8,128)S(1)} %get-tuple-element.24.base_offset), custom_call_target="tpu_custom_call" | custom-call | flops 1500000 | bytes 1100000 | tf_op jit(solution)/shard_map/offset/pallas_call | solution.py:291
  40.0 8.3 %all-to-all-start.2 = ((bf16[4,80,128]{2,1,0:T(8,128)(2,1)}), bf16[4,80,128]{2,1,0:T(8,128)(2,1)S(1)}, u32[]{:S(2)}, u32[]{:S(2)}) async-start(bf16[4,80,128]{2,1,0:T(8,128)(2,1)} %offset.1._), calls=%async_computation.2 | async-start | bytes 163840 | tf_op jit(solution)/shard_map/all_to_all | solution.py:307
  48.3 4.8 %all-to-all-done.2.received = bf16[4,80,128]{2,1,0:T(8,128)(2,1)S(1)} async-done(((bf16[4,80,128]{2,1,0:T(8,128)(2,1)}), bf16[4,80,128]{2,1,0:T(8,128)(2,1)S(1)}, u32[]{:S(2)}, u32[]{:S(2)}) %all-to-all-start.2) | async-done | bytes 81952 | tf_op jit(solution)/shard_map/all_to_all | solution.py:307
  53.0 0.7 fold.2
  53.7 10.3 %all-to-all-start.3 = ((bf16[4,80,128]{2,1,0:T(8,128)(2,1)}), bf16[4,80,128]{2,1,0:T(8,128)(2,1)S(1)}, u32[]{:S(2)}, u32[]{:S(2)}) async-start(bf16[4,80,128]{2,1,0:T(8,128)(2,1)} %get-tuple-element.25), calls=%async_computation.3 | async-start | bytes 163840 | tf_op jit(solution)/shard_map/all_to_all | solution.py:307
  64.0 13.5 %all-to-all-done.3.received = bf16[4,80,128]{2,1,0:T(8,128)(2,1)S(1)} async-done(((bf16[4,80,128]{2,1,0:T(8,128)(2,1)}), bf16[4,80,128]{2,1,0:T(8,128)(2,1)S(1)}, u32[]{:S(2)}, u32[]{:S(2)}) %all-to-all-start.3) | async-done | bytes 81952 | tf_op jit(solution)/shard_map/all_to_all | solution.py:307
  77.4 0.6 fold.3
  78.1 4.3 %all-to-all-start.4 = ((bf16[4,80,128]{2,1,0:T(8,128)(2,1)}), bf16[4,80,128]{2,1,0:T(8,128)(2,1)S(1)}, u32[]{:S(2)}, u32[]{:S(2)}) async-start(bf16[4,80,128]{2,1,0:T(8,128)(2,1)} %get-tuple-element.26), calls=%async_computation.4 | async-start | bytes 163840 | tf_op jit(solution)/shard_map/all_to_all | solution.py:307
  82.4 1.2 %copy-done.4 = f32[32,64,128]{2,1,0:T(8,128)S(1)} copy-done((f32[32,64,128]{2,1,0:T(8,128)S(1)}, f32[32,64,128]{2,1,0:T(8,128)}, u32[]{:S(2)}) %copy-start.4) | copy-done | bytes 1048600
  83.6 2.0 %local.1 = (f32[32,64,128]{2,1,0:T(8,128)}, f32[32,64,128]{2,1,0:T(8,128)}) custom-call(f32[32]{0:T(128)S(1)} %get-tuple-element.35.keep, f32[32]{0:T(128)S(1)} %get-tuple-element.34.take, f32[32,64,128]{2,1,0:T(8,128)S(1)} %copy-done, f32[32,64,128]{2,1,0:T(8,128)S(1)} %copy-done.4, bf16[32,64,128]{2,1,0:T(8,128)(2,1)S(1)} %copy-done.1, ...), custom_call_target="tpu_custom_call" | custom-call | flops 3000000 | bytes 5000000 | tf_op jit(solution)/shard_map/local/pallas_call | solution.py:294
  85.6 2.5 %all-to-all-done.4.received = bf16[4,80,128]{2,1,0:T(8,128)(2,1)S(1)} async-done(((bf16[4,80,128]{2,1,0:T(8,128)(2,1)}), bf16[4,80,128]{2,1,0:T(8,128)(2,1)S(1)}, u32[]{:S(2)}, u32[]{:S(2)}) %all-to-all-start.4) | async-done | bytes 81952 | tf_op jit(solution)/shard_map/all_to_all | solution.py:307
  88.1 2.5 %final.1 = f32[32,64,128]{2,1,0:T(8,128)} custom-call(s32[1]{0:T(128)} %bitcast.place, f32[32]{0:T(128)S(1)} %get-tuple-element.35.keep, bf16[4,80,128]{2,1,0:T(8,128)(2,1)S(1)} %all-to-all-done.4.received, f32[64,128]{1,0:T(8,128)S(1)} %get-tuple-element.27.before1, f32[8,128]{1,0:T(8,128)S(1)} %get-tuple-element.28.gain1, ...), custom_call_target="tpu_custom_call", output_to_operand_aliasing={{}: (8, {})} | custom-call | flops 800000 | bytes 2300000 | tf_op jit(solution)/shard_map/final/pallas_call | solution.py:314
  (5 shorter events, 0.0 us)
Async XLA Ops:
  3.2 15.1 %all-to-all-start = ((bf16[8,256,128]{2,1,0:T(8,128)(2,1)}), bf16[8,256,128]{2,1,0:T(8,128)(2,1)}, u32[]{:S(2)}, u32[]{:S(2)}) async-start(bf16[8,256,128]{2,1,0:T(8,128)(2,1)} %bitcast.7), calls=%async_computation | async-start | bytes 1048576 | tf_op jit(solution)/shard_map/all_to_all | solution.py:257
  7.7 8.9 %collective-permute-start = (bf16[3,64,128]{2,1,0:T(8,128)(2,1)}, bf16[3,64,128]{2,1,0:T(8,128)(2,1)S(1)}, u32[]{:S(2)}, u32[]{:S(2)}) collective-permute-start(bf16[3,64,128]{2,1,0:T(8,128)(2,1)} %get-tuple-element.19), channel_id=1, source_target_pairs={{0,8},{8,16},{16,24},{24,32},{32,40},{40,48},{48,56},{56,64},{64,7... | collective-permute-start | bytes 147464 | tf_op jit(solution)/shard_map/ppermute | solution.py:262
  11.5 16.7 %copy-start.6 = (f32[32]{0:T(128)S(1)}, f32[32]{0:T(128)}, u32[]{:S(2)}) copy-start(f32[32]{0:T(128)} %param.10) | copy-start | bytes 388
  11.5 16.7 %copy-start = (f32[32,64,128]{2,1,0:T(8,128)S(1)}, f32[32,64,128]{2,1,0:T(8,128)}, u32[]{:S(2)}) copy-start(f32[32,64,128]{2,1,0:T(8,128)} %velocity.5) | copy-start | bytes 3145732
  11.5 16.7 %copy-start.1 = (bf16[32,64,128]{2,1,0:T(8,128)(2,1)S(1)}, bf16[32,64,128]{2,1,0:T(8,128)(2,1)}, u32[]{:S(2)}) copy-start(bf16[32,64,128]{2,1,0:T(8,128)(2,1)} %eddy.5) | copy-start | bytes 1572868
  11.5 6.8 %collective-permute-start.1 = (bf16[3,64,128]{2,1,0:T(8,128)(2,1)}, bf16[3,64,128]{2,1,0:T(8,128)(2,1)S(1)}, u32[]{:S(2)}, u32[]{:S(2)}) collective-permute-start(bf16[3,64,128]{2,1,0:T(8,128)(2,1)} %get-tuple-element.20), channel_id=1, source_target_pairs={{8,0},{16,8},{24,16},{32,24},{40,32},{48,40},{56,48},{64,56},{72,6... | collective-permute-start | bytes 147464 | tf_op jit(solution)/shard_map/ppermute | solution.py:263
  23.6 15.0 %all-to-all-start.1 = ((bf16[8,256,128]{2,1,0:T(8,128)(2,1)}), bf16[8,256,128]{2,1,0:T(8,128)(2,1)S(1)}, u32[]{:S(2)}, u32[]{:S(2)}) async-start(bf16[8,256,128]{2,1,0:T(8,128)(2,1)} %span.1), calls=%async_computation.1 | async-start | bytes 1048576 | tf_op jit(solution)/shard_map/all_to_all | solution.py:289
  28.3 1.2 %copy-start.2 = (f32[32,64,128]{2,1,0:T(8,128)S(1)}, f32[32,64,128]{2,1,0:T(8,128)}, u32[]{:S(2)}) copy-start(f32[32,64,128]{2,1,0:T(8,128)} %register.1) | copy-start | bytes 3145732
  31.4 1.0 %copy-start.3 = (f32[32,64,128]{2,1,0:T(8,128)}, f32[32,64,128]{2,1,0:T(8,128)S(1)}, u32[]{:S(2)}) copy-start(f32[32,64,128]{2,1,0:T(8,128)S(1)} %get-tuple-element.31.base) | copy-start | bytes 3145732
  40.0 48.1 %copy-start.5 = (f32[64,128]{1,0:T(8,128)S(1)}, f32[64,128]{1,0:T(8,128)}, u32[]{:S(2)}) copy-start(f32[64,128]{1,0:T(8,128)} %inflow.1) | copy-start | bytes 98308
  40.0 13.0 %all-to-all-start.2 = ((bf16[4,80,128]{2,1,0:T(8,128)(2,1)}), bf16[4,80,128]{2,1,0:T(8,128)(2,1)S(1)}, u32[]{:S(2)}, u32[]{:S(2)}) async-start(bf16[4,80,128]{2,1,0:T(8,128)(2,1)} %offset.1._), calls=%async_computation.2 | async-start | bytes 163840 | tf_op jit(solution)/shard_map/all_to_all | solution.py:307
  53.7 23.7 %all-to-all-start.3 = ((bf16[4,80,128]{2,1,0:T(8,128)(2,1)}), bf16[4,80,128]{2,1,0:T(8,128)(2,1)S(1)}, u32[]{:S(2)}, u32[]{:S(2)}) async-start(bf16[4,80,128]{2,1,0:T(8,128)(2,1)} %get-tuple-element.25), calls=%async_computation.3 | async-start | bytes 163840 | tf_op jit(solution)/shard_map/all_to_all | solution.py:307
  78.1 10.0 %all-to-all-start.4 = ((bf16[4,80,128]{2,1,0:T(8,128)(2,1)}), bf16[4,80,128]{2,1,0:T(8,128)(2,1)S(1)}, u32[]{:S(2)}, u32[]{:S(2)}) async-start(bf16[4,80,128]{2,1,0:T(8,128)(2,1)} %get-tuple-element.26), calls=%async_computation.4 | async-start | bytes 163840 | tf_op jit(solution)/shard_map/all_to_all | solution.py:307
  82.4 1.2 %copy-start.4 = (f32[32,64,128]{2,1,0:T(8,128)S(1)}, f32[32,64,128]{2,1,0:T(8,128)}, u32[]{:S(2)}) copy-start(f32[32,64,128]{2,1,0:T(8,128)} %copy-done.3) | copy-start | bytes 3145732

commit v2 on v1

v2 whole, which is shorter than its diff:
```python
import math

import jax
import jax.numpy as jnp
import numpy as np
from jax import lax
from jax.experimental import pallas as pl
from jax.experimental.pallas import tpu as pltpu
from jax.sharding import PartitionSpec as P

coef_zero = -49.0 / 18.0
coef_one = 1.5
coef_two = -3.0 / 20.0
coef_three = 1.0 / 90.0
decay = -5.0 / 9.0
weight = 15.0 / 16.0

STATIONS, NY, WIDTH, PARTS = 32, 64, 128, 8
CUTS = 4
LENGTH = WIDTH * PARTS
ROWS = STATIONS * NY // PARTS
MIB = 1024 * 1024
SLABS = 4
LARGE = 62.75
F32, BF16 = jnp.float32, jnp.bfloat16
PAYLOAD = NY + 16

GROUPS = (
    [[x * 16 + h * 4 + l for l in range(4)] for x in range(4) for h in range(4)],
    [[x * 16 + h * 4 + l for h in range(4)] for x in range(4) for l in range(4)],
    [[x * 16 + z for x in range(4)] for z in range(16)],
)


def span_tables():
    position = np.arange(LENGTH, dtype=np.int64)
    product = position[:, None] * position[None, 1 : LENGTH // 2 + 1] % LENGTH
    angle = product.astype(np.float32) * np.float32(2.0 * math.pi / LENGTH)
    table = np.concatenate([np.cos(angle), np.sin(angle)], axis=1).astype(BF16)
    wave = np.arange(1, LENGTH // 2 + 1).astype(np.float32) * np.float32(2.0 * math.pi / LENGTH)
    factor = -(wave * wave) / np.float32(LENGTH)
    twice = np.where(np.arange(1, LENGTH // 2 + 1) < LENGTH // 2, 2.0, 1.0).astype(np.float32)
    factor = np.concatenate([factor * twice] * 2)[None, :].astype(np.float32)
    return table, factor


def stencil_kernel(keep, take, far_velocity, far_register, eddy, low, high, *rest):
    base, (offset, velocity, register, sem) = rest[:CUTS], rest[CUTS:]
    step = STATIONS // CUTS
    cuts = [pl.ds(c * step, step) for c in range(CUTS)]
    loads = [
        [
            pltpu.make_async_copy(far.at[cuts[c]], near.at[cuts[c]], sem.at[k, c])
            for c in range(CUTS)
        ]
        for k, (far, near) in enumerate(((far_velocity, velocity), (far_register, register)))
    ]
    for c in range(CUTS):
        loads[0][c].start()
        loads[1][c].start()

    def plane(i):
        if i < 0:
            return low[i + 3].astype(F32)
        if i >= STATIONS:
            return high[i - STATIONS].astype(F32)
        return velocity[i]

    running = jnp.zeros((NY, WIDTH), F32)
    loads[0][0].wait()
    for c in range(CUTS):
        if c + 1 < CUTS:
            loads[0][c + 1].wait()
        loads[1][c].wait()
        for i in range(c * step, (c + 1) * step):
            here = velocity[i]
            total = (2.0 * coef_zero) * here
            for shift, coef in ((1, coef_one), (2, coef_two), (3, coef_three)):
                along = plane(i - shift) + plane(i + shift)
                across = pltpu.roll(here, shift, 0) + pltpu.roll(here, NY - shift, 0)
                total = total + coef * (along + across)
            part = decay * register[i] + eddy[i].astype(F32) * total
            base[c][i - c * step] = part
            running = keep[i] * running + take[i] * (here + weight * part)
    offset[...] = running


def span_kernel(lines, factor, _buffer, *rest):
    slabs, out, scaled, held, sem = rest[:SLABS], *rest[SLABS:]
    step = LENGTH // SLABS
    whole = jnp.concatenate([lines[b] for b in range(PARTS)], axis=1)
    for n, slab in enumerate(slabs):
        part = jnp.dot(whole, slab[...], preferred_element_type=F32)
        scaled[n] = (part * factor[:, n * step : (n + 1) * step]).astype(BF16)
    wide = 256
    per = wide // WIDTH
    blocks = [pl.ds(n * per, per) for n in range(LENGTH // wide)]
    copies = [pltpu.make_async_copy(held.at[b], out.at[b], sem.at[n]) for n, b in enumerate(blocks)]
    for n in range(LENGTH // wide):
        part = jnp.zeros((ROWS, wide), F32)
        for m, slab in enumerate(slabs):
            part = part + lax.dot_general(
                scaled[m], slab[n * wide : (n + 1) * wide, :], (((1,), (1,)), ((), ())), preferred_element_type=F32
            )
        part = part.astype(BF16)
        for b in range(per):
            held[n * per + b] = part[:, b * WIDTH : (b + 1) * WIDTH]
        copies[n].start()
    for copy in copies:
        copy.wait()


def store_payload(out, plane, gain):
    upper = gain.astype(BF16).astype(F32)
    tail = jnp.concatenate([upper, gain - upper], axis=0).astype(BF16)
    plane = plane.astype(BF16)
    for m in range(4):
        out[m, 0:NY] = plane
        out[m, NY:PAYLOAD] = tail


def offset_kernel(keep, take, second, eddy, base_offset, out):
    running = jnp.zeros((NY, WIDTH), F32)
    gain = jnp.ones((8, WIDTH), F32)
    for i in range(STATIONS):
        term = eddy[i].astype(F32) * second[i].astype(F32)
        running = keep[i] * running + (take[i] * weight) * term
        gain = gain * keep[i]
    store_payload(out, running + base_offset[...], gain)


def local_kernel(keep, take, velocity, eddy, second, _, *rest):
    base, register, local, (held, sem) = rest[:CUTS], rest[CUTS], rest[CUTS + 1 : 2 * CUTS + 1], rest[2 * CUTS + 1 :]
    step = STATIONS // CUTS
    cuts = [pl.ds(c * step, step) for c in range(CUTS)]
    copies = [pltpu.make_async_copy(held.at[cuts[c]], register.at[cuts[c]], sem.at[c]) for c in range(CUTS)]
    running = jnp.zeros((NY, WIDTH), F32)
    for c in range(CUTS):
        for i in range(c * step, (c + 1) * step):
            new = base[c][i - c * step] + eddy[i].astype(F32) * second[i].astype(F32)
            held[i] = new
            running = keep[i] * running + take[i] * (velocity[i] + weight * new)
            local[c][i - c * step] = running
        copies[c].start()
    for copy in copies:
        copy.wait()


def fold(place, received):
    total = jnp.zeros((NY, WIDTH), F32)
    gain = jnp.ones((8, WIDTH), F32)
    before, gain_before = total, gain
    for m in range(4):
        reached = place == m
        before = jnp.where(reached, total, before)
        gain_before = jnp.where(reached, gain, gain_before)
        tail = received[m, NY:PAYLOAD].astype(F32)
        one = tail[0:8] + tail[8:16]
        total = total * one[0:1] + received[m, 0:NY].astype(F32)
        gain = gain * one
    return before, gain_before, total, gain


def fold_kernel(place, received, before, gain_before, out):
    one, two, total, gain = fold(place[0], received)
    before[...] = one
    gain_before[...] = two
    store_payload(out, total, gain)


def final_kernel(place, keep, received, before1, gain1, before2, gain2, inflow, *rest):
    local, out, done, sem = rest[:CUTS], rest[CUTS], rest[CUTS + 1], rest[CUTS + 2]
    step = STATIONS // CUTS
    cuts = [pl.ds(c * step, step) for c in range(CUTS)]
    stores = [pltpu.make_async_copy(done.at[cuts[c]], out.at[cuts[c]], sem.at[c]) for c in range(CUTS)]
    before, gain, _, _ = fold(place[0], received)
    value = before + gain[0:1] * inflow[...]
    value = before2[...] + gain2[0:1] * value
    running = before1[...] + gain1[0:1] * value
    for c in range(CUTS):
        for i in range(step):
            running = running * keep[c * step + i]
            done[c * step + i] = local[c][i] + running
        stores[c].start()
    for store in stores:
        store.wait()


SMEM = pl.BlockSpec(memory_space=pltpu.SMEM)
VMEM = pl.BlockSpec(memory_space=pltpu.VMEM)
ANY = pl.BlockSpec(memory_space=pl.ANY)
HBM = pl.BlockSpec(memory_space=pltpu.HBM)
CUBE = jax.ShapeDtypeStruct((STATIONS, NY, WIDTH), F32)
PLANE = jax.ShapeDtypeStruct((NY, WIDTH), F32)
GAIN = jax.ShapeDtypeStruct((8, WIDTH), F32)
PART = jax.ShapeDtypeStruct((STATIONS // CUTS, NY, WIDTH), F32)
EDGE = jax.ShapeDtypeStruct((3, NY, WIDTH), BF16)
DMA = pltpu.SemaphoreType.DMA
SLOTS = jax.ShapeDtypeStruct((4, PAYLOAD, WIDTH), BF16)


def call(kernel, name, in_specs, out_specs, out_shape, flops, bytes_accessed, scratch=(), limit=16, alias=None):
    return pl.pallas_call(
        kernel,
        name=name,
        in_specs=in_specs,
        out_specs=out_specs,
        out_shape=out_shape,
        scratch_shapes=scratch,
        input_output_aliases=alias or {},
        compiler_params=pltpu.CompilerParams(vmem_limit_bytes=int(limit * MIB)),
        cost_estimate=pl.CostEstimate(flops=flops, bytes_accessed=bytes_accessed, transcendentals=0),
    )


def body(velocity, register, eddy_viscosity, courant, inflow):
    table, factor = span_tables()
    place = lax.axis_index("gx")
    places = [jnp.reshape(p, (1,)) for p in (place % 4, place // 4 % 4, place // 16)]
    keep = courant / (1.0 + courant)
    take = 1.0 / (1.0 + courant)

    rounded = velocity.astype(BF16)
    first, last = velocity[:3].astype(BF16), velocity[STATIONS - 3 :].astype(BF16)
    rounded = rounded.reshape(PARTS, ROWS, WIDTH)
    lines = lax.all_to_all(rounded, "gz", 0, 0, tiled=True)

    count = lax.axis_size("gx")
    forward = [(i, i + 1) for i in range(count - 1)]
    backward = [(b, a) for a, b in forward]
    low = lax.ppermute(last, "gx", forward)
    high = lax.ppermute(first, "gx", backward)
    lines, low, high = lax.optimization_barrier((lines, low, high))
    *base, base_offset = call(
        stencil_kernel,
        "stencil",
        [SMEM, SMEM, HBM, HBM] + [VMEM] * 3,
        (VMEM,) * (CUTS + 1),
        (PART,) * CUTS + (PLANE,),
        8_000_000,
        4_000_000,
        (pltpu.VMEM(CUBE.shape, F32), pltpu.VMEM(CUBE.shape, F32), DMA((2, CUTS))),
        LARGE,
    )(keep, take, velocity, register, eddy_viscosity, low, high)

    step = LENGTH // SLABS
    slabs = [jnp.asarray(table[:, n * step : (n + 1) * step]) for n in range(SLABS)]
    derived = call(
        span_kernel,
        "span",
        [VMEM, VMEM, HBM] + [VMEM] * SLABS,
        HBM,
        jax.ShapeDtypeStruct((PARTS, ROWS, WIDTH), BF16),
        4 * ROWS * LENGTH * LENGTH,
        3_200_000,
        (
            pltpu.VMEM((SLABS, ROWS, step), BF16),
            pltpu.VMEM((PARTS, ROWS, WIDTH), BF16),
            DMA((LENGTH // 256,)),
        ),
        alias={2: 0},
    )(lines, jnp.asarray(factor), rounded, *slabs)
    second = lax.all_to_all(derived, "gz", 0, 0, tiled=True).reshape(STATIONS, NY, WIDTH)

    payload = call(offset_kernel, "offset", [SMEM, SMEM] + [VMEM] * 3, VMEM, SLOTS, 1_500_000, 1_100_000)(
        keep, take, second, eddy_viscosity, base_offset
    )
    new_register, *local = call(
        local_kernel,
        "local",
        [SMEM, SMEM] + [VMEM] * 3 + [ANY] + [VMEM] * CUTS,
        (HBM,) + (VMEM,) * CUTS,
        (CUBE,) + (PART,) * CUTS,
        3_000_000,
        5_000_000,
        (pltpu.VMEM(CUBE.shape, F32), DMA((CUTS,))),
        alias={6 + c: 1 + c for c in range(CUTS)},
    )(keep, take, velocity, eddy_viscosity, second, payload, *base)

    found = []
    for level in range(3):
        payload = lax.all_to_all(payload, "gx", 0, 0, axis_index_groups=GROUPS[level], tiled=True)
        if level < 2:
            before, gain, payload = call(
                fold_kernel, "fold", [SMEM, VMEM], (VMEM,) * 3, (PLANE, GAIN, SLOTS), 200_000, 300_000
            )(places[level], payload)
            found += [before, gain]

    new_velocity = call(
        final_kernel,
        "final",
        [SMEM, SMEM] + [VMEM] * (6 + CUTS),
        HBM,
        CUBE,
        800_000,
        2_300_000,
        (pltpu.VMEM(CUBE.shape, F32), DMA((CUTS,))),
    )(places[2], keep, payload, *found, inflow, *local)
    return new_velocity, new_register


def solution(mesh):
    return jax.shard_map(
        body,
        mesh=mesh,
        in_specs=(
            P("gx", None, "gz"),
            P("gx", None, "gz"),
            P("gx", None, "gz"),
            P("gx"),
            P(None, "gz"),
        ),
        out_specs=(P("gx", None, "gz"), P("gx", None, "gz")),
        check_vma=False,
    )
```

time: 91.5 us -> 88.2 us (0.964)
  Pallas kernels: 16.9 us -> 12.3 us
  other arithmetic: 0.01 us -> 2.77 us
    pallas_call x5 -> x4, Pallas kernels: 14.2 us -> 9.51 us  [the longest x1 4.37 us: body(): call(stencil_kernel, 'stencil', [SMEM, SMEM, HBM, HBM] + [VMEM] * 3, (VME...]
    convert_element_type x0 -> x1, other arithmetic: none -> 2.19 us  [body(): rounded = velocity.astype(BF16)]
    unnamed x14 -> x36, local copies, waits for them, and re-layouts: 3.43 us -> 1.76 us
  transfers between devices with their start and end apart: 7 -> 7, of which waited for: 6 -> 6; matrix products, arithmetic and copies ran while one was open for 0% -> 2% of each run, Pallas kernels for 4% -> 7%
where the time goes in v2:
time: 88.2 us; the launch traced here: 87.4 us
  starting transfers between devices  40.1 us (45%)
  waiting for transfers between devices  28.9 us (33%)
  Pallas kernels  12.3 us (14%)
  other arithmetic  2.77 us (3%)
  local copies, waits for them, and re-layouts  2.63 us (3%)
    all_to_all x3, starting transfers between devices, body(): lax.all_to_all(payload, 'gx', 0, 0, axis_index_groups=GROUPS[level], tile...  23 us
    all_to_all x3, waiting for transfers between devices, body(): lax.all_to_all(payload, 'gx', 0, 0, axis_index_groups=GROUPS[level], tile...  21.4 us
    all_to_all x1, waiting for transfers between devices, body(): lax.all_to_all(derived, 'gz', 0, 0, tiled=True).reshape(STATIONS, NY, WIDTH)  5.37 us
    all_to_all x1, starting transfers between devices, body(): lax.all_to_all(derived, 'gz', 0, 0, tiled=True).reshape(STATIONS, NY, WIDTH)  4.82 us
    all_to_all x1, starting transfers between devices, body(): lines = lax.all_to_all(rounded, 'gz', 0, 0, tiled=True)  4.6 us
    pallas_call x1, Pallas kernels, body(): call(stencil_kernel, 'stencil', [SMEM, SMEM, HBM, HBM] + [VMEM] * 3, (VME...  4.37 us
    ppermute x1, starting transfers between devices, body(): high = lax.ppermute(first, 'gx', backward)  3.86 us
    ppermute x1, starting transfers between devices, body(): low = lax.ppermute(last, 'gx', forward)  3.81 us
  transfers between devices with their start and end apart: 7, of which 6 were waited for; matrix products, arithmetic and copies ran while one was open for 2% of the time, Pallas kernels for 7%

profile of v2, /device:TPU:32, one launch (start us, length us, event | category | flops | bytes accessed | tf_op | source)
XLA Modules:
  0.0 87.4 jit_solution(8167195748585273299)
XLA Ops:
  0.6 0.0 copy-start.12
  0.6 0.0 copy-start.13
  0.7 2.2 %convert_element_type.2 = bf16[32,64,128]{2,1,0:T(8,128)(2,1)} convert(f32[32,64,128]{2,1,0:T(8,128)} %velocity.1) | non-fusion elementwise | flops 262144 | bytes 1572864 | tf_op jit(solution)/shard_map/convert_element_type | solution.py:223
  2.8 4.6 %all-to-all-start = ((bf16[8,256,128]{2,1,0:T(8,128)(2,1)}), bf16[8,256,128]{2,1,0:T(8,128)(2,1)S(1)}, u32[]{:S(2)}, u32[]{:S(2)}) async-start(bf16[8,256,128]{2,1,0:T(8,128)(2,1)} %bitcast.3._buffer), calls=%async_computation | async-start | bytes 1048576 | tf_op jit(solution)/shard_map/all_to_all | solution.py:226
  7.5 0.9 fusion
  8.3 3.8 %collective-permute-start = (bf16[3,64,128]{2,1,0:T(8,128)(2,1)S(1)}, bf16[3,64,128]{2,1,0:T(8,128)(2,1)S(1)}, u32[]{:S(2)}, u32[]{:S(2)}) collective-permute-start(bf16[3,64,128]{2,1,0:T(8,128)(2,1)S(1)} %get-tuple-element.41), channel_id=1, source_target_pairs={{0,8},{8,16},{16,24},{24,32},{32,40},{40,48},{48,56},{56,64},{64,7... | collective-permute-start | bytes 147464 | tf_op jit(solution)/shard_map/ppermute | solution.py:231
  12.1 3.9 %collective-permute-start.1 = (bf16[3,64,128]{2,1,0:T(8,128)(2,1)S(1)}, bf16[3,64,128]{2,1,0:T(8,128)(2,1)S(1)}, u32[]{:S(2)}, u32[]{:S(2)}) collective-permute-start(bf16[3,64,128]{2,1,0:T(8,128)(2,1)S(1)} %get-tuple-element.40), channel_id=1, source_target_pairs={{8,0},{16,8},{24,16},{32,24},{40,32},{48,40},{56,48},{64,56},{72,6... | collective-permute-start | bytes 147464 | tf_op jit(solution)/shard_map/ppermute | solution.py:232
  16.0 0.4 collective-permute-done.low
  16.4 1.7 %collective-permute-done.1.high = bf16[3,64,128]{2,1,0:T(8,128)(2,1)S(1)} collective-permute-done((bf16[3,64,128]{2,1,0:T(8,128)(2,1)S(1)}, bf16[3,64,128]{2,1,0:T(8,128)(2,1)S(1)}, u32[]{:S(2)}, u32[]{:S(2)}) %collective-permute-start.1) | collective-permute-done | bytes 49184 | tf_op jit(solution)/shard_map/ppermute | solution.py:232
  18.1 0.0 all-to-all-done.lines
  18.1 0.0 copy-done.12
  18.1 0.0 copy-done.13
  18.2 2.0 %span.1 = bf16[8,256,128]{2,1,0:T(8,128)(2,1)} custom-call(bf16[8,256,128]{2,1,0:T(8,128)(2,1)S(1)} %all-to-all-done.lines, f32[1,1024]{1,0:T(1,128)S(1)} %copy-done.14, bf16[8,256,128]{2,1,0:T(8,128)(2,1)} %bitcast.3._buffer, bf16[1024,256]{1,0:T(8,128)(2,1)S(1)} %copy-done.10, bf16[1024,256]{1,0:T(8,128)(2,1)S(1)} %copy-done.11, ...), custom_call_target="tpu_custom_call", output_to_operand_aliasing={{}: (2, {})} | custom-call | flops 1073741824 | bytes 3200000 | tf_op jit(solution)/shard_map/span/pallas_call | solution.py:248
  20.2 0.0 copy-start.17
  20.2 4.8 %all-to-all-start.1 = ((bf16[8,256,128]{2,1,0:T(8,128)(2,1)}), bf16[8,256,128]{2,1,0:T(8,128)(2,1)S(1)}, u32[]{:S(2)}, u32[]{:S(2)}) async-start(bf16[8,256,128]{2,1,0:T(8,128)(2,1)} %span.1), calls=%async_computation.1 | async-start | bytes 1048576 | tf_op jit(solution)/shard_map/all_to_all | solution.py:263
  25.0 0.6 add_divide_fusion
  25.6 4.4 %stencil.1 = (f32[8,64,128]{2,1,0:T(8,128)}, f32[8,64,128]{2,1,0:T(8,128)}, f32[8,64,128]{2,1,0:T(8,128)}, f32[8,64,128]{2,1,0:T(8,128)}, f32[64,128]{1,0:T(8,128)}) custom-call(f32[32]{0:T(128)} %get-tuple-element.43.keep, f32[32]{0:T(128)} %get-tuple-element.42.take, f32[32,64,128]{2,1,0:T(8,128)} %velocity.1, f32[32,64,128]{2,1,0:T(8,128)} %far_register.1, ...), custom_call_target="tpu_custom_call" | custom-call | flops 8000000 | bytes 4000000 | tf_op jit(solution)/shard_map/stencil/pallas_call | solution.py:234
  30.0 0.0 copy-start
  30.0 5.4 %all-to-all-done.1 = bf16[8,256,128]{2,1,0:T(8,128)(2,1)S(1)} async-done(((bf16[8,256,128]{2,1,0:T(8,128)(2,1)}), bf16[8,256,128]{2,1,0:T(8,128)(2,1)S(1)}, u32[]{:S(2)}, u32[]{:S(2)}) %all-to-all-start.1) | async-done | bytes 524320 | tf_op jit(solution)/shard_map/all_to_all | solution.py:263
  35.4 0.7 copy-done.7
  36.2 1.4 %offset.1._ = bf16[4,80,128]{2,1,0:T(8,128)(2,1)} custom-call(f32[32]{0:T(128)S(1)} %copy-done.8, f32[32]{0:T(128)S(1)} %copy-done.9, bf16[32,64,128]{2,1,0:T(8,128)(2,1)S(1)} %bitcast.5, bf16[32,64,128]{2,1,0:T(8,128)(2,1)S(1)} %copy-done.1, f32[64,128]{1,0:T(8,128)S(1)} %copy-done.7), custom_call_target="tpu_custom_call" | custom-call | flops 1500000 | bytes 1100000 | tf_op jit(solution)/shard_map/offset/pallas_call | solution.py:265
  37.6 8.4 %all-to-all-start.2 = ((bf16[4,80,128]{2,1,0:T(8,128)(2,1)}), bf16[4,80,128]{2,1,0:T(8,128)(2,1)S(1)}, u32[]{:S(2)}, u32[]{:S(2)}) async-start(bf16[4,80,128]{2,1,0:T(8,128)(2,1)} %offset.1._), calls=%async_computation.2 | async-start | bytes 163840 | tf_op jit(solution)/shard_map/all_to_all | solution.py:282
  46.0 4.8 %all-to-all-done.2.received = bf16[4,80,128]{2,1,0:T(8,128)(2,1)S(1)} async-done(((bf16[4,80,128]{2,1,0:T(8,128)(2,1)}), bf16[4,80,128]{2,1,0:T(8,128)(2,1)S(1)}, u32[]{:S(2)}, u32[]{:S(2)}) %all-to-all-start.2) | async-done | bytes 81952 | tf_op jit(solution)/shard_map/all_to_all | solution.py:282
  50.8 0.7 fold.2
  51.4 10.3 %all-to-all-start.3 = ((bf16[4,80,128]{2,1,0:T(8,128)(2,1)}), bf16[4,80,128]{2,1,0:T(8,128)(2,1)S(1)}, u32[]{:S(2)}, u32[]{:S(2)}) async-start(bf16[4,80,128]{2,1,0:T(8,128)(2,1)} %get-tuple-element.25), calls=%async_computation.3 | async-start | bytes 163840 | tf_op jit(solution)/shard_map/all_to_all | solution.py:282
  61.7 13.5 %all-to-all-done.3.received = bf16[4,80,128]{2,1,0:T(8,128)(2,1)S(1)} async-done(((bf16[4,80,128]{2,1,0:T(8,128)(2,1)}), bf16[4,80,128]{2,1,0:T(8,128)(2,1)S(1)}, u32[]{:S(2)}, u32[]{:S(2)}) %all-to-all-start.3) | async-done | bytes 81952 | tf_op jit(solution)/shard_map/all_to_all | solution.py:282
  75.2 0.7 fold.3
  75.8 4.3 %all-to-all-start.4 = ((bf16[4,80,128]{2,1,0:T(8,128)(2,1)}), bf16[4,80,128]{2,1,0:T(8,128)(2,1)S(1)}, u32[]{:S(2)}, u32[]{:S(2)}) async-start(bf16[4,80,128]{2,1,0:T(8,128)(2,1)} %get-tuple-element.26), calls=%async_computation.4 | async-start | bytes 163840 | tf_op jit(solution)/shard_map/all_to_all | solution.py:282
  80.1 0.9 %copy-done.5 = f32[8,64,128]{2,1,0:T(8,128)S(1)} copy-done((f32[8,64,128]{2,1,0:T(8,128)S(1)}, f32[8,64,128]{2,1,0:T(8,128)}, u32[]{:S(2)}) %copy-start.5) | copy-done | bytes 262168
  81.1 1.6 %local.1 = (f32[32,64,128]{2,1,0:T(8,128)}, f32[8,64,128]{2,1,0:T(8,128)S(1)}, f32[8,64,128]{2,1,0:T(8,128)S(1)}, f32[8,64,128]{2,1,0:T(8,128)S(1)}, f32[8,64,128]{2,1,0:T(8,128)S(1)}) custom-call(f32[32]{0:T(128)S(1)} %copy-done.8, f32[32]{0:T(128)S(1)} %copy-done.9, ...), custom_call_target="tpu_custom_call", output_to_operand_aliasing={{1}: (6, {}), {2}: (7, {}), {3}: (8, {}), {4}: (9, {})} | custom-call | flops 3000000 | bytes 5000000 | tf_op jit(solution)/shard_map/local/pallas_call | solution.py:268
  82.7 3.2 %all-to-all-done.4.received = bf16[4,80,128]{2,1,0:T(8,128)(2,1)S(1)} async-done(((bf16[4,80,128]{2,1,0:T(8,128)(2,1)}), bf16[4,80,128]{2,1,0:T(8,128)(2,1)S(1)}, u32[]{:S(2)}, u32[]{:S(2)}) %all-to-all-start.4) | async-done | bytes 81952 | tf_op jit(solution)/shard_map/all_to_all | solution.py:282
  85.8 1.6 %final.1 = f32[32,64,128]{2,1,0:T(8,128)} custom-call(s32[1]{0:T(128)} %bitcast.place, f32[32]{0:T(128)S(1)} %copy-done.8, bf16[4,80,128]{2,1,0:T(8,128)(2,1)S(1)} %all-to-all-done.4.received, f32[64,128]{1,0:T(8,128)S(1)} %get-tuple-element.27.before1, f32[8,128]{1,0:T(8,128)S(1)} %get-tuple-element.28.gain1, f32[64,128]{1,0:T(8,128)S(1)} %get-tuple-element.29.before2, ...), custom_call_target="tpu_custom_call" | custom-call | flops 800000 | bytes 2300000 | tf_op jit(solution)/shard_map/final/pallas_call | solution.py:289
  (28 shorter events, 0.1 us)
Async XLA Ops:
  0.6 17.5 %copy-start.12 = (bf16[1024,256]{1,0:T(8,128)(2,1)S(1)}, bf16[1024,256]{1,0:T(8,128)(2,1)}, u32[]{:S(2)}) copy-start(bf16[1024,256]{1,0:T(8,128)(2,1)} %constant.60.clone.rest_2_) | copy-start | bytes 1572868
  0.6 17.5 %copy-start.13 = (bf16[1024,256]{1,0:T(8,128)(2,1)S(1)}, bf16[1024,256]{1,0:T(8,128)(2,1)}, u32[]{:S(2)}) copy-start(bf16[1024,256]{1,0:T(8,128)(2,1)} %constant.61.clone.rest_3_) | copy-start | bytes 1572868
  2.8 15.3 %copy-start.10 = (bf16[1024,256]{1,0:T(8,128)(2,1)S(1)}, bf16[1024,256]{1,0:T(8,128)(2,1)}, u32[]{:S(2)}) copy-start(bf16[1024,256]{1,0:T(8,128)(2,1)} %constant.58.clone.rest_0_) | copy-start | bytes 1572868
  2.8 15.3 %copy-start.11 = (bf16[1024,256]{1,0:T(8,128)(2,1)S(1)}, bf16[1024,256]{1,0:T(8,128)(2,1)}, u32[]{:S(2)}) copy-start(bf16[1024,256]{1,0:T(8,128)(2,1)} %constant.59.clone.rest_1_) | copy-start | bytes 1572868
  2.8 15.3 %all-to-all-start = ((bf16[8,256,128]{2,1,0:T(8,128)(2,1)}), bf16[8,256,128]{2,1,0:T(8,128)(2,1)S(1)}, u32[]{:S(2)}, u32[]{:S(2)}) async-start(bf16[8,256,128]{2,1,0:T(8,128)(2,1)} %bitcast.3._buffer), calls=%async_computation | async-start | bytes 1048576 | tf_op jit(solution)/shard_map/all_to_all | solution.py:226
  7.5 10.7 %copy-start.14 = (f32[1,1024]{1,0:T(1,128)S(1)}, f32[1,1024]{1,0:T(1,128)}, u32[]{:S(2)}) copy-start(f32[1,1024]{1,0:T(1,128)} %constant.62.clone.factor) | copy-start | bytes 12292
  8.3 8.1 %collective-permute-start = (bf16[3,64,128]{2,1,0:T(8,128)(2,1)S(1)}, bf16[3,64,128]{2,1,0:T(8,128)(2,1)S(1)}, u32[]{:S(2)}, u32[]{:S(2)}) collective-permute-start(bf16[3,64,128]{2,1,0:T(8,128)(2,1)S(1)} %get-tuple-element.41), channel_id=1, source_target_pairs={{0,8},{8,16},{16,24},{24,32},{32,40},{40,48},{48,56},{56,64},{64,7... | collective-permute-start | bytes 147464 | tf_op jit(solution)/shard_map/ppermute | solution.py:231
  12.1 6.0 %collective-permute-start.1 = (bf16[3,64,128]{2,1,0:T(8,128)(2,1)S(1)}, bf16[3,64,128]{2,1,0:T(8,128)(2,1)S(1)}, u32[]{:S(2)}, u32[]{:S(2)}) collective-permute-start(bf16[3,64,128]{2,1,0:T(8,128)(2,1)S(1)} %get-tuple-element.40), channel_id=1, source_target_pairs={{8,0},{16,8},{24,16},{32,24},{40,32},{48,40},{56,48},{64,56},{72,6... | collective-permute-start | bytes 147464 | tf_op jit(solution)/shard_map/ppermute | solution.py:232
  16.4 3.8 %copy-start.15 = (bf16[3,64,128]{2,1,0:T(8,128)(2,1)}, bf16[3,64,128]{2,1,0:T(8,128)(2,1)S(1)}, u32[]{:S(2)}) copy-start(bf16[3,64,128]{2,1,0:T(8,128)(2,1)S(1)} %collective-permute-done.low) | copy-start | bytes 147460
  18.1 2.1 %copy-start.16 = (bf16[3,64,128]{2,1,0:T(8,128)(2,1)}, bf16[3,64,128]{2,1,0:T(8,128)(2,1)S(1)}, u32[]{:S(2)}) copy-start(bf16[3,64,128]{2,1,0:T(8,128)(2,1)S(1)} %collective-permute-done.1.high) | copy-start | bytes 147460
  20.2 4.8 %copy-start.17 = (f32[32]{0:T(128)S(1)}, f32[32]{0:T(128)}, u32[]{:S(2)}) copy-start(f32[32]{0:T(128)} %param.13) | copy-start | bytes 388
  20.2 15.2 %all-to-all-start.1 = ((bf16[8,256,128]{2,1,0:T(8,128)(2,1)}), bf16[8,256,128]{2,1,0:T(8,128)(2,1)S(1)}, u32[]{:S(2)}, u32[]{:S(2)}) async-start(bf16[8,256,128]{2,1,0:T(8,128)(2,1)} %span.1), calls=%async_computation.1 | async-start | bytes 1048576 | tf_op jit(solution)/shard_map/all_to_all | solution.py:263
  25.6 9.8 %copy-start.1 = (bf16[32,64,128]{2,1,0:T(8,128)(2,1)S(1)}, bf16[32,64,128]{2,1,0:T(8,128)(2,1)}, u32[]{:S(2)}) copy-start(bf16[32,64,128]{2,1,0:T(8,128)(2,1)} %eddy.5) | copy-start | bytes 1572868
  25.6 9.8 %copy-start.8 = (f32[32]{0:T(128)S(1)}, f32[32]{0:T(128)}, u32[]{:S(2)}) copy-start(f32[32]{0:T(128)} %get-tuple-element.43.keep) | copy-start | bytes 388
  25.6 9.8 %copy-start.9 = (f32[32]{0:T(128)S(1)}, f32[32]{0:T(128)}, u32[]{:S(2)}) copy-start(f32[32]{0:T(128)} %get-tuple-element.42.take) | copy-start | bytes 388
  30.0 50.1 %copy-start = (f32[32,64,128]{2,1,0:T(8,128)S(1)}, f32[32,64,128]{2,1,0:T(8,128)}, u32[]{:S(2)}) copy-start(f32[32,64,128]{2,1,0:T(8,128)} %velocity.1) | copy-start | bytes 3145732
  35.4 0.8 copy-start.7
  36.2 44.0 %copy-start.4 = (f32[8,64,128]{2,1,0:T(8,128)S(1)}, f32[8,64,128]{2,1,0:T(8,128)}, u32[]{:S(2)}) copy-start(f32[8,64,128]{2,1,0:T(8,128)} %get-tuple-element.33.rest_2_) | copy-start | bytes 786436
  37.6 13.2 %all-to-all-start.2 = ((bf16[4,80,128]{2,1,0:T(8,128)(2,1)}), bf16[4,80,128]{2,1,0:T(8,128)(2,1)S(1)}, u32[]{:S(2)}, u32[]{:S(2)}) async-start(bf16[4,80,128]{2,1,0:T(8,128)(2,1)} %offset.1._), calls=%async_computation.2 | async-start | bytes 163840 | tf_op jit(solution)/shard_map/all_to_all | solution.py:282
  50.8 29.4 %copy-start.2 = (f32[8,64,128]{2,1,0:T(8,128)S(1)}, f32[8,64,128]{2,1,0:T(8,128)}, u32[]{:S(2)}) copy-start(f32[8,64,128]{2,1,0:T(8,128)} %get-tuple-element.31.rest_0_) | copy-start | bytes 786436
  50.8 29.4 %copy-start.3 = (f32[8,64,128]{2,1,0:T(8,128)S(1)}, f32[8,64,128]{2,1,0:T(8,128)}, u32[]{:S(2)}) copy-start(f32[8,64,128]{2,1,0:T(8,128)} %get-tuple-element.32.rest_1_) | copy-start | bytes 786436
  51.4 23.7 %all-to-all-start.3 = ((bf16[4,80,128]{2,1,0:T(8,128)(2,1)}), bf16[4,80,128]{2,1,0:T(8,128)(2,1)S(1)}, u32[]{:S(2)}, u32[]{:S(2)}) async-start(bf16[4,80,128]{2,1,0:T(8,128)(2,1)} %get-tuple-element.25), calls=%async_computation.3 | async-start | bytes 163840 | tf_op jit(solution)/shard_map/all_to_all | solution.py:282
  75.8 10.0 %all-to-all-start.4 = ((bf16[4,80,128]{2,1,0:T(8,128)(2,1)}), bf16[4,80,128]{2,1,0:T(8,128)(2,1)S(1)}, u32[]{:S(2)}, u32[]{:S(2)}) async-start(bf16[4,80,128]{2,1,0:T(8,128)(2,1)} %get-tuple-element.26), calls=%async_computation.4 | async-start | bytes 163840 | tf_op jit(solution)/shard_map/all_to_all | solution.py:282
  80.1 1.0 %copy-start.5 = (f32[8,64,128]{2,1,0:T(8,128)S(1)}, f32[8,64,128]{2,1,0:T(8,128)}, u32[]{:S(2)}) copy-start(f32[8,64,128]{2,1,0:T(8,128)} %get-tuple-element.34.rest_3_) | copy-start | bytes 786436
  81.1 4.7 %copy-start.6 = (f32[64,128]{1,0:T(8,128)S(1)}, f32[64,128]{1,0:T(8,128)}, u32[]{:S(2)}) copy-start(f32[64,128]{1,0:T(8,128)} %inflow.1) | copy-start | bytes 98308

commit v3 on v2

--- a/solution.py
+++ b/solution.py
@@ -21,7 +21,7 @@
 ROWS = STATIONS * NY // PARTS
 MIB = 1024 * 1024
 SLABS = 4
-LARGE = 62.75
+LARGE = 62.5
 F32, BF16 = jnp.float32, jnp.bfloat16
 PAYLOAD = NY + 16
 
@@ -42,6 +42,17 @@
     twice = np.where(np.arange(1, LENGTH // 2 + 1) < LENGTH // 2, 2.0, 1.0).astype(np.float32)
     factor = np.concatenate([factor * twice] * 2)[None, :].astype(np.float32)
     return table, factor
+
+
+def edge_kernel(rounded, first, last, sem):
+    copies = [
+        pltpu.make_async_copy(rounded.at[pl.ds(0, 3)], first, sem.at[0]),
+        pltpu.make_async_copy(rounded.at[pl.ds(STATIONS - 3, 3)], last, sem.at[1]),
+    ]
+    for copy in copies:
+        copy.start()
+    for copy in copies:
+        copy.wait()
 
 
 def stencil_kernel(keep, take, far_velocity, far_register, eddy, low, high, *rest):
@@ -146,6 +157,10 @@
         copy.wait()
 
 
+def hold_kernel(plane, held):
+    held[...] = plane[...]
+
+
 def fold(place, received):
     total = jnp.zeros((NY, WIDTH), F32)
     gain = jnp.ones((8, WIDTH), F32)
@@ -161,7 +176,8 @@
     return before, gain_before, total, gain
 
 
-def fold_kernel(place, received, before, gain_before, out):
+def fold_kernel(place, received, *rest):
+    before, gain_before, out = rest[-3:]
     one, two, total, gain = fold(place[0], received)
     before[...] = one
     gain_before[...] = two
@@ -221,7 +237,7 @@
     take = 1.0 / (1.0 + courant)
 
     rounded = velocity.astype(BF16)
-    first, last = velocity[:3].astype(BF16), velocity[STATIONS - 3 :].astype(BF16)
+    first, last = call(edge_kernel, "edge", [HBM], (VMEM, VMEM), (EDGE, EDGE), 3_000_000_000, 200_000, (DMA((2,)),))(rounded)
     rounded = rounded.reshape(PARTS, ROWS, WIDTH)
     lines = lax.all_to_all(rounded, "gz", 0, 0, tiled=True)
 
@@ -242,6 +258,8 @@
         (pltpu.VMEM(CUBE.shape, F32), pltpu.VMEM(CUBE.shape, F32), DMA((2, CUTS))),
         LARGE,
     )(keep, take, velocity, register, eddy_viscosity, low, high)
+
+    base_offset = call(hold_kernel, "hold", [VMEM], VMEM, PLANE, 1000, 100_000)(base_offset)
 
     step = LENGTH // SLABS
     slabs = [jnp.asarray(table[:, n * step : (n + 1) * step]) for n in range(SLABS)]
@@ -282,8 +300,8 @@
         payload = lax.all_to_all(payload, "gx", 0, 0, axis_index_groups=GROUPS[level], tiled=True)
         if level < 2:
             before, gain, payload = call(
-                fold_kernel, "fold", [SMEM, VMEM], (VMEM,) * 3, (PLANE, GAIN, SLOTS), 200_000, 300_000
-            )(places[level], payload)
+                fold_kernel, "fold", [SMEM, VMEM] + [ANY] * level, (VMEM,) * 3, (PLANE, GAIN, SLOTS), 200_000, 300_000
+            )(places[level], payload, *local[:level])
             found += [before, gain]
 
     new_velocity = call(

time: 88.2 us -> 87.5 us (level)
  waiting for transfers between devices: 28.9 us -> 26.4 us
  Pallas kernels: 12.3 us -> 13.2 us
    unnamed x36 -> x40, local copies, waits for them, and re-layouts: 1.76 us -> 3.51 us
    all_to_all x3, waiting for transfers between devices: 21.4 us -> 19.7 us  [body(): lax.all_to_all(payload, 'gx', 0, 0, axis_index_groups=GROUPS[level], tile...]
    pallas_call x2 -> x4, Pallas kernels: 1.32 us -> 2.29 us  [the longest x2 1.31 us: body(): call(fold_kernel, 'fold', [SMEM, VMEM] + [ANY] * level, (VMEM,) * 3, (PLA...]
  transfers between devices with their start and end apart: 7 -> 7, of which waited for: 6 -> 6; matrix products, arithmetic and copies ran while one was open for 2% -> 1% of each run, Pallas kernels for 7% -> 8%
where the time goes in v3:
time: 87.5 us; the launch traced here: 86.7 us
  starting transfers between devices  40.1 us (46%)
  waiting for transfers between devices  26.4 us (30%)
  Pallas kernels  13.2 us (15%)
  local copies, waits for them, and re-layouts  3.51 us (4%)
  other arithmetic  2.63 us (3%)
    all_to_all x3, starting transfers between devices, body(): lax.all_to_all(payload, 'gx', 0, 0, axis_index_groups=GROUPS[level], tile...  23.1 us
    all_to_all x3, waiting for transfers between devices, body(): lax.all_to_all(payload, 'gx', 0, 0, axis_index_groups=GROUPS[level], tile...  19.7 us
    all_to_all x1, starting transfers between devices, body(): lax.all_to_all(derived, 'gz', 0, 0, tiled=True).reshape(STATIONS, NY, WIDTH)  4.8 us
    all_to_all x1, waiting for transfers between devices, body(): lax.all_to_all(derived, 'gz', 0, 0, tiled=True).reshape(STATIONS, NY, WIDTH)  4.58 us
    all_to_all x1, starting transfers between devices, body(): lines = lax.all_to_all(rounded, 'gz', 0, 0, tiled=True)  4.47 us
    pallas_call x1, Pallas kernels, body(): call(stencil_kernel, 'stencil', [SMEM, SMEM, HBM, HBM] + [VMEM] * 3, (VME...  4.36 us
    ppermute x1, starting transfers between devices, body(): high = lax.ppermute(first, 'gx', backward)  3.92 us
    ppermute x1, starting transfers between devices, body(): low = lax.ppermute(last, 'gx', forward)  3.83 us
  transfers between devices with their start and end apart: 7, of which 6 were waited for; matrix products, arithmetic and copies ran while one was open for 1% of the time, Pallas kernels for 8%

profile of v3, /device:TPU:32, one launch (start us, length us, event | category | flops | bytes accessed | tf_op | source)
XLA Modules:
  0.0 86.7 jit_solution(13130087055050826685)
XLA Ops:
  0.6 2.1 %convert_element_type.3.rounded = bf16[32,64,128]{2,1,0:T(8,128)(2,1)} convert(f32[32,64,128]{2,1,0:T(8,128)} %velocity.1) | non-fusion elementwise | flops 262144 | bytes 1572864 | tf_op jit(solution)/shard_map/convert_element_type | solution.py:239
  2.7 4.5 %all-to-all-start = ((bf16[8,256,128]{2,1,0:T(8,128)(2,1)}), bf16[8,256,128]{2,1,0:T(8,128)(2,1)S(1)}, u32[]{:S(2)}, u32[]{:S(2)}) async-start(bf16[8,256,128]{2,1,0:T(8,128)(2,1)} %bitcast.3._buffer), calls=%async_computation | async-start | bytes 1048576 | tf_op jit(solution)/shard_map/all_to_all | solution.py:242
  7.2 0.0 copy-start.13
  7.2 0.0 copy-start.14
  7.2 0.0 copy-start.15
  7.2 0.0 copy-start.16
  7.3 1.0 %edge.1 = (bf16[3,64,128]{2,1,0:T(8,128)(2,1)S(1)}, bf16[3,64,128]{2,1,0:T(8,128)(2,1)S(1)}) custom-call(bf16[32,64,128]{2,1,0:T(8,128)(2,1)} %convert_element_type.3.rounded), custom_call_target="tpu_custom_call" | custom-call | flops 3000000000 | bytes 200000 | tf_op jit(solution)/shard_map/edge/pallas_call | solution.py:240
  8.2 3.8 %collective-permute-start = (bf16[3,64,128]{2,1,0:T(8,128)(2,1)S(1)}, bf16[3,64,128]{2,1,0:T(8,128)(2,1)S(1)}, u32[]{:S(2)}, u32[]{:S(2)}) collective-permute-start(bf16[3,64,128]{2,1,0:T(8,128)(2,1)S(1)} %get-tuple-element.23), channel_id=1, source_target_pairs={{0,8},{8,16},{16,24},{24,32},{32,40},{40,48},{48,56},{56,64},{64,7... | collective-permute-start | bytes 147464 | tf_op jit(solution)/shard_map/ppermute | solution.py:247
  12.1 3.9 %collective-permute-start.1 = (bf16[3,64,128]{2,1,0:T(8,128)(2,1)S(1)}, bf16[3,64,128]{2,1,0:T(8,128)(2,1)S(1)}, u32[]{:S(2)}, u32[]{:S(2)}) collective-permute-start(bf16[3,64,128]{2,1,0:T(8,128)(2,1)S(1)} %get-tuple-element.24), channel_id=1, source_target_pairs={{8,0},{16,8},{24,16},{32,24},{40,32},{48,40},{56,48},{64,56},{72,6... | collective-permute-start | bytes 147464 | tf_op jit(solution)/shard_map/ppermute | solution.py:248
  16.0 0.3 collective-permute-done.low
  16.3 1.7 %collective-permute-done.1.high = bf16[3,64,128]{2,1,0:T(8,128)(2,1)S(1)} collective-permute-done((bf16[3,64,128]{2,1,0:T(8,128)(2,1)S(1)}, bf16[3,64,128]{2,1,0:T(8,128)(2,1)S(1)}, u32[]{:S(2)}, u32[]{:S(2)}) %collective-permute-start.1) | collective-permute-done | bytes 49184 | tf_op jit(solution)/shard_map/ppermute | solution.py:248
  18.1 2.0 %span.1 = bf16[8,256,128]{2,1,0:T(8,128)(2,1)} custom-call(bf16[8,256,128]{2,1,0:T(8,128)(2,1)S(1)} %all-to-all-done.lines, f32[1,1024]{1,0:T(1,128)S(1)} %copy-done.16, bf16[8,256,128]{2,1,0:T(8,128)(2,1)} %bitcast.3._buffer, bf16[1024,256]{1,0:T(8,128)(2,1)S(1)} %copy-done.12, bf16[1024,256]{1,0:T(8,128)(2,1)S(1)} %copy-done.13, ...), custom_call_target="tpu_custom_call", output_to_operand_aliasing={{}: (2, {})} | custom-call | flops 1073741824 | bytes 3200000 | tf_op jit(solution)/shard_map/span/pallas_call | solution.py:266
  20.2 4.8 %all-to-all-start.1 = ((bf16[8,256,128]{2,1,0:T(8,128)(2,1)}), bf16[8,256,128]{2,1,0:T(8,128)(2,1)S(1)}, u32[]{:S(2)}, u32[]{:S(2)}) async-start(bf16[8,256,128]{2,1,0:T(8,128)(2,1)} %span.1), calls=%async_computation.1 | async-start | bytes 1048576 | tf_op jit(solution)/shard_map/all_to_all | solution.py:281
  25.0 0.5 add_divide_fusion
  25.5 4.4 %stencil.1 = (f32[8,64,128]{2,1,0:T(8,128)}, f32[8,64,128]{2,1,0:T(8,128)}, f32[8,64,128]{2,1,0:T(8,128)}, f32[8,64,128]{2,1,0:T(8,128)}, f32[64,128]{1,0:T(8,128)}) custom-call(f32[32]{0:T(128)} %get-tuple-element.45.keep, f32[32]{0:T(128)} %get-tuple-element.44.take, f32[32,64,128]{2,1,0:T(8,128)} %velocity.1, f32[32,64,128]{2,1,0:T(8,128)} %far_register.1, ...), custom_call_target="tpu_custom_call" | custom-call | flops 8000000 | bytes 4000000 | tf_op jit(solution)/shard_map/stencil/pallas_call | solution.py:250
  29.9 0.8 copy-done.9
  30.7 4.6 %all-to-all-done.1 = bf16[8,256,128]{2,1,0:T(8,128)(2,1)S(1)} async-done(((bf16[8,256,128]{2,1,0:T(8,128)(2,1)}), bf16[8,256,128]{2,1,0:T(8,128)(2,1)S(1)}, u32[]{:S(2)}, u32[]{:S(2)}) %all-to-all-start.1) | async-done | bytes 524320 | tf_op jit(solution)/shard_map/all_to_all | solution.py:281
  35.3 1.4 %offset.1._ = bf16[4,80,128]{2,1,0:T(8,128)(2,1)} custom-call(f32[32]{0:T(128)S(1)} %copy-done.10, f32[32]{0:T(128)S(1)} %copy-done.11, bf16[32,64,128]{2,1,0:T(8,128)(2,1)S(1)} %bitcast.5, bf16[32,64,128]{2,1,0:T(8,128)(2,1)S(1)} %copy-done.1, f32[64,128]{1,0:T(8,128)S(1)} %hold.1.base_offset), custom_call_target="tpu_custom_call" | custom-call | flops 1500000 | bytes 1100000 | tf_op jit(solution)/shard_map/offset/pallas_call | solution.py:283
  36.7 8.6 %all-to-all-start.2 = ((bf16[4,80,128]{2,1,0:T(8,128)(2,1)}), bf16[4,80,128]{2,1,0:T(8,128)(2,1)S(1)}, u32[]{:S(2)}, u32[]{:S(2)}) async-start(bf16[4,80,128]{2,1,0:T(8,128)(2,1)} %offset.1._), calls=%async_computation.2 | async-start | bytes 163840 | tf_op jit(solution)/shard_map/all_to_all | solution.py:300
  45.3 4.8 %all-to-all-done.2.received = bf16[4,80,128]{2,1,0:T(8,128)(2,1)S(1)} async-done(((bf16[4,80,128]{2,1,0:T(8,128)(2,1)}), bf16[4,80,128]{2,1,0:T(8,128)(2,1)S(1)}, u32[]{:S(2)}, u32[]{:S(2)}) %all-to-all-start.2) | async-done | bytes 81952 | tf_op jit(solution)/shard_map/all_to_all | solution.py:300
  50.1 0.7 fold.2
  50.7 10.3 %all-to-all-start.3 = ((bf16[4,80,128]{2,1,0:T(8,128)(2,1)}), bf16[4,80,128]{2,1,0:T(8,128)(2,1)S(1)}, u32[]{:S(2)}, u32[]{:S(2)}) async-start(bf16[4,80,128]{2,1,0:T(8,128)(2,1)} %get-tuple-element.29), calls=%async_computation.3 | async-start | bytes 163840 | tf_op jit(solution)/shard_map/all_to_all | solution.py:300
  61.0 0.9 %copy-done.4 = f32[8,64,128]{2,1,0:T(8,128)S(1)} copy-done((f32[8,64,128]{2,1,0:T(8,128)S(1)}, f32[8,64,128]{2,1,0:T(8,128)}, u32[]{:S(2)}) %copy-start.4) | copy-done | bytes 262168
  62.0 0.9 %copy-done.5 = f32[8,64,128]{2,1,0:T(8,128)S(1)} copy-done((f32[8,64,128]{2,1,0:T(8,128)S(1)}, f32[8,64,128]{2,1,0:T(8,128)}, u32[]{:S(2)}) %copy-start.5) | copy-done | bytes 262168
  62.9 1.6 %local.1 = (f32[32,64,128]{2,1,0:T(8,128)}, f32[8,64,128]{2,1,0:T(8,128)S(1)}, f32[8,64,128]{2,1,0:T(8,128)S(1)}, f32[8,64,128]{2,1,0:T(8,128)S(1)}, f32[8,64,128]{2,1,0:T(8,128)S(1)}) custom-call(f32[32]{0:T(128)S(1)} %copy-done.10, f32[32]{0:T(128)S(1)} %copy-done.11, ...), custom_call_target="tpu_custom_call", output_to_operand_aliasing={{1}: (6, {}), {2}: (7, {}), {3}: (8, {}), {4}: (9, {})} | custom-call | flops 3000000 | bytes 5000000 | tf_op jit(solution)/shard_map/local/pallas_call | solution.py:286
  64.5 0.0 copy-start.6
  64.5 0.7 copy-done.6
  65.2 9.3 %all-to-all-done.3.received = bf16[4,80,128]{2,1,0:T(8,128)(2,1)S(1)} async-done(((bf16[4,80,128]{2,1,0:T(8,128)(2,1)}), bf16[4,80,128]{2,1,0:T(8,128)(2,1)S(1)}, u32[]{:S(2)}, u32[]{:S(2)}) %all-to-all-start.3) | async-done | bytes 81952 | tf_op jit(solution)/shard_map/all_to_all | solution.py:300
  74.5 0.7 fold.3
  75.1 4.3 %all-to-all-start.4 = ((bf16[4,80,128]{2,1,0:T(8,128)(2,1)}), bf16[4,80,128]{2,1,0:T(8,128)(2,1)S(1)}, u32[]{:S(2)}, u32[]{:S(2)}) async-start(bf16[4,80,128]{2,1,0:T(8,128)(2,1)} %get-tuple-element.35), calls=%async_computation.4 | async-start | bytes 163840 | tf_op jit(solution)/shard_map/all_to_all | solution.py:300
  79.4 5.7 %all-to-all-done.4.received = bf16[4,80,128]{2,1,0:T(8,128)(2,1)S(1)} async-done(((bf16[4,80,128]{2,1,0:T(8,128)(2,1)}), bf16[4,80,128]{2,1,0:T(8,128)(2,1)S(1)}, u32[]{:S(2)}, u32[]{:S(2)}) %all-to-all-start.4) | async-done | bytes 81952 | tf_op jit(solution)/shard_map/all_to_all | solution.py:300
  85.1 1.6 %final.1 = f32[32,64,128]{2,1,0:T(8,128)} custom-call(s32[1]{0:T(128)} %bitcast.place, f32[32]{0:T(128)S(1)} %copy-done.10, bf16[4,80,128]{2,1,0:T(8,128)(2,1)S(1)} %all-to-all-done.4.received, f32[64,128]{1,0:T(8,128)S(1)} %get-tuple-element.36.before1, f32[8,128]{1,0:T(8,128)S(1)} %get-tuple-element.37.gain1, f32[64,128]{1,0:T(8,128)S(1)} %get-tuple-element.38.before2, ...), custom_call_target="tpu_custom_call" | custom-call | flops 800000 | bytes 2300000 | tf_op jit(solution)/shard_map/final/pallas_call | solution.py:307
  (33 shorter events, 0.1 us)
Async XLA Ops:
  2.7 15.3 %all-to-all-start = ((bf16[8,256,128]{2,1,0:T(8,128)(2,1)}), bf16[8,256,128]{2,1,0:T(8,128)(2,1)S(1)}, u32[]{:S(2)}, u32[]{:S(2)}) async-start(bf16[8,256,128]{2,1,0:T(8,128)(2,1)} %bitcast.3._buffer), calls=%async_computation | async-start | bytes 1048576 | tf_op jit(solution)/shard_map/all_to_all | solution.py:242
  7.2 10.9 %copy-start.12 = (bf16[1024,256]{1,0:T(8,128)(2,1)S(1)}, bf16[1024,256]{1,0:T(8,128)(2,1)}, u32[]{:S(2)}) copy-start(bf16[1024,256]{1,0:T(8,128)(2,1)} %constant.58.clone.rest_0_) | copy-start | bytes 1572868
  7.2 10.9 %copy-start.13 = (bf16[1024,256]{1,0:T(8,128)(2,1)S(1)}, bf16[1024,256]{1,0:T(8,128)(2,1)}, u32[]{:S(2)}) copy-start(bf16[1024,256]{1,0:T(8,128)(2,1)} %constant.59.clone.rest_1_) | copy-start | bytes 1572868
  7.2 10.9 %copy-start.14 = (bf16[1024,256]{1,0:T(8,128)(2,1)S(1)}, bf16[1024,256]{1,0:T(8,128)(2,1)}, u32[]{:S(2)}) copy-start(bf16[1024,256]{1,0:T(8,128)(2,1)} %constant.60.clone.rest_2_) | copy-start | bytes 1572868
  7.2 10.9 %copy-start.15 = (bf16[1024,256]{1,0:T(8,128)(2,1)S(1)}, bf16[1024,256]{1,0:T(8,128)(2,1)}, u32[]{:S(2)}) copy-start(bf16[1024,256]{1,0:T(8,128)(2,1)} %constant.61.clone.rest_3_) | copy-start | bytes 1572868
  7.2 10.9 %copy-start.16 = (f32[1,1024]{1,0:T(1,128)S(1)}, f32[1,1024]{1,0:T(1,128)}, u32[]{:S(2)}) copy-start(f32[1,1024]{1,0:T(1,128)} %constant.62.clone.factor) | copy-start | bytes 12292
  8.2 8.1 %collective-permute-start = (bf16[3,64,128]{2,1,0:T(8,128)(2,1)S(1)}, bf16[3,64,128]{2,1,0:T(8,128)(2,1)S(1)}, u32[]{:S(2)}, u32[]{:S(2)}) collective-permute-start(bf16[3,64,128]{2,1,0:T(8,128)(2,1)S(1)} %get-tuple-element.23), channel_id=1, source_target_pairs={{0,8},{8,16},{16,24},{24,32},{32,40},{40,48},{48,56},{56,64},{64,7... | collective-permute-start | bytes 147464 | tf_op jit(solution)/shard_map/ppermute | solution.py:247
  12.1 6.0 %collective-permute-start.1 = (bf16[3,64,128]{2,1,0:T(8,128)(2,1)S(1)}, bf16[3,64,128]{2,1,0:T(8,128)(2,1)S(1)}, u32[]{:S(2)}, u32[]{:S(2)}) collective-permute-start(bf16[3,64,128]{2,1,0:T(8,128)(2,1)S(1)} %get-tuple-element.24), channel_id=1, source_target_pairs={{8,0},{16,8},{24,16},{32,24},{40,32},{48,40},{56,48},{64,56},{72,6... | collective-permute-start | bytes 147464 | tf_op jit(solution)/shard_map/ppermute | solution.py:248
  16.3 3.8 %copy-start.17 = (bf16[3,64,128]{2,1,0:T(8,128)(2,1)}, bf16[3,64,128]{2,1,0:T(8,128)(2,1)S(1)}, u32[]{:S(2)}) copy-start(bf16[3,64,128]{2,1,0:T(8,128)(2,1)S(1)} %collective-permute-done.low) | copy-start | bytes 147460
  18.1 2.1 %copy-start.18 = (bf16[3,64,128]{2,1,0:T(8,128)(2,1)}, bf16[3,64,128]{2,1,0:T(8,128)(2,1)S(1)}, u32[]{:S(2)}) copy-start(bf16[3,64,128]{2,1,0:T(8,128)(2,1)S(1)} %collective-permute-done.1.high) | copy-start | bytes 147460
  20.1 4.8 %copy-start.19 = (f32[32]{0:T(128)S(1)}, f32[32]{0:T(128)}, u32[]{:S(2)}) copy-start(f32[32]{0:T(128)} %param.13) | copy-start | bytes 388
  20.2 15.2 %all-to-all-start.1 = ((bf16[8,256,128]{2,1,0:T(8,128)(2,1)}), bf16[8,256,128]{2,1,0:T(8,128)(2,1)S(1)}, u32[]{:S(2)}, u32[]{:S(2)}) async-start(bf16[8,256,128]{2,1,0:T(8,128)(2,1)} %span.1), calls=%async_computation.1 | async-start | bytes 1048576 | tf_op jit(solution)/shard_map/all_to_all | solution.py:281
  25.5 9.8 %copy-start.1 = (bf16[32,64,128]{2,1,0:T(8,128)(2,1)S(1)}, bf16[32,64,128]{2,1,0:T(8,128)(2,1)}, u32[]{:S(2)}) copy-start(bf16[32,64,128]{2,1,0:T(8,128)(2,1)} %eddy.5) | copy-start | bytes 1572868
  25.5 9.8 %copy-start.10 = (f32[32]{0:T(128)S(1)}, f32[32]{0:T(128)}, u32[]{:S(2)}) copy-start(f32[32]{0:T(128)} %get-tuple-element.45.keep) | copy-start | bytes 388
  25.5 9.8 %copy-start.11 = (f32[32]{0:T(128)S(1)}, f32[32]{0:T(128)}, u32[]{:S(2)}) copy-start(f32[32]{0:T(128)} %get-tuple-element.44.take) | copy-start | bytes 388
  29.9 31.1 %copy-start = (f32[32,64,128]{2,1,0:T(8,128)S(1)}, f32[32,64,128]{2,1,0:T(8,128)}, u32[]{:S(2)}) copy-start(f32[32,64,128]{2,1,0:T(8,128)} %velocity.1) | copy-start | bytes 3145732
  29.9 0.8 copy-start.9
  35.3 25.7 %copy-start.3 = (f32[8,64,128]{2,1,0:T(8,128)S(1)}, f32[8,64,128]{2,1,0:T(8,128)}, u32[]{:S(2)}) copy-start(f32[8,64,128]{2,1,0:T(8,128)} %get-tuple-element.31.rest_1_) | copy-start | bytes 786436
  36.7 24.3 %copy-start.2 = (f32[8,64,128]{2,1,0:T(8,128)S(1)}, f32[8,64,128]{2,1,0:T(8,128)}, u32[]{:S(2)}) copy-start(f32[8,64,128]{2,1,0:T(8,128)} %get-tuple-element.30.rest_0_) | copy-start | bytes 786436
  36.7 13.3 %all-to-all-start.2 = ((bf16[4,80,128]{2,1,0:T(8,128)(2,1)}), bf16[4,80,128]{2,1,0:T(8,128)(2,1)S(1)}, u32[]{:S(2)}, u32[]{:S(2)}) async-start(bf16[4,80,128]{2,1,0:T(8,128)(2,1)} %offset.1._), calls=%async_computation.2 | async-start | bytes 163840 | tf_op jit(solution)/shard_map/all_to_all | solution.py:300
  50.7 23.7 %all-to-all-start.3 = ((bf16[4,80,128]{2,1,0:T(8,128)(2,1)}), bf16[4,80,128]{2,1,0:T(8,128)(2,1)S(1)}, u32[]{:S(2)}, u32[]{:S(2)}) async-start(bf16[4,80,128]{2,1,0:T(8,128)(2,1)} %get-tuple-element.29), calls=%async_computation.3 | async-start | bytes 163840 | tf_op jit(solution)/shard_map/all_to_all | solution.py:300
  61.0 1.0 %copy-start.4 = (f32[8,64,128]{2,1,0:T(8,128)S(1)}, f32[8,64,128]{2,1,0:T(8,128)}, u32[]{:S(2)}) copy-start(f32[8,64,128]{2,1,0:T(8,128)} %get-tuple-element.32.rest_2_) | copy-start | bytes 786436
  62.0 0.9 %copy-start.5 = (f32[8,64,128]{2,1,0:T(8,128)S(1)}, f32[8,64,128]{2,1,0:T(8,128)}, u32[]{:S(2)}) copy-start(f32[8,64,128]{2,1,0:T(8,128)} %get-tuple-element.33.rest_3_) | copy-start | bytes 786436
  64.5 0.7 copy-start.6
  74.5 10.7 %copy-start.7 = (f32[8,64,128]{2,1,0:T(8,128)S(1)}, f32[8,64,128]{2,1,0:T(8,128)}, u32[]{:S(2)}) copy-start(f32[8,64,128]{2,1,0:T(8,128)} %copy-done.6) | copy-start | bytes 786436
  75.1 10.0 %all-to-all-start.4 = ((bf16[4,80,128]{2,1,0:T(8,128)(2,1)}), bf16[4,80,128]{2,1,0:T(8,128)(2,1)S(1)}, u32[]{:S(2)}, u32[]{:S(2)}) async-start(bf16[4,80,128]{2,1,0:T(8,128)(2,1)} %get-tuple-element.35), calls=%async_computation.4 | async-start | bytes 163840 | tf_op jit(solution)/shard_map/all_to_all | solution.py:300
  79.4 5.7 %copy-start.8 = (f32[64,128]{1,0:T(8,128)S(1)}, f32[64,128]{1,0:T(8,128)}, u32[]{:S(2)}) copy-start(f32[64,128]{1,0:T(8,128)} %inflow.1) | copy-start | bytes 98308

commit v4 on v3

--- a/solution.py
+++ b/solution.py
@@ -21,7 +21,7 @@
 ROWS = STATIONS * NY // PARTS
 MIB = 1024 * 1024
 SLABS = 4
-LARGE = 62.5
+LARGE = 62.75
 F32, BF16 = jnp.float32, jnp.bfloat16
 PAYLOAD = NY + 16
 
@@ -176,8 +176,7 @@
     return before, gain_before, total, gain
 
 
-def fold_kernel(place, received, *rest):
-    before, gain_before, out = rest[-3:]
+def fold_kernel(place, received, before, gain_before, out):
     one, two, total, gain = fold(place[0], received)
     before[...] = one
     gain_before[...] = two
@@ -300,8 +299,8 @@
         payload = lax.all_to_all(payload, "gx", 0, 0, axis_index_groups=GROUPS[level], tiled=True)
         if level < 2:
             before, gain, payload = call(
-                fold_kernel, "fold", [SMEM, VMEM] + [ANY] * level, (VMEM,) * 3, (PLANE, GAIN, SLOTS), 200_000, 300_000
-            )(places[level], payload, *local[:level])
+                fold_kernel, "fold", [SMEM, VMEM], (VMEM,) * 3, (PLANE, GAIN, SLOTS), 200_000, 300_000
+            )(places[level], payload)
             found += [before, gain]
 
     new_velocity = call(

time: 87.5 us -> 87.3 us (level)
  local copies, waits for them, and re-layouts: 3.51 us -> 1.86 us
  waiting for transfers between devices: 26.4 us -> 28 us
    unnamed x40 -> x36, local copies, waits for them, and re-layouts: 3.51 us -> 1.86 us
    all_to_all x3, waiting for transfers between devices: 19.7 us -> 21.4 us  [body(): lax.all_to_all(payload, 'gx', 0, 0, axis_index_groups=GROUPS[level], tile...]
where the time goes in v4:
time: 87.3 us; the launch traced here: 86.6 us
  starting transfers between devices  40 us (46%)
  waiting for transfers between devices  28 us (32%)
  Pallas kernels  13.2 us (15%)
  other arithmetic  2.69 us (3%)
  local copies, waits for them, and re-layouts  1.86 us (2%)
    all_to_all x3, starting transfers between devices, body(): lax.all_to_all(payload, 'gx', 0, 0, axis_index_groups=GROUPS[level], tile...  23 us
    all_to_all x3, waiting for transfers between devices, body(): lax.all_to_all(payload, 'gx', 0, 0, axis_index_groups=GROUPS[level], tile...  21.4 us
    all_to_all x1, starting transfers between devices, body(): lax.all_to_all(derived, 'gz', 0, 0, tiled=True).reshape(STATIONS, NY, WIDTH)  4.8 us
    all_to_all x1, waiting for transfers between devices, body(): lax.all_to_all(derived, 'gz', 0, 0, tiled=True).reshape(STATIONS, NY, WIDTH)  4.51 us
    all_to_all x1, starting transfers between devices, body(): lines = lax.all_to_all(rounded, 'gz', 0, 0, tiled=True)  4.47 us
    pallas_call x1, Pallas kernels, body(): call(stencil_kernel, 'stencil', [SMEM, SMEM, HBM, HBM] + [VMEM] * 3, (VME...  4.37 us
    ppermute x1, starting transfers between devices, body(): high = lax.ppermute(first, 'gx', backward)  3.92 us
    ppermute x1, starting transfers between devices, body(): low = lax.ppermute(last, 'gx', forward)  3.83 us
  transfers between devices with their start and end apart: 7, of which 6 were waited for; matrix products, arithmetic and copies ran while one was open for 1% of the time, Pallas kernels for 8%

profile of v4, /device:TPU:32, one launch (start us, length us, event | category | flops | bytes accessed | tf_op | source)
XLA Modules:
  0.0 86.6 jit_solution(15165556834975354244)
XLA Ops:
  0.6 2.1 %convert_element_type.3.rounded = bf16[32,64,128]{2,1,0:T(8,128)(2,1)} convert(f32[32,64,128]{2,1,0:T(8,128)} %velocity.1) | non-fusion elementwise | flops 262144 | bytes 1572864 | tf_op jit(solution)/shard_map/convert_element_type | solution.py:238
  2.7 4.5 %all-to-all-start = ((bf16[8,256,128]{2,1,0:T(8,128)(2,1)}), bf16[8,256,128]{2,1,0:T(8,128)(2,1)S(1)}, u32[]{:S(2)}, u32[]{:S(2)}) async-start(bf16[8,256,128]{2,1,0:T(8,128)(2,1)} %bitcast.3._buffer), calls=%async_computation | async-start | bytes 1048576 | tf_op jit(solution)/shard_map/all_to_all | solution.py:241
  7.2 0.0 copy-start.11
  7.2 0.0 copy-start.12
  7.2 0.0 copy-start.13
  7.2 0.0 copy-start.14
  7.3 1.0 %edge.1 = (bf16[3,64,128]{2,1,0:T(8,128)(2,1)S(1)}, bf16[3,64,128]{2,1,0:T(8,128)(2,1)S(1)}) custom-call(bf16[32,64,128]{2,1,0:T(8,128)(2,1)} %convert_element_type.3.rounded), custom_call_target="tpu_custom_call" | custom-call | flops 3000000000 | bytes 200000 | tf_op jit(solution)/shard_map/edge/pallas_call | solution.py:239
  8.2 3.8 %collective-permute-start = (bf16[3,64,128]{2,1,0:T(8,128)(2,1)S(1)}, bf16[3,64,128]{2,1,0:T(8,128)(2,1)S(1)}, u32[]{:S(2)}, u32[]{:S(2)}) collective-permute-start(bf16[3,64,128]{2,1,0:T(8,128)(2,1)S(1)} %get-tuple-element.23), channel_id=1, source_target_pairs={{0,8},{8,16},{16,24},{24,32},{32,40},{40,48},{48,56},{56,64},{64,7... | collective-permute-start | bytes 147464 | tf_op jit(solution)/shard_map/ppermute | solution.py:246
  12.1 3.9 %collective-permute-start.1 = (bf16[3,64,128]{2,1,0:T(8,128)(2,1)S(1)}, bf16[3,64,128]{2,1,0:T(8,128)(2,1)S(1)}, u32[]{:S(2)}, u32[]{:S(2)}) collective-permute-start(bf16[3,64,128]{2,1,0:T(8,128)(2,1)S(1)} %get-tuple-element.24), channel_id=1, source_target_pairs={{8,0},{16,8},{24,16},{32,24},{40,32},{48,40},{56,48},{64,56},{72,6... | collective-permute-start | bytes 147464 | tf_op jit(solution)/shard_map/ppermute | solution.py:247
  16.0 0.3 collective-permute-done.low
  16.3 1.7 %collective-permute-done.1.high = bf16[3,64,128]{2,1,0:T(8,128)(2,1)S(1)} collective-permute-done((bf16[3,64,128]{2,1,0:T(8,128)(2,1)S(1)}, bf16[3,64,128]{2,1,0:T(8,128)(2,1)S(1)}, u32[]{:S(2)}, u32[]{:S(2)}) %collective-permute-start.1) | collective-permute-done | bytes 49184 | tf_op jit(solution)/shard_map/ppermute | solution.py:247
  18.1 0.0 all-to-all-done.lines
  18.1 2.0 %span.1 = bf16[8,256,128]{2,1,0:T(8,128)(2,1)} custom-call(bf16[8,256,128]{2,1,0:T(8,128)(2,1)S(1)} %all-to-all-done.lines, f32[1,1024]{1,0:T(1,128)S(1)} %copy-done.14, bf16[8,256,128]{2,1,0:T(8,128)(2,1)} %bitcast.3._buffer, bf16[1024,256]{1,0:T(8,128)(2,1)S(1)} %copy-done.10, bf16[1024,256]{1,0:T(8,128)(2,1)S(1)} %copy-done.11, ...), custom_call_target="tpu_custom_call", output_to_operand_aliasing={{}: (2, {})} | custom-call | flops 1073741824 | bytes 3200000 | tf_op jit(solution)/shard_map/span/pallas_call | solution.py:265
  20.1 0.0 copy-start.17
  20.2 4.8 %all-to-all-start.1 = ((bf16[8,256,128]{2,1,0:T(8,128)(2,1)}), bf16[8,256,128]{2,1,0:T(8,128)(2,1)S(1)}, u32[]{:S(2)}, u32[]{:S(2)}) async-start(bf16[8,256,128]{2,1,0:T(8,128)(2,1)} %span.1), calls=%async_computation.1 | async-start | bytes 1048576 | tf_op jit(solution)/shard_map/all_to_all | solution.py:280
  25.0 0.6 add_divide_fusion
  25.5 4.4 %stencil.1 = (f32[8,64,128]{2,1,0:T(8,128)}, f32[8,64,128]{2,1,0:T(8,128)}, f32[8,64,128]{2,1,0:T(8,128)}, f32[8,64,128]{2,1,0:T(8,128)}, f32[64,128]{1,0:T(8,128)}) custom-call(f32[32]{0:T(128)} %get-tuple-element.45.keep, f32[32]{0:T(128)} %get-tuple-element.44.take, f32[32,64,128]{2,1,0:T(8,128)} %velocity.1, f32[32,64,128]{2,1,0:T(8,128)} %far_register.1, ...), custom_call_target="tpu_custom_call" | custom-call | flops 8000000 | bytes 4000000 | tf_op jit(solution)/shard_map/stencil/pallas_call | solution.py:249
  29.9 0.0 copy-start
  29.9 0.8 copy-done.7
  30.8 4.5 %all-to-all-done.1 = bf16[8,256,128]{2,1,0:T(8,128)(2,1)S(1)} async-done(((bf16[8,256,128]{2,1,0:T(8,128)(2,1)}), bf16[8,256,128]{2,1,0:T(8,128)(2,1)S(1)}, u32[]{:S(2)}, u32[]{:S(2)}) %all-to-all-start.1) | async-done | bytes 524320 | tf_op jit(solution)/shard_map/all_to_all | solution.py:280
  35.3 1.4 %offset.1._ = bf16[4,80,128]{2,1,0:T(8,128)(2,1)} custom-call(f32[32]{0:T(128)S(1)} %copy-done.8, f32[32]{0:T(128)S(1)} %copy-done.9, bf16[32,64,128]{2,1,0:T(8,128)(2,1)S(1)} %bitcast.5, bf16[32,64,128]{2,1,0:T(8,128)(2,1)S(1)} %copy-done.1, f32[64,128]{1,0:T(8,128)S(1)} %hold.1.base_offset), custom_call_target="tpu_custom_call" | custom-call | flops 1500000 | bytes 1100000 | tf_op jit(solution)/shard_map/offset/pallas_call | solution.py:282
  36.7 8.4 %all-to-all-start.2 = ((bf16[4,80,128]{2,1,0:T(8,128)(2,1)}), bf16[4,80,128]{2,1,0:T(8,128)(2,1)S(1)}, u32[]{:S(2)}, u32[]{:S(2)}) async-start(bf16[4,80,128]{2,1,0:T(8,128)(2,1)} %offset.1._), calls=%async_computation.2 | async-start | bytes 163840 | tf_op jit(solution)/shard_map/all_to_all | solution.py:299
  45.2 4.8 %all-to-all-done.2.received = bf16[4,80,128]{2,1,0:T(8,128)(2,1)S(1)} async-done(((bf16[4,80,128]{2,1,0:T(8,128)(2,1)}), bf16[4,80,128]{2,1,0:T(8,128)(2,1)S(1)}, u32[]{:S(2)}, u32[]{:S(2)}) %all-to-all-start.2) | async-done | bytes 81952 | tf_op jit(solution)/shard_map/all_to_all | solution.py:299
  49.9 0.7 fold.2
  50.6 10.3 %all-to-all-start.3 = ((bf16[4,80,128]{2,1,0:T(8,128)(2,1)}), bf16[4,80,128]{2,1,0:T(8,128)(2,1)S(1)}, u32[]{:S(2)}, u32[]{:S(2)}) async-start(bf16[4,80,128]{2,1,0:T(8,128)(2,1)} %get-tuple-element.29), calls=%async_computation.3 | async-start | bytes 163840 | tf_op jit(solution)/shard_map/all_to_all | solution.py:299
  60.9 13.5 %all-to-all-done.3.received = bf16[4,80,128]{2,1,0:T(8,128)(2,1)S(1)} async-done(((bf16[4,80,128]{2,1,0:T(8,128)(2,1)}), bf16[4,80,128]{2,1,0:T(8,128)(2,1)S(1)}, u32[]{:S(2)}, u32[]{:S(2)}) %all-to-all-start.3) | async-done | bytes 81952 | tf_op jit(solution)/shard_map/all_to_all | solution.py:299
  74.3 0.7 fold.3
  75.0 4.3 %all-to-all-start.4 = ((bf16[4,80,128]{2,1,0:T(8,128)(2,1)}), bf16[4,80,128]{2,1,0:T(8,128)(2,1)S(1)}, u32[]{:S(2)}, u32[]{:S(2)}) async-start(bf16[4,80,128]{2,1,0:T(8,128)(2,1)} %get-tuple-element.30), calls=%async_computation.4 | async-start | bytes 163840 | tf_op jit(solution)/shard_map/all_to_all | solution.py:299
  79.3 0.9 %copy-done.5 = f32[8,64,128]{2,1,0:T(8,128)S(1)} copy-done((f32[8,64,128]{2,1,0:T(8,128)S(1)}, f32[8,64,128]{2,1,0:T(8,128)}, u32[]{:S(2)}) %copy-start.5) | copy-done | bytes 262168
  80.3 1.6 %local.1 = (f32[32,64,128]{2,1,0:T(8,128)}, f32[8,64,128]{2,1,0:T(8,128)S(1)}, f32[8,64,128]{2,1,0:T(8,128)S(1)}, f32[8,64,128]{2,1,0:T(8,128)S(1)}, f32[8,64,128]{2,1,0:T(8,128)S(1)}) custom-call(f32[32]{0:T(128)S(1)} %copy-done.8, f32[32]{0:T(128)S(1)} %copy-done.9, ...), custom_call_target="tpu_custom_call", output_to_operand_aliasing={{1}: (6, {}), {2}: (7, {}), {3}: (8, {}), {4}: (9, {})} | custom-call | flops 3000000 | bytes 5000000 | tf_op jit(solution)/shard_map/local/pallas_call | solution.py:285
  81.8 3.2 %all-to-all-done.4.received = bf16[4,80,128]{2,1,0:T(8,128)(2,1)S(1)} async-done(((bf16[4,80,128]{2,1,0:T(8,128)(2,1)}), bf16[4,80,128]{2,1,0:T(8,128)(2,1)S(1)}, u32[]{:S(2)}, u32[]{:S(2)}) %all-to-all-start.4) | async-done | bytes 81952 | tf_op jit(solution)/shard_map/all_to_all | solution.py:299
  85.0 1.6 %final.1 = f32[32,64,128]{2,1,0:T(8,128)} custom-call(s32[1]{0:T(128)} %bitcast.place, f32[32]{0:T(128)S(1)} %copy-done.8, bf16[4,80,128]{2,1,0:T(8,128)(2,1)S(1)} %all-to-all-done.4.received, f32[64,128]{1,0:T(8,128)S(1)} %get-tuple-element.31.before1, f32[8,128]{1,0:T(8,128)S(1)} %get-tuple-element.32.gain1, f32[64,128]{1,0:T(8,128)S(1)} %get-tuple-element.33.before2, ...), custom_call_target="tpu_custom_call" | custom-call | flops 800000 | bytes 2300000 | tf_op jit(solution)/shard_map/final/pallas_call | solution.py:306
  (29 shorter events, 0.1 us)
Async XLA Ops:
  2.7 15.3 %all-to-all-start = ((bf16[8,256,128]{2,1,0:T(8,128)(2,1)}), bf16[8,256,128]{2,1,0:T(8,128)(2,1)S(1)}, u32[]{:S(2)}, u32[]{:S(2)}) async-start(bf16[8,256,128]{2,1,0:T(8,128)(2,1)} %bitcast.3._buffer), calls=%async_computation | async-start | bytes 1048576 | tf_op jit(solution)/shard_map/all_to_all | solution.py:241
  7.2 10.9 %copy-start.10 = (bf16[1024,256]{1,0:T(8,128)(2,1)S(1)}, bf16[1024,256]{1,0:T(8,128)(2,1)}, u32[]{:S(2)}) copy-start(bf16[1024,256]{1,0:T(8,128)(2,1)} %constant.58.clone.rest_0_) | copy-start | bytes 1572868
  7.2 10.9 %copy-start.11 = (bf16[1024,256]{1,0:T(8,128)(2,1)S(1)}, bf16[1024,256]{1,0:T(8,128)(2,1)}, u32[]{:S(2)}) copy-start(bf16[1024,256]{1,0:T(8,128)(2,1)} %constant.59.clone.rest_1_) | copy-start | bytes 1572868
  7.2 10.9 %copy-start.12 = (bf16[1024,256]{1,0:T(8,128)(2,1)S(1)}, bf16[1024,256]{1,0:T(8,128)(2,1)}, u32[]{:S(2)}) copy-start(bf16[1024,256]{1,0:T(8,128)(2,1)} %constant.60.clone.rest_2_) | copy-start | bytes 1572868
  7.2 10.9 %copy-start.13 = (bf16[1024,256]{1,0:T(8,128)(2,1)S(1)}, bf16[1024,256]{1,0:T(8,128)(2,1)}, u32[]{:S(2)}) copy-start(bf16[1024,256]{1,0:T(8,128)(2,1)} %constant.61.clone.rest_3_) | copy-start | bytes 1572868
  7.2 10.9 %copy-start.14 = (f32[1,1024]{1,0:T(1,128)S(1)}, f32[1,1024]{1,0:T(1,128)}, u32[]{:S(2)}) copy-start(f32[1,1024]{1,0:T(1,128)} %constant.62.clone.factor) | copy-start | bytes 12292
  8.2 8.1 %collective-permute-start = (bf16[3,64,128]{2,1,0:T(8,128)(2,1)S(1)}, bf16[3,64,128]{2,1,0:T(8,128)(2,1)S(1)}, u32[]{:S(2)}, u32[]{:S(2)}) collective-permute-start(bf16[3,64,128]{2,1,0:T(8,128)(2,1)S(1)} %get-tuple-element.23), channel_id=1, source_target_pairs={{0,8},{8,16},{16,24},{24,32},{32,40},{40,48},{48,56},{56,64},{64,7... | collective-permute-start | bytes 147464 | tf_op jit(solution)/shard_map/ppermute | solution.py:246
  12.1 6.0 %collective-permute-start.1 = (bf16[3,64,128]{2,1,0:T(8,128)(2,1)S(1)}, bf16[3,64,128]{2,1,0:T(8,128)(2,1)S(1)}, u32[]{:S(2)}, u32[]{:S(2)}) collective-permute-start(bf16[3,64,128]{2,1,0:T(8,128)(2,1)S(1)} %get-tuple-element.24), channel_id=1, source_target_pairs={{8,0},{16,8},{24,16},{32,24},{40,32},{48,40},{56,48},{64,56},{72,6... | collective-permute-start | bytes 147464 | tf_op jit(solution)/shard_map/ppermute | solution.py:247
  16.3 3.8 %copy-start.15 = (bf16[3,64,128]{2,1,0:T(8,128)(2,1)}, bf16[3,64,128]{2,1,0:T(8,128)(2,1)S(1)}, u32[]{:S(2)}) copy-start(bf16[3,64,128]{2,1,0:T(8,128)(2,1)S(1)} %collective-permute-done.low) | copy-start | bytes 147460
  18.1 2.1 %copy-start.16 = (bf16[3,64,128]{2,1,0:T(8,128)(2,1)}, bf16[3,64,128]{2,1,0:T(8,128)(2,1)S(1)}, u32[]{:S(2)}) copy-start(bf16[3,64,128]{2,1,0:T(8,128)(2,1)S(1)} %collective-permute-done.1.high) | copy-start | bytes 147460
  20.1 4.8 %copy-start.17 = (f32[32]{0:T(128)S(1)}, f32[32]{0:T(128)}, u32[]{:S(2)}) copy-start(f32[32]{0:T(128)} %param.13) | copy-start | bytes 388
  20.2 15.2 %all-to-all-start.1 = ((bf16[8,256,128]{2,1,0:T(8,128)(2,1)}), bf16[8,256,128]{2,1,0:T(8,128)(2,1)S(1)}, u32[]{:S(2)}, u32[]{:S(2)}) async-start(bf16[8,256,128]{2,1,0:T(8,128)(2,1)} %span.1), calls=%async_computation.1 | async-start | bytes 1048576 | tf_op jit(solution)/shard_map/all_to_all | solution.py:280
  25.5 9.8 %copy-start.1 = (bf16[32,64,128]{2,1,0:T(8,128)(2,1)S(1)}, bf16[32,64,128]{2,1,0:T(8,128)(2,1)}, u32[]{:S(2)}) copy-start(bf16[32,64,128]{2,1,0:T(8,128)(2,1)} %eddy.5) | copy-start | bytes 1572868
  25.5 9.8 %copy-start.8 = (f32[32]{0:T(128)S(1)}, f32[32]{0:T(128)}, u32[]{:S(2)}) copy-start(f32[32]{0:T(128)} %get-tuple-element.45.keep) | copy-start | bytes 388
  25.5 9.8 %copy-start.9 = (f32[32]{0:T(128)S(1)}, f32[32]{0:T(128)}, u32[]{:S(2)}) copy-start(f32[32]{0:T(128)} %get-tuple-element.44.take) | copy-start | bytes 388
  29.9 49.4 %copy-start = (f32[32,64,128]{2,1,0:T(8,128)S(1)}, f32[32,64,128]{2,1,0:T(8,128)}, u32[]{:S(2)}) copy-start(f32[32,64,128]{2,1,0:T(8,128)} %velocity.1) | copy-start | bytes 3145732
  29.9 0.8 copy-start.7
  35.3 44.0 %copy-start.4 = (f32[8,64,128]{2,1,0:T(8,128)S(1)}, f32[8,64,128]{2,1,0:T(8,128)}, u32[]{:S(2)}) copy-start(f32[8,64,128]{2,1,0:T(8,128)} %get-tuple-element.37.rest_2_) | copy-start | bytes 786436
  36.7 13.2 %all-to-all-start.2 = ((bf16[4,80,128]{2,1,0:T(8,128)(2,1)}), bf16[4,80,128]{2,1,0:T(8,128)(2,1)S(1)}, u32[]{:S(2)}, u32[]{:S(2)}) async-start(bf16[4,80,128]{2,1,0:T(8,128)(2,1)} %offset.1._), calls=%async_computation.2 | async-start | bytes 163840 | tf_op jit(solution)/shard_map/all_to_all | solution.py:299
  49.9 29.4 %copy-start.2 = (f32[8,64,128]{2,1,0:T(8,128)S(1)}, f32[8,64,128]{2,1,0:T(8,128)}, u32[]{:S(2)}) copy-start(f32[8,64,128]{2,1,0:T(8,128)} %get-tuple-element.35.rest_0_) | copy-start | bytes 786436
  49.9 29.4 %copy-start.3 = (f32[8,64,128]{2,1,0:T(8,128)S(1)}, f32[8,64,128]{2,1,0:T(8,128)}, u32[]{:S(2)}) copy-start(f32[8,64,128]{2,1,0:T(8,128)} %get-tuple-element.36.rest_1_) | copy-start | bytes 786436
  50.6 23.7 %all-to-all-start.3 = ((bf16[4,80,128]{2,1,0:T(8,128)(2,1)}), bf16[4,80,128]{2,1,0:T(8,128)(2,1)S(1)}, u32[]{:S(2)}, u32[]{:S(2)}) async-start(bf16[4,80,128]{2,1,0:T(8,128)(2,1)} %get-tuple-element.29), calls=%async_computation.3 | async-start | bytes 163840 | tf_op jit(solution)/shard_map/all_to_all | solution.py:299
  75.0 10.0 %all-to-all-start.4 = ((bf16[4,80,128]{2,1,0:T(8,128)(2,1)}), bf16[4,80,128]{2,1,0:T(8,128)(2,1)S(1)}, u32[]{:S(2)}, u32[]{:S(2)}) async-start(bf16[4,80,128]{2,1,0:T(8,128)(2,1)} %get-tuple-element.30), calls=%async_computation.4 | async-start | bytes 163840 | tf_op jit(solution)/shard_map/all_to_all | solution.py:299
  79.3 1.0 %copy-start.5 = (f32[8,64,128]{2,1,0:T(8,128)S(1)}, f32[8,64,128]{2,1,0:T(8,128)}, u32[]{:S(2)}) copy-start(f32[8,64,128]{2,1,0:T(8,128)} %get-tuple-element.38.rest_3_) | copy-start | bytes 786436
  80.3 4.7 %copy-start.6 = (f32[64,128]{1,0:T(8,128)S(1)}, f32[64,128]{1,0:T(8,128)}, u32[]{:S(2)}) copy-start(f32[64,128]{1,0:T(8,128)} %inflow.1) | copy-start | bytes 98308

commit v5 on v4

--- a/solution.py
+++ b/solution.py
@@ -1,3 +1,4 @@
+import functools
 import math
 
 import jax
@@ -25,10 +26,13 @@
 F32, BF16 = jnp.float32, jnp.bfloat16
 PAYLOAD = NY + 16
 
+SPAN_ORDER = (5, 4, 6, 7, 0, 1, 2, 3)
+ORDERS = ((3, 2, 1, 0), (2, 3, 0, 1), (2, 3, 0, 1))
+SPAN_GROUPS = [list(SPAN_ORDER)]
 GROUPS = (
-    [[x * 16 + h * 4 + l for l in range(4)] for x in range(4) for h in range(4)],
-    [[x * 16 + h * 4 + l for h in range(4)] for x in range(4) for l in range(4)],
-    [[x * 16 + z for x in range(4)] for z in range(16)],
+    [[x * 16 + h * 4 + l for l in ORDERS[0]] for x in range(4) for h in range(4)],
+    [[x * 16 + h * 4 + l for h in ORDERS[1]] for x in range(4) for l in range(4)],
+    [[x * 16 + z for x in ORDERS[2]] for z in range(16)],
 )
 
 
@@ -99,14 +103,13 @@
 def span_kernel(lines, factor, _buffer, *rest):
     slabs, out, scaled, held, sem = rest[:SLABS], *rest[SLABS:]
     step = LENGTH // SLABS
-    whole = jnp.concatenate([lines[b] for b in range(PARTS)], axis=1)
+    whole = jnp.concatenate([lines[SPAN_ORDER.index(b)] for b in range(PARTS)], axis=1)
     for n, slab in enumerate(slabs):
         part = jnp.dot(whole, slab[...], preferred_element_type=F32)
         scaled[n] = (part * factor[:, n * step : (n + 1) * step]).astype(BF16)
     wide = 256
     per = wide // WIDTH
-    blocks = [pl.ds(n * per, per) for n in range(LENGTH // wide)]
-    copies = [pltpu.make_async_copy(held.at[b], out.at[b], sem.at[n]) for n, b in enumerate(blocks)]
+    copies = [pltpu.make_async_copy(held.at[b], out.at[SPAN_ORDER.index(b)], sem.at[b]) for b in range(PARTS)]
     for n in range(LENGTH // wide):
         part = jnp.zeros((ROWS, wide), F32)
         for m, slab in enumerate(slabs):
@@ -116,7 +119,7 @@
         part = part.astype(BF16)
         for b in range(per):
             held[n * per + b] = part[:, b * WIDTH : (b + 1) * WIDTH]
-        copies[n].start()
+            copies[n * per + b].start()
     for copy in copies:
         copy.wait()
 
@@ -161,7 +164,7 @@
     held[...] = plane[...]
 
 
-def fold(place, received):
+def fold(place, received, order):
     total = jnp.zeros((NY, WIDTH), F32)
     gain = jnp.ones((8, WIDTH), F32)
     before, gain_before = total, gain
@@ -169,15 +172,16 @@
         reached = place == m
         before = jnp.where(reached, total, before)
         gain_before = jnp.where(reached, gain, gain_before)
-        tail = received[m, NY:PAYLOAD].astype(F32)
+        slot = order.index(m)
+        tail = received[slot, NY:PAYLOAD].astype(F32)
         one = tail[0:8] + tail[8:16]
-        total = total * one[0:1] + received[m, 0:NY].astype(F32)
+        total = total * one[0:1] + received[slot, 0:NY].astype(F32)
         gain = gain * one
     return before, gain_before, total, gain
 
 
-def fold_kernel(place, received, before, gain_before, out):
-    one, two, total, gain = fold(place[0], received)
+def fold_kernel(order, place, received, before, gain_before, out):
+    one, two, total, gain = fold(place[0], received, order)
     before[...] = one
     gain_before[...] = two
     store_payload(out, total, gain)
@@ -188,7 +192,7 @@
     step = STATIONS // CUTS
     cuts = [pl.ds(c * step, step) for c in range(CUTS)]
     stores = [pltpu.make_async_copy(done.at[cuts[c]], out.at[cuts[c]], sem.at[c]) for c in range(CUTS)]
-    before, gain, _, _ = fold(place[0], received)
+    before, gain, _, _ = fold(place[0], received, ORDERS[2])
     value = before + gain[0:1] * inflow[...]
     value = before2[...] + gain2[0:1] * value
     running = before1[...] + gain1[0:1] * value
@@ -238,14 +242,14 @@
     rounded = velocity.astype(BF16)
     first, last = call(edge_kernel, "edge", [HBM], (VMEM, VMEM), (EDGE, EDGE), 3_000_000_000, 200_000, (DMA((2,)),))(rounded)
     rounded = rounded.reshape(PARTS, ROWS, WIDTH)
-    lines = lax.all_to_all(rounded, "gz", 0, 0, tiled=True)
+    lines = lax.all_to_all(rounded, "gz", 0, 0, axis_index_groups=SPAN_GROUPS, tiled=True)
 
     count = lax.axis_size("gx")
     forward = [(i, i + 1) for i in range(count - 1)]
     backward = [(b, a) for a, b in forward]
     low = lax.ppermute(last, "gx", forward)
     high = lax.ppermute(first, "gx", backward)
-    lines, low, high = lax.optimization_barrier((lines, low, high))
+    lines, low, high, places[0] = lax.optimization_barrier((lines, low, high, places[0]))
     *base, base_offset = call(
         stencil_kernel,
         "stencil",
@@ -273,11 +277,11 @@
         (
             pltpu.VMEM((SLABS, ROWS, step), BF16),
             pltpu.VMEM((PARTS, ROWS, WIDTH), BF16),
-            DMA((LENGTH // 256,)),
+            DMA((PARTS,)),
         ),
         alias={2: 0},
     )(lines, jnp.asarray(factor), rounded, *slabs)
-    second = lax.all_to_all(derived, "gz", 0, 0, tiled=True).reshape(STATIONS, NY, WIDTH)
+    second = lax.all_to_all(derived, "gz", 0, 0, axis_index_groups=SPAN_GROUPS, tiled=True).reshape(STATIONS, NY, WIDTH)
 
     payload = call(offset_kernel, "offset", [SMEM, SMEM] + [VMEM] * 3, VMEM, SLOTS, 1_500_000, 1_100_000)(
         keep, take, second, eddy_viscosity, base_offset
@@ -299,7 +303,7 @@
         payload = lax.all_to_all(payload, "gx", 0, 0, axis_index_groups=GROUPS[level], tiled=True)
         if level < 2:
             before, gain, payload = call(
-                fold_kernel, "fold", [SMEM, VMEM], (VMEM,) * 3, (PLANE, GAIN, SLOTS), 200_000, 300_000
+                functools.partial(fold_kernel, ORDERS[level]), "fold", [SMEM, VMEM], (VMEM,) * 3, (PLANE, GAIN, SLOTS), 200_000, 300_000
             )(places[level], payload)
             found += [before, gain]
 

time: 87.3 us -> 76.3 us (0.87)
  the two profiles are of different devices: /device:TPU:32 before, /device:TPU:4 now
where the time goes in v5:
time: 76.3 us; the launch traced here: 75.6 us
  starting transfers between devices  40.3 us (53%)
  Pallas kernels  12.7 us (17%)
  waiting for transfers between devices  9.45 us (12%)
  blocking collectives  7.74 us (10%)
  other arithmetic  2.69 us (4%)
  local copies, waits for them, and re-layouts  1.85 us (2%)
  between operations  0.87 us (1%)
    all_to_all x2, starting transfers between devices, body(): lax.all_to_all(payload, 'gx', 0, 0, axis_index_groups=GROUPS[level], tile...  16.4 us
    ppermute x1, starting transfers between devices, body(): high = lax.ppermute(first, 'gx', backward)  9.47 us
    all_to_all x1, blocking collectives, body(): lax.all_to_all(payload, 'gx', 0, 0, axis_index_groups=GROUPS[level], tile...  7.74 us
    all_to_all x2, waiting for transfers between devices, body(): lax.all_to_all(payload, 'gx', 0, 0, axis_index_groups=GROUPS[level], tile...  6.22 us
    all_to_all x1, starting transfers between devices, body(): lax.all_to_all(rounded, 'gz', 0, 0, axis_index_groups=SPAN_GROUPS, tiled=...  6.05 us
    all_to_all x1, starting transfers between devices, body(): lax.all_to_all(derived, 'gz', 0, 0, axis_index_groups=SPAN_GROUPS, tiled=...  4.54 us
    pallas_call x1, Pallas kernels, body(): call(stencil_kernel, 'stencil', [SMEM, SMEM, HBM, HBM] + [VMEM] * 3, (VME...  4.39 us
    ppermute x1, starting transfers between devices, body(): low = lax.ppermute(last, 'gx', forward)  3.83 us
  transfers between devices with their start and end apart: 6, of which 5 were waited for; matrix products, arithmetic and copies ran while one was open for 1% of the time, Pallas kernels for 9%

profile of v5, /device:TPU:4, one launch (start us, length us, event | category | flops | bytes accessed | tf_op | source)
XLA Modules:
  0.0 75.6 jit_solution(3406929820180989670)
XLA Ops:
  0.6 2.1 %convert_element_type.3.rounded = bf16[32,64,128]{2,1,0:T(8,128)(2,1)} convert(f32[32,64,128]{2,1,0:T(8,128)} %velocity.1) | non-fusion elementwise | flops 262144 | bytes 1572864 | tf_op jit(solution)/shard_map/convert_element_type | solution.py:242
  2.7 6.0 %all-to-all-start = ((bf16[8,256,128]{2,1,0:T(8,128)(2,1)}), bf16[8,256,128]{2,1,0:T(8,128)(2,1)S(1)}, u32[]{:S(2)}, u32[]{:S(2)}) async-start(bf16[8,256,128]{2,1,0:T(8,128)(2,1)} %bitcast.2._buffer), calls=%async_computation | async-start | bytes 1048576 | tf_op jit(solution)/shard_map/all_to_all | solution.py:245
  8.8 0.0 copy-start.13
  8.8 1.0 %edge.1 = (bf16[3,64,128]{2,1,0:T(8,128)(2,1)S(1)}, bf16[3,64,128]{2,1,0:T(8,128)(2,1)S(1)}) custom-call(bf16[32,64,128]{2,1,0:T(8,128)(2,1)} %convert_element_type.3.rounded), custom_call_target="tpu_custom_call" | custom-call | flops 3000000000 | bytes 200000 | tf_op jit(solution)/shard_map/edge/pallas_call | solution.py:243
  9.8 3.8 %collective-permute-start = (bf16[3,64,128]{2,1,0:T(8,128)(2,1)S(1)}, bf16[3,64,128]{2,1,0:T(8,128)(2,1)S(1)}, u32[]{:S(2)}, u32[]{:S(2)}) collective-permute-start(bf16[3,64,128]{2,1,0:T(8,128)(2,1)S(1)} %get-tuple-element.24), channel_id=1, source_target_pairs={{0,8},{8,16},{16,24},{24,32},{32,40},{40,48},{48,56},{56,64},{64,7... | collective-permute-start | bytes 147464 | tf_op jit(solution)/shard_map/ppermute | solution.py:250
  13.6 9.5 %collective-permute-start.1 = (bf16[3,64,128]{2,1,0:T(8,128)(2,1)S(1)}, bf16[3,64,128]{2,1,0:T(8,128)(2,1)S(1)}, u32[]{:S(2)}, u32[]{:S(2)}) collective-permute-start(bf16[3,64,128]{2,1,0:T(8,128)(2,1)S(1)} %get-tuple-element.25), channel_id=1, source_target_pairs={{8,0},{16,8},{24,16},{32,24},{40,32},{48,40},{56,48},{64,56},{72,6... | collective-permute-start | bytes 147464 | tf_op jit(solution)/shard_map/ppermute | solution.py:251
  23.1 0.0 copy-start.14
  23.1 0.1 collective-permute-done.low
  23.2 1.6 %collective-permute-done.1.high = bf16[3,64,128]{2,1,0:T(8,128)(2,1)S(1)} collective-permute-done((bf16[3,64,128]{2,1,0:T(8,128)(2,1)S(1)}, bf16[3,64,128]{2,1,0:T(8,128)(2,1)S(1)}, u32[]{:S(2)}, u32[]{:S(2)}) %collective-permute-start.1) | collective-permute-done | bytes 49184 | tf_op jit(solution)/shard_map/ppermute | solution.py:251
  24.8 0.0 all-to-all-done.lines
  24.9 0.0 copy-done.10
  24.9 2.0 %span.1 = bf16[8,256,128]{2,1,0:T(8,128)(2,1)} custom-call(bf16[8,256,128]{2,1,0:T(8,128)(2,1)S(1)} %all-to-all-done.lines, f32[1,1024]{1,0:T(1,128)S(1)} %copy-done.14, bf16[8,256,128]{2,1,0:T(8,128)(2,1)} %bitcast.2._buffer, bf16[1024,256]{1,0:T(8,128)(2,1)S(1)} %copy-done.10, bf16[1024,256]{1,0:T(8,128)(2,1)S(1)} %copy-done.11, ...), custom_call_target="tpu_custom_call", output_to_operand_aliasing={{}: (2, {})} | custom-call | flops 1073741824 | bytes 3200000 | tf_op jit(solution)/shard_map/span/pallas_call | solution.py:269
  26.9 0.0 copy-start.17
  27.0 4.5 %all-to-all-start.1 = ((bf16[8,256,128]{2,1,0:T(8,128)(2,1)}), bf16[8,256,128]{2,1,0:T(8,128)(2,1)S(1)}, u32[]{:S(2)}, u32[]{:S(2)}) async-start(bf16[8,256,128]{2,1,0:T(8,128)(2,1)} %span.1), calls=%async_computation.1 | async-start | bytes 1048576 | tf_op jit(solution)/shard_map/all_to_all | solution.py:284
  31.5 0.0 copy-done.17
  31.5 0.6 add_divide_fusion
  32.1 4.4 %stencil.1 = (f32[8,64,128]{2,1,0:T(8,128)}, f32[8,64,128]{2,1,0:T(8,128)}, f32[8,64,128]{2,1,0:T(8,128)}, f32[8,64,128]{2,1,0:T(8,128)}, f32[64,128]{1,0:T(8,128)}) custom-call(f32[32]{0:T(128)} %get-tuple-element.47.keep, f32[32]{0:T(128)} %get-tuple-element.46.take, f32[32,64,128]{2,1,0:T(8,128)} %velocity.1, f32[32,64,128]{2,1,0:T(8,128)} %far_register.1, ...), custom_call_target="tpu_custom_call" | custom-call | flops 8000000 | bytes 4000000 | tf_op jit(solution)/shard_map/stencil/pallas_call | solution.py:253
  36.5 0.0 copy-start
  36.5 0.8 %copy-done.7 = f32[64,128]{1,0:T(8,128)S(1)} copy-done((f32[64,128]{1,0:T(8,128)S(1)}, f32[64,128]{1,0:T(8,128)}, u32[]{:S(2)}) %copy-start.7) | copy-done | bytes 32792
  37.4 1.5 %all-to-all-done.1 = bf16[8,256,128]{2,1,0:T(8,128)(2,1)S(1)} async-done(((bf16[8,256,128]{2,1,0:T(8,128)(2,1)}), bf16[8,256,128]{2,1,0:T(8,128)(2,1)S(1)}, u32[]{:S(2)}, u32[]{:S(2)}) %all-to-all-start.1) | async-done | bytes 524320 | tf_op jit(solution)/shard_map/all_to_all | solution.py:284
  38.9 0.8 %offset.1._ = bf16[4,80,128]{2,1,0:T(8,128)(2,1)S(1)} custom-call(f32[32]{0:T(128)S(1)} %copy-done.8, f32[32]{0:T(128)S(1)} %copy-done.9, bf16[32,64,128]{2,1,0:T(8,128)(2,1)S(1)} %bitcast.5, bf16[32,64,128]{2,1,0:T(8,128)(2,1)S(1)} %copy-done.1, f32[64,128]{1,0:T(8,128)S(1)} %hold.1.base_offset), custom_call_target="tpu_custom_call" | custom-call | flops 1500000 | bytes 1100000 | tf_op jit(solution)/shard_map/offset/pallas_call | solution.py:286
  39.7 7.7 %all_to_all.25.received = bf16[4,80,128]{2,1,0:T(8,128)(2,1)S(1)} all-to-all(bf16[4,80,128]{2,1,0:T(8,128)(2,1)S(1)} %offset.1._), channel_id=1, replica_groups={{24,16,8,0},{56,48,40,32},{88,80,72,64},{120,112,104,96},{152,144,136,1..., dimensions={0} | all-to-all | bytes 163840 | tf_op jit(solution)/shard_map/all_to_all | solution.py:303
  47.4 0.7 fold.2
  48.1 13.1 %all-to-all-start.3 = ((bf16[4,80,128]{2,1,0:T(8,128)(2,1)}), bf16[4,80,128]{2,1,0:T(8,128)(2,1)S(1)}, u32[]{:S(2)}, u32[]{:S(2)}) async-start(bf16[4,80,128]{2,1,0:T(8,128)(2,1)} %get-tuple-element.31), calls=%async_computation.3 | async-start | bytes 163840 | tf_op jit(solution)/shard_map/all_to_all | solution.py:303
  61.2 3.1 %all-to-all-done.3.received = bf16[4,80,128]{2,1,0:T(8,128)(2,1)S(1)} async-done(((bf16[4,80,128]{2,1,0:T(8,128)(2,1)}), bf16[4,80,128]{2,1,0:T(8,128)(2,1)S(1)}, u32[]{:S(2)}, u32[]{:S(2)}) %all-to-all-start.3) | async-done | bytes 81952 | tf_op jit(solution)/shard_map/all_to_all | solution.py:303
  64.4 0.7 fold.3
  65.0 3.3 %all-to-all-start.4 = ((bf16[4,80,128]{2,1,0:T(8,128)(2,1)}), bf16[4,80,128]{2,1,0:T(8,128)(2,1)S(1)}, u32[]{:S(2)}, u32[]{:S(2)}) async-start(bf16[4,80,128]{2,1,0:T(8,128)(2,1)} %get-tuple-element.32), calls=%async_computation.4 | async-start | bytes 163840 | tf_op jit(solution)/shard_map/all_to_all | solution.py:303
  68.3 0.0 copy-done
  68.4 0.9 %copy-done.5 = f32[8,64,128]{2,1,0:T(8,128)S(1)} copy-done((f32[8,64,128]{2,1,0:T(8,128)S(1)}, f32[8,64,128]{2,1,0:T(8,128)}, u32[]{:S(2)}) %copy-start.5) | copy-done | bytes 262168
  69.3 1.6 %local.1 = (f32[32,64,128]{2,1,0:T(8,128)}, f32[8,64,128]{2,1,0:T(8,128)S(1)}, f32[8,64,128]{2,1,0:T(8,128)S(1)}, f32[8,64,128]{2,1,0:T(8,128)S(1)}, f32[8,64,128]{2,1,0:T(8,128)S(1)}) custom-call(f32[32]{0:T(128)S(1)} %copy-done.8, f32[32]{0:T(128)S(1)} %copy-done.9, ...), custom_call_target="tpu_custom_call", output_to_operand_aliasing={{1}: (6, {}), {2}: (7, {}), {3}: (8, {}), {4}: (9, {})} | custom-call | flops 3000000 | bytes 5000000 | tf_op jit(solution)/shard_map/local/pallas_call | solution.py:289
  70.9 3.1 %all-to-all-done.4.received = bf16[4,80,128]{2,1,0:T(8,128)(2,1)S(1)} async-done(((bf16[4,80,128]{2,1,0:T(8,128)(2,1)}), bf16[4,80,128]{2,1,0:T(8,128)(2,1)S(1)}, u32[]{:S(2)}, u32[]{:S(2)}) %all-to-all-start.4) | async-done | bytes 81952 | tf_op jit(solution)/shard_map/all_to_all | solution.py:303
  74.0 1.6 %final.1 = f32[32,64,128]{2,1,0:T(8,128)} custom-call(s32[1]{0:T(128)} %bitcast.place, f32[32]{0:T(128)S(1)} %copy-done.8, bf16[4,80,128]{2,1,0:T(8,128)(2,1)S(1)} %all-to-all-done.4.received, f32[64,128]{1,0:T(8,128)S(1)} %get-tuple-element.33.before1, f32[8,128]{1,0:T(8,128)S(1)} %get-tuple-element.34.gain1, f32[64,128]{1,0:T(8,128)S(1)} %get-tuple-element.35.before2, ...), custom_call_target="tpu_custom_call" | custom-call | flops 800000 | bytes 2300000 | tf_op jit(solution)/shard_map/final/pallas_call | solution.py:310
  (28 shorter events, 0.1 us)
Async XLA Ops:
  2.7 22.1 %all-to-all-start = ((bf16[8,256,128]{2,1,0:T(8,128)(2,1)}), bf16[8,256,128]{2,1,0:T(8,128)(2,1)S(1)}, u32[]{:S(2)}, u32[]{:S(2)}) async-start(bf16[8,256,128]{2,1,0:T(8,128)(2,1)} %bitcast.2._buffer), calls=%async_computation | async-start | bytes 1048576 | tf_op jit(solution)/shard_map/all_to_all | solution.py:245
  8.8 16.1 %copy-start.10 = (bf16[1024,256]{1,0:T(8,128)(2,1)S(1)}, bf16[1024,256]{1,0:T(8,128)(2,1)}, u32[]{:S(2)}) copy-start(bf16[1024,256]{1,0:T(8,128)(2,1)} %constant.58.clone.rest_0_) | copy-start | bytes 1572868
  8.8 16.1 %copy-start.11 = (bf16[1024,256]{1,0:T(8,128)(2,1)S(1)}, bf16[1024,256]{1,0:T(8,128)(2,1)}, u32[]{:S(2)}) copy-start(bf16[1024,256]{1,0:T(8,128)(2,1)} %constant.59.clone.rest_1_) | copy-start | bytes 1572868
  8.8 16.1 %copy-start.12 = (bf16[1024,256]{1,0:T(8,128)(2,1)S(1)}, bf16[1024,256]{1,0:T(8,128)(2,1)}, u32[]{:S(2)}) copy-start(bf16[1024,256]{1,0:T(8,128)(2,1)} %constant.60.clone.rest_2_) | copy-start | bytes 1572868
  8.8 16.1 %copy-start.13 = (bf16[1024,256]{1,0:T(8,128)(2,1)S(1)}, bf16[1024,256]{1,0:T(8,128)(2,1)}, u32[]{:S(2)}) copy-start(bf16[1024,256]{1,0:T(8,128)(2,1)} %constant.61.clone.rest_3_) | copy-start | bytes 1572868
  9.8 13.4 %collective-permute-start = (bf16[3,64,128]{2,1,0:T(8,128)(2,1)S(1)}, bf16[3,64,128]{2,1,0:T(8,128)(2,1)S(1)}, u32[]{:S(2)}, u32[]{:S(2)}) collective-permute-start(bf16[3,64,128]{2,1,0:T(8,128)(2,1)S(1)} %get-tuple-element.24), channel_id=1, source_target_pairs={{0,8},{8,16},{16,24},{24,32},{32,40},{40,48},{48,56},{56,64},{64,7... | collective-permute-start | bytes 147464 | tf_op jit(solution)/shard_map/ppermute | solution.py:250
  13.6 11.2 %collective-permute-start.1 = (bf16[3,64,128]{2,1,0:T(8,128)(2,1)S(1)}, bf16[3,64,128]{2,1,0:T(8,128)(2,1)S(1)}, u32[]{:S(2)}, u32[]{:S(2)}) collective-permute-start(bf16[3,64,128]{2,1,0:T(8,128)(2,1)S(1)} %get-tuple-element.25), channel_id=1, source_target_pairs={{8,0},{16,8},{24,16},{32,24},{40,32},{48,40},{56,48},{64,56},{72,6... | collective-permute-start | bytes 147464 | tf_op jit(solution)/shard_map/ppermute | solution.py:251
  23.1 1.8 %copy-start.14 = (f32[1,1024]{1,0:T(1,128)S(1)}, f32[1,1024]{1,0:T(1,128)}, u32[]{:S(2)}) copy-start(f32[1,1024]{1,0:T(1,128)} %constant.62.clone.factor) | copy-start | bytes 12292
  23.2 3.7 %copy-start.15 = (bf16[3,64,128]{2,1,0:T(8,128)(2,1)}, bf16[3,64,128]{2,1,0:T(8,128)(2,1)S(1)}, u32[]{:S(2)}) copy-start(bf16[3,64,128]{2,1,0:T(8,128)(2,1)S(1)} %collective-permute-done.low) | copy-start | bytes 147460
  24.8 2.1 %copy-start.16 = (bf16[3,64,128]{2,1,0:T(8,128)(2,1)}, bf16[3,64,128]{2,1,0:T(8,128)(2,1)S(1)}, u32[]{:S(2)}) copy-start(bf16[3,64,128]{2,1,0:T(8,128)(2,1)S(1)} %collective-permute-done.1.high) | copy-start | bytes 147460
  26.9 4.5 %copy-start.17 = (f32[32]{0:T(128)S(1)}, f32[32]{0:T(128)}, u32[]{:S(2)}) copy-start(f32[32]{0:T(128)} %param.13) | copy-start | bytes 388
  27.0 11.9 %all-to-all-start.1 = ((bf16[8,256,128]{2,1,0:T(8,128)(2,1)}), bf16[8,256,128]{2,1,0:T(8,128)(2,1)S(1)}, u32[]{:S(2)}, u32[]{:S(2)}) async-start(bf16[8,256,128]{2,1,0:T(8,128)(2,1)} %span.1), calls=%async_computation.1 | async-start | bytes 1048576 | tf_op jit(solution)/shard_map/all_to_all | solution.py:284
  32.1 6.8 %copy-start.1 = (bf16[32,64,128]{2,1,0:T(8,128)(2,1)S(1)}, bf16[32,64,128]{2,1,0:T(8,128)(2,1)}, u32[]{:S(2)}) copy-start(bf16[32,64,128]{2,1,0:T(8,128)(2,1)} %eddy.5) | copy-start | bytes 1572868
  32.1 6.8 %copy-start.8 = (f32[32]{0:T(128)S(1)}, f32[32]{0:T(128)}, u32[]{:S(2)}) copy-start(f32[32]{0:T(128)} %get-tuple-element.47.keep) | copy-start | bytes 388
  32.1 6.8 %copy-start.9 = (f32[32]{0:T(128)S(1)}, f32[32]{0:T(128)}, u32[]{:S(2)}) copy-start(f32[32]{0:T(128)} %get-tuple-element.46.take) | copy-start | bytes 388
  36.5 31.9 %copy-start = (f32[32,64,128]{2,1,0:T(8,128)S(1)}, f32[32,64,128]{2,1,0:T(8,128)}, u32[]{:S(2)}) copy-start(f32[32,64,128]{2,1,0:T(8,128)} %velocity.1) | copy-start | bytes 3145732
  36.5 0.8 %copy-start.7 = (f32[64,128]{1,0:T(8,128)S(1)}, f32[64,128]{1,0:T(8,128)}, u32[]{:S(2)}) copy-start(f32[64,128]{1,0:T(8,128)} %get-tuple-element.30.plane) | copy-start | bytes 98308
  38.9 29.5 %copy-start.4 = (f32[8,64,128]{2,1,0:T(8,128)S(1)}, f32[8,64,128]{2,1,0:T(8,128)}, u32[]{:S(2)}) copy-start(f32[8,64,128]{2,1,0:T(8,128)} %get-tuple-element.39.rest_2_) | copy-start | bytes 786436
  47.4 20.9 %copy-start.2 = (f32[8,64,128]{2,1,0:T(8,128)S(1)}, f32[8,64,128]{2,1,0:T(8,128)}, u32[]{:S(2)}) copy-start(f32[8,64,128]{2,1,0:T(8,128)} %get-tuple-element.37.rest_0_) | copy-start | bytes 786436
  47.4 20.9 %copy-start.3 = (f32[8,64,128]{2,1,0:T(8,128)S(1)}, f32[8,64,128]{2,1,0:T(8,128)}, u32[]{:S(2)}) copy-start(f32[8,64,128]{2,1,0:T(8,128)} %get-tuple-element.38.rest_1_) | copy-start | bytes 786436
  48.1 16.3 %all-to-all-start.3 = ((bf16[4,80,128]{2,1,0:T(8,128)(2,1)}), bf16[4,80,128]{2,1,0:T(8,128)(2,1)S(1)}, u32[]{:S(2)}, u32[]{:S(2)}) async-start(bf16[4,80,128]{2,1,0:T(8,128)(2,1)} %get-tuple-element.31), calls=%async_computation.3 | async-start | bytes 163840 | tf_op jit(solution)/shard_map/all_to_all | solution.py:303
  65.0 9.0 %all-to-all-start.4 = ((bf16[4,80,128]{2,1,0:T(8,128)(2,1)}), bf16[4,80,128]{2,1,0:T(8,128)(2,1)S(1)}, u32[]{:S(2)}, u32[]{:S(2)}) async-start(bf16[4,80,128]{2,1,0:T(8,128)(2,1)} %get-tuple-element.32), calls=%async_computation.4 | async-start | bytes 163840 | tf_op jit(solution)/shard_map/all_to_all | solution.py:303
  68.4 1.0 %copy-start.5 = (f32[8,64,128]{2,1,0:T(8,128)S(1)}, f32[8,64,128]{2,1,0:T(8,128)}, u32[]{:S(2)}) copy-start(f32[8,64,128]{2,1,0:T(8,128)} %get-tuple-element.40.rest_3_) | copy-start | bytes 786436
  69.3 4.7 %copy-start.6 = (f32[64,128]{1,0:T(8,128)S(1)}, f32[64,128]{1,0:T(8,128)}, u32[]{:S(2)}) copy-start(f32[64,128]{1,0:T(8,128)} %inflow.1) | copy-start | bytes 98308

commit v6 on v5

--- a/solution.py
+++ b/solution.py
@@ -249,7 +249,9 @@
     backward = [(b, a) for a, b in forward]
     low = lax.ppermute(last, "gx", forward)
     high = lax.ppermute(first, "gx", backward)
-    lines, low, high, places[0] = lax.optimization_barrier((lines, low, high, places[0]))
+    lines, low, high, places[0], places[1] = lax.optimization_barrier(
+        (lines, low, high, places[0], places[1])
+    )
     *base, base_offset = call(
         stencil_kernel,
         "stencil",

time: 76.3 us -> 75.7 us (level)
  blocking collectives: 7.74 us -> 24.1 us
  starting transfers between devices: 40.3 us -> 27.2 us
  waiting for transfers between devices: 9.45 us -> 6.3 us
    all_to_all x1 -> x2, blocking collectives: 7.74 us -> 24.1 us  [body(): lax.all_to_all(payload, 'gx', 0, 0, axis_index_groups=GROUPS[level], tile...]
    all_to_all x2 -> x1, starting transfers between devices: 16.4 us -> 3.29 us  [body(): lax.all_to_all(payload, 'gx', 0, 0, axis_index_groups=GROUPS[level], tile...]
    all_to_all x2 -> x1, waiting for transfers between devices: 6.22 us -> 3.09 us  [body(): lax.all_to_all(payload, 'gx', 0, 0, axis_index_groups=GROUPS[level], tile...]
  transfers between devices with their start and end apart: 6 -> 5, of which waited for: 5 -> 4; matrix products, arithmetic and copies ran while one was open for 1% -> 1% of each run, Pallas kernels for 9% -> 9%
where the time goes in v6:
time: 75.7 us; the launch traced here: 75 us
  starting transfers between devices  27.2 us (36%)
  blocking collectives  24.1 us (32%)
  Pallas kernels  12 us (16%)
  waiting for transfers between devices  6.3 us (8%)
  other arithmetic  2.69 us (4%)
  local copies, waits for them, and re-layouts  1.85 us (2%)
  between operations  0.9 us (1%)
    all_to_all x2, blocking collectives, body(): lax.all_to_all(payload, 'gx', 0, 0, axis_index_groups=GROUPS[level], tile...  24.1 us
    ppermute x1, starting transfers between devices, body(): high = lax.ppermute(first, 'gx', backward)  9.47 us
    all_to_all x1, starting transfers between devices, body(): lax.all_to_all(rounded, 'gz', 0, 0, axis_index_groups=SPAN_GROUPS, tiled=...  6.05 us
    all_to_all x1, starting transfers between devices, body(): lax.all_to_all(derived, 'gz', 0, 0, axis_index_groups=SPAN_GROUPS, tiled=...  4.54 us
    pallas_call x1, Pallas kernels, body(): call(stencil_kernel, 'stencil', [SMEM, SMEM, HBM, HBM] + [VMEM] * 3, (VME...  4.39 us
    ppermute x1, starting transfers between devices, body(): low = lax.ppermute(last, 'gx', forward)  3.83 us
    all_to_all x1, starting transfers between devices, body(): lax.all_to_all(payload, 'gx', 0, 0, axis_index_groups=GROUPS[level], tile...  3.29 us
    all_to_all x1, waiting for transfers between devices, body(): lax.all_to_all(payload, 'gx', 0, 0, axis_index_groups=GROUPS[level], tile...  3.09 us
  transfers between devices with their start and end apart: 5, of which 4 were waited for; matrix products, arithmetic and copies ran while one was open for 1% of the time, Pallas kernels for 9%

profile of v6, /device:TPU:4, one launch (start us, length us, event | category | flops | bytes accessed | tf_op | source)
XLA Modules:
  0.0 75.0 jit_solution(14770595754503890865)
XLA Ops:
  0.6 2.1 %convert_element_type.3.rounded = bf16[32,64,128]{2,1,0:T(8,128)(2,1)} convert(f32[32,64,128]{2,1,0:T(8,128)} %velocity.1) | non-fusion elementwise | flops 262144 | bytes 1572864 | tf_op jit(solution)/shard_map/convert_element_type | solution.py:242
  2.7 6.0 %all-to-all-start = ((bf16[8,256,128]{2,1,0:T(8,128)(2,1)}), bf16[8,256,128]{2,1,0:T(8,128)(2,1)S(1)}, u32[]{:S(2)}, u32[]{:S(2)}) async-start(bf16[8,256,128]{2,1,0:T(8,128)(2,1)} %bitcast.1._buffer), calls=%async_computation | async-start | bytes 1048576 | tf_op jit(solution)/shard_map/all_to_all | solution.py:245
  8.8 0.0 copy-start.13
  8.8 1.0 %edge.1 = (bf16[3,64,128]{2,1,0:T(8,128)(2,1)S(1)}, bf16[3,64,128]{2,1,0:T(8,128)(2,1)S(1)}) custom-call(bf16[32,64,128]{2,1,0:T(8,128)(2,1)} %convert_element_type.3.rounded), custom_call_target="tpu_custom_call" | custom-call | flops 3000000000 | bytes 200000 | tf_op jit(solution)/shard_map/edge/pallas_call | solution.py:243
  9.8 3.8 %collective-permute-start = (bf16[3,64,128]{2,1,0:T(8,128)(2,1)S(1)}, bf16[3,64,128]{2,1,0:T(8,128)(2,1)S(1)}, u32[]{:S(2)}, u32[]{:S(2)}) collective-permute-start(bf16[3,64,128]{2,1,0:T(8,128)(2,1)S(1)} %get-tuple-element.25), channel_id=1, source_target_pairs={{0,8},{8,16},{16,24},{24,32},{32,40},{40,48},{48,56},{56,64},{64,7... | collective-permute-start | bytes 147464 | tf_op jit(solution)/shard_map/ppermute | solution.py:250
  13.6 9.5 %collective-permute-start.1 = (bf16[3,64,128]{2,1,0:T(8,128)(2,1)S(1)}, bf16[3,64,128]{2,1,0:T(8,128)(2,1)S(1)}, u32[]{:S(2)}, u32[]{:S(2)}) collective-permute-start(bf16[3,64,128]{2,1,0:T(8,128)(2,1)S(1)} %get-tuple-element.26), channel_id=1, source_target_pairs={{8,0},{16,8},{24,16},{32,24},{40,32},{48,40},{56,48},{64,56},{72,6... | collective-permute-start | bytes 147464 | tf_op jit(solution)/shard_map/ppermute | solution.py:251
  23.1 0.0 copy-start.14
  23.2 0.1 collective-permute-done.low
  23.2 1.6 %collective-permute-done.1.high = bf16[3,64,128]{2,1,0:T(8,128)(2,1)S(1)} collective-permute-done((bf16[3,64,128]{2,1,0:T(8,128)(2,1)S(1)}, bf16[3,64,128]{2,1,0:T(8,128)(2,1)S(1)}, u32[]{:S(2)}, u32[]{:S(2)}) %collective-permute-start.1) | collective-permute-done | bytes 49184 | tf_op jit(solution)/shard_map/ppermute | solution.py:251
  24.8 0.0 all-to-all-done.lines
  24.9 0.0 copy-done.10
  24.9 0.0 copy-done.11
  24.9 2.0 %span.1 = bf16[8,256,128]{2,1,0:T(8,128)(2,1)} custom-call(bf16[8,256,128]{2,1,0:T(8,128)(2,1)S(1)} %all-to-all-done.lines, f32[1,1024]{1,0:T(1,128)S(1)} %copy-done.14, bf16[8,256,128]{2,1,0:T(8,128)(2,1)} %bitcast.1._buffer, bf16[1024,256]{1,0:T(8,128)(2,1)S(1)} %copy-done.10, bf16[1024,256]{1,0:T(8,128)(2,1)S(1)} %copy-done.11, ...), custom_call_target="tpu_custom_call", output_to_operand_aliasing={{}: (2, {})} | custom-call | flops 1073741824 | bytes 3200000 | tf_op jit(solution)/shard_map/span/pallas_call | solution.py:271
  26.9 0.0 copy-done.15
  26.9 0.0 copy-done.16
  26.9 0.0 copy-start.17
  27.0 4.5 %all-to-all-start.1 = ((bf16[8,256,128]{2,1,0:T(8,128)(2,1)}), bf16[8,256,128]{2,1,0:T(8,128)(2,1)S(1)}, u32[]{:S(2)}, u32[]{:S(2)}) async-start(bf16[8,256,128]{2,1,0:T(8,128)(2,1)} %span.1), calls=%async_computation.1 | async-start | bytes 1048576 | tf_op jit(solution)/shard_map/all_to_all | solution.py:286
  31.5 0.6 add_divide_fusion
  32.1 4.4 %stencil.1 = (f32[8,64,128]{2,1,0:T(8,128)}, f32[8,64,128]{2,1,0:T(8,128)}, f32[8,64,128]{2,1,0:T(8,128)}, f32[8,64,128]{2,1,0:T(8,128)}, f32[64,128]{1,0:T(8,128)}) custom-call(f32[32]{0:T(128)} %get-tuple-element.49.keep, f32[32]{0:T(128)} %get-tuple-element.48.take, f32[32,64,128]{2,1,0:T(8,128)} %velocity.1, f32[32,64,128]{2,1,0:T(8,128)} %far_register.1, ...), custom_call_target="tpu_custom_call" | custom-call | flops 8000000 | bytes 4000000 | tf_op jit(solution)/shard_map/stencil/pallas_call | solution.py:255
  36.5 0.0 copy-start
  36.5 0.8 %copy-done.7 = f32[64,128]{1,0:T(8,128)S(1)} copy-done((f32[64,128]{1,0:T(8,128)S(1)}, f32[64,128]{1,0:T(8,128)}, u32[]{:S(2)}) %copy-start.7) | copy-done | bytes 32792
  37.3 1.5 %all-to-all-done.1 = bf16[8,256,128]{2,1,0:T(8,128)(2,1)S(1)} async-done(((bf16[8,256,128]{2,1,0:T(8,128)(2,1)}), bf16[8,256,128]{2,1,0:T(8,128)(2,1)S(1)}, u32[]{:S(2)}, u32[]{:S(2)}) %all-to-all-start.1) | async-done | bytes 524320 | tf_op jit(solution)/shard_map/all_to_all | solution.py:286
  38.9 0.0 copy-done.9
  38.9 0.8 %offset.1._ = bf16[4,80,128]{2,1,0:T(8,128)(2,1)S(1)} custom-call(f32[32]{0:T(128)S(1)} %copy-done.8, f32[32]{0:T(128)S(1)} %copy-done.9, bf16[32,64,128]{2,1,0:T(8,128)(2,1)S(1)} %bitcast.5, bf16[32,64,128]{2,1,0:T(8,128)(2,1)S(1)} %copy-done.1, f32[64,128]{1,0:T(8,128)S(1)} %hold.1.base_offset), custom_call_target="tpu_custom_call" | custom-call | flops 1500000 | bytes 1100000 | tf_op jit(solution)/shard_map/offset/pallas_call | solution.py:288
  39.7 7.9 %all_to_all.25.received = bf16[4,80,128]{2,1,0:T(8,128)(2,1)S(1)} all-to-all(bf16[4,80,128]{2,1,0:T(8,128)(2,1)S(1)} %offset.1._), channel_id=1, replica_groups={{24,16,8,0},{56,48,40,32},{88,80,72,64},{120,112,104,96},{152,144,136,1..., dimensions={0} | all-to-all | bytes 163840 | tf_op jit(solution)/shard_map/all_to_all | solution.py:305
  47.6 16.2 %all_to_all.26.received = bf16[4,80,128]{2,1,0:T(8,128)(2,1)S(1)} all-to-all(bf16[4,80,128]{2,1,0:T(8,128)(2,1)S(1)} %get-tuple-element.33), channel_id=1, replica_groups={{64,96,0,32},{72,104,8,40},{80,112,16,48},{88,120,24,56},{192,224,128,1..., dimensions={0} | all-to-all | bytes 163840 | tf_op jit(solution)/shard_map/all_to_all | solution.py:305
  63.8 0.7 fold.3
  64.5 3.3 %all-to-all-start.4 = ((bf16[4,80,128]{2,1,0:T(8,128)(2,1)}), bf16[4,80,128]{2,1,0:T(8,128)(2,1)S(1)}, u32[]{:S(2)}, u32[]{:S(2)}) async-start(bf16[4,80,128]{2,1,0:T(8,128)(2,1)} %get-tuple-element.34), calls=%async_computation.4 | async-start | bytes 163840 | tf_op jit(solution)/shard_map/all_to_all | solution.py:305
  67.8 0.9 %copy-done.5 = f32[8,64,128]{2,1,0:T(8,128)S(1)} copy-done((f32[8,64,128]{2,1,0:T(8,128)S(1)}, f32[8,64,128]{2,1,0:T(8,128)}, u32[]{:S(2)}) %copy-start.5) | copy-done | bytes 262168
  68.8 1.6 %local.1 = (f32[32,64,128]{2,1,0:T(8,128)}, f32[8,64,128]{2,1,0:T(8,128)S(1)}, f32[8,64,128]{2,1,0:T(8,128)S(1)}, f32[8,64,128]{2,1,0:T(8,128)S(1)}, f32[8,64,128]{2,1,0:T(8,128)S(1)}) custom-call(f32[32]{0:T(128)S(1)} %copy-done.8, f32[32]{0:T(128)S(1)} %copy-done.9, ...), custom_call_target="tpu_custom_call", output_to_operand_aliasing={{1}: (6, {}), {2}: (7, {}), {3}: (8, {}), {4}: (9, {})} | custom-call | flops 3000000 | bytes 5000000 | tf_op jit(solution)/shard_map/local/pallas_call | solution.py:291
  70.4 3.1 %all-to-all-done.4.received = bf16[4,80,128]{2,1,0:T(8,128)(2,1)S(1)} async-done(((bf16[4,80,128]{2,1,0:T(8,128)(2,1)}), bf16[4,80,128]{2,1,0:T(8,128)(2,1)S(1)}, u32[]{:S(2)}, u32[]{:S(2)}) %all-to-all-start.4) | async-done | bytes 81952 | tf_op jit(solution)/shard_map/all_to_all | solution.py:305
  73.5 1.6 %final.1 = f32[32,64,128]{2,1,0:T(8,128)} custom-call(s32[1]{0:T(128)} %bitcast.place, f32[32]{0:T(128)S(1)} %copy-done.8, bf16[4,80,128]{2,1,0:T(8,128)(2,1)S(1)} %all-to-all-done.4.received, f32[64,128]{1,0:T(8,128)S(1)} %get-tuple-element.35.before1, f32[8,128]{1,0:T(8,128)S(1)} %get-tuple-element.36.gain1, f32[64,128]{1,0:T(8,128)S(1)} %get-tuple-element.37.before2, ...), custom_call_target="tpu_custom_call" | custom-call | flops 800000 | bytes 2300000 | tf_op jit(solution)/shard_map/final/pallas_call | solution.py:312
  (27 shorter events, 0.1 us)
Async XLA Ops:
  2.7 22.1 %all-to-all-start = ((bf16[8,256,128]{2,1,0:T(8,128)(2,1)}), bf16[8,256,128]{2,1,0:T(8,128)(2,1)S(1)}, u32[]{:S(2)}, u32[]{:S(2)}) async-start(bf16[8,256,128]{2,1,0:T(8,128)(2,1)} %bitcast.1._buffer), calls=%async_computation | async-start | bytes 1048576 | tf_op jit(solution)/shard_map/all_to_all | solution.py:245
  8.8 16.1 %copy-start.10 = (bf16[1024,256]{1,0:T(8,128)(2,1)S(1)}, bf16[1024,256]{1,0:T(8,128)(2,1)}, u32[]{:S(2)}) copy-start(bf16[1024,256]{1,0:T(8,128)(2,1)} %constant.58.clone.rest_0_) | copy-start | bytes 1572868
  8.8 16.1 %copy-start.11 = (bf16[1024,256]{1,0:T(8,128)(2,1)S(1)}, bf16[1024,256]{1,0:T(8,128)(2,1)}, u32[]{:S(2)}) copy-start(bf16[1024,256]{1,0:T(8,128)(2,1)} %constant.59.clone.rest_1_) | copy-start | bytes 1572868
  8.8 16.1 %copy-start.12 = (bf16[1024,256]{1,0:T(8,128)(2,1)S(1)}, bf16[1024,256]{1,0:T(8,128)(2,1)}, u32[]{:S(2)}) copy-start(bf16[1024,256]{1,0:T(8,128)(2,1)} %constant.60.clone.rest_2_) | copy-start | bytes 1572868
  8.8 16.1 %copy-start.13 = (bf16[1024,256]{1,0:T(8,128)(2,1)S(1)}, bf16[1024,256]{1,0:T(8,128)(2,1)}, u32[]{:S(2)}) copy-start(bf16[1024,256]{1,0:T(8,128)(2,1)} %constant.61.clone.rest_3_) | copy-start | bytes 1572868
  9.8 13.4 %collective-permute-start = (bf16[3,64,128]{2,1,0:T(8,128)(2,1)S(1)}, bf16[3,64,128]{2,1,0:T(8,128)(2,1)S(1)}, u32[]{:S(2)}, u32[]{:S(2)}) collective-permute-start(bf16[3,64,128]{2,1,0:T(8,128)(2,1)S(1)} %get-tuple-element.25), channel_id=1, source_target_pairs={{0,8},{8,16},{16,24},{24,32},{32,40},{40,48},{48,56},{56,64},{64,7... | collective-permute-start | bytes 147464 | tf_op jit(solution)/shard_map/ppermute | solution.py:250
  13.6 11.2 %collective-permute-start.1 = (bf16[3,64,128]{2,1,0:T(8,128)(2,1)S(1)}, bf16[3,64,128]{2,1,0:T(8,128)(2,1)S(1)}, u32[]{:S(2)}, u32[]{:S(2)}) collective-permute-start(bf16[3,64,128]{2,1,0:T(8,128)(2,1)S(1)} %get-tuple-element.26), channel_id=1, source_target_pairs={{8,0},{16,8},{24,16},{32,24},{40,32},{48,40},{56,48},{64,56},{72,6... | collective-permute-start | bytes 147464 | tf_op jit(solution)/shard_map/ppermute | solution.py:251
  23.1 1.7 %copy-start.14 = (f32[1,1024]{1,0:T(1,128)S(1)}, f32[1,1024]{1,0:T(1,128)}, u32[]{:S(2)}) copy-start(f32[1,1024]{1,0:T(1,128)} %constant.62.clone.factor) | copy-start | bytes 12292
  23.2 3.7 %copy-start.15 = (bf16[3,64,128]{2,1,0:T(8,128)(2,1)}, bf16[3,64,128]{2,1,0:T(8,128)(2,1)S(1)}, u32[]{:S(2)}) copy-start(bf16[3,64,128]{2,1,0:T(8,128)(2,1)S(1)} %collective-permute-done.low) | copy-start | bytes 147460
  24.8 2.1 %copy-start.16 = (bf16[3,64,128]{2,1,0:T(8,128)(2,1)}, bf16[3,64,128]{2,1,0:T(8,128)(2,1)S(1)}, u32[]{:S(2)}) copy-start(bf16[3,64,128]{2,1,0:T(8,128)(2,1)S(1)} %collective-permute-done.1.high) | copy-start | bytes 147460
  26.9 4.5 %copy-start.17 = (f32[32]{0:T(128)S(1)}, f32[32]{0:T(128)}, u32[]{:S(2)}) copy-start(f32[32]{0:T(128)} %param.13) | copy-start | bytes 388
  27.0 11.9 %all-to-all-start.1 = ((bf16[8,256,128]{2,1,0:T(8,128)(2,1)}), bf16[8,256,128]{2,1,0:T(8,128)(2,1)S(1)}, u32[]{:S(2)}, u32[]{:S(2)}) async-start(bf16[8,256,128]{2,1,0:T(8,128)(2,1)} %span.1), calls=%async_computation.1 | async-start | bytes 1048576 | tf_op jit(solution)/shard_map/all_to_all | solution.py:286
  32.1 6.8 %copy-start.1 = (bf16[32,64,128]{2,1,0:T(8,128)(2,1)S(1)}, bf16[32,64,128]{2,1,0:T(8,128)(2,1)}, u32[]{:S(2)}) copy-start(bf16[32,64,128]{2,1,0:T(8,128)(2,1)} %eddy.5) | copy-start | bytes 1572868
  32.1 6.8 %copy-start.8 = (f32[32]{0:T(128)S(1)}, f32[32]{0:T(128)}, u32[]{:S(2)}) copy-start(f32[32]{0:T(128)} %get-tuple-element.49.keep) | copy-start | bytes 388
  32.1 6.8 %copy-start.9 = (f32[32]{0:T(128)S(1)}, f32[32]{0:T(128)}, u32[]{:S(2)}) copy-start(f32[32]{0:T(128)} %get-tuple-element.48.take) | copy-start | bytes 388
  36.5 31.3 %copy-start = (f32[32,64,128]{2,1,0:T(8,128)S(1)}, f32[32,64,128]{2,1,0:T(8,128)}, u32[]{:S(2)}) copy-start(f32[32,64,128]{2,1,0:T(8,128)} %velocity.1) | copy-start | bytes 3145732
  36.5 0.8 %copy-start.7 = (f32[64,128]{1,0:T(8,128)S(1)}, f32[64,128]{1,0:T(8,128)}, u32[]{:S(2)}) copy-start(f32[64,128]{1,0:T(8,128)} %get-tuple-element.32.plane) | copy-start | bytes 98308
  38.9 28.9 %copy-start.4 = (f32[8,64,128]{2,1,0:T(8,128)S(1)}, f32[8,64,128]{2,1,0:T(8,128)}, u32[]{:S(2)}) copy-start(f32[8,64,128]{2,1,0:T(8,128)} %get-tuple-element.41.rest_2_) | copy-start | bytes 786436
  39.7 28.1 %copy-start.3 = (f32[8,64,128]{2,1,0:T(8,128)S(1)}, f32[8,64,128]{2,1,0:T(8,128)}, u32[]{:S(2)}) copy-start(f32[8,64,128]{2,1,0:T(8,128)} %get-tuple-element.40.rest_1_) | copy-start | bytes 786436
  47.6 20.2 %copy-start.2 = (f32[8,64,128]{2,1,0:T(8,128)S(1)}, f32[8,64,128]{2,1,0:T(8,128)}, u32[]{:S(2)}) copy-start(f32[8,64,128]{2,1,0:T(8,128)} %get-tuple-element.39.rest_0_) | copy-start | bytes 786436
  64.5 9.0 %all-to-all-start.4 = ((bf16[4,80,128]{2,1,0:T(8,128)(2,1)}), bf16[4,80,128]{2,1,0:T(8,128)(2,1)S(1)}, u32[]{:S(2)}, u32[]{:S(2)}) async-start(bf16[4,80,128]{2,1,0:T(8,128)(2,1)} %get-tuple-element.34), calls=%async_computation.4 | async-start | bytes 163840 | tf_op jit(solution)/shard_map/all_to_all | solution.py:305
  67.8 1.0 %copy-start.5 = (f32[8,64,128]{2,1,0:T(8,128)S(1)}, f32[8,64,128]{2,1,0:T(8,128)}, u32[]{:S(2)}) copy-start(f32[8,64,128]{2,1,0:T(8,128)} %get-tuple-element.42.rest_3_) | copy-start | bytes 786436
  68.8 4.7 %copy-start.6 = (f32[64,128]{1,0:T(8,128)S(1)}, f32[64,128]{1,0:T(8,128)}, u32[]{:S(2)}) copy-start(f32[64,128]{1,0:T(8,128)} %inflow.1) | copy-start | bytes 98308

commit v7 on v6

--- a/solution.py
+++ b/solution.py
@@ -27,7 +27,7 @@
 PAYLOAD = NY + 16
 
 SPAN_ORDER = (5, 4, 6, 7, 0, 1, 2, 3)
-ORDERS = ((3, 2, 1, 0), (2, 3, 0, 1), (2, 3, 0, 1))
+ORDERS = ((3, 2, 1, 0), (2, 3, 0, 1), (3, 2, 0, 1))
 SPAN_GROUPS = [list(SPAN_ORDER)]
 GROUPS = (
     [[x * 16 + h * 4 + l for l in ORDERS[0]] for x in range(4) for h in range(4)],

time: 75.7 us -> 76 us (level)
  the two profiles are of different devices: /device:TPU:4 before, /device:TPU:32 now
where the time goes in v7:
time: 76 us; the launch traced here: 75.4 us
  blocking collectives  29.2 us (38%)
  starting transfers between devices  23.8 us (31%)
  Pallas kernels  12 us (16%)
  waiting for transfers between devices  5 us (7%)
  other arithmetic  2.69 us (4%)
  local copies, waits for them, and re-layouts  1.85 us (2%)
  between operations  0.87 us (1%)
    all_to_all x2, blocking collectives, body(): lax.all_to_all(payload, 'gx', 0, 0, axis_index_groups=GROUPS[level], tile...  29.2 us
    all_to_all x1, starting transfers between devices, body(): lax.all_to_all(rounded, 'gz', 0, 0, axis_index_groups=SPAN_GROUPS, tiled=...  6.05 us
    all_to_all x1, starting transfers between devices, body(): lax.all_to_all(payload, 'gx', 0, 0, axis_index_groups=GROUPS[level], tile...  6.02 us
    all_to_all x1, starting transfers between devices, body(): lax.all_to_all(derived, 'gz', 0, 0, axis_index_groups=SPAN_GROUPS, tiled=...  4.54 us
    pallas_call x1, Pallas kernels, body(): call(stencil_kernel, 'stencil', [SMEM, SMEM, HBM, HBM] + [VMEM] * 3, (VME...  4.39 us
    ppermute x1, starting transfers between devices, body(): low = lax.ppermute(last, 'gx', forward)  3.83 us
    ppermute x1, starting transfers between devices, body(): high = lax.ppermute(first, 'gx', backward)  3.33 us
    ppermute x1, waiting for transfers between devices, body(): high = lax.ppermute(first, 'gx', backward)  2.52 us
  transfers between devices with their start and end apart: 5, of which 4 were waited for; matrix products, arithmetic and copies ran while one was open for 1% of the time, Pallas kernels for 9%

profile of v7, /device:TPU:32, one launch (start us, length us, event | category | flops | bytes accessed | tf_op | source)
XLA Modules:
  0.0 75.4 jit_solution(1150483657669648391)
XLA Ops:
  0.6 2.1 %convert_element_type.3.rounded = bf16[32,64,128]{2,1,0:T(8,128)(2,1)} convert(f32[32,64,128]{2,1,0:T(8,128)} %velocity.1) | non-fusion elementwise | flops 262144 | bytes 1572864 | tf_op jit(solution)/shard_map/convert_element_type | solution.py:242
  2.7 6.0 %all-to-all-start = ((bf16[8,256,128]{2,1,0:T(8,128)(2,1)}), bf16[8,256,128]{2,1,0:T(8,128)(2,1)S(1)}, u32[]{:S(2)}, u32[]{:S(2)}) async-start(bf16[8,256,128]{2,1,0:T(8,128)(2,1)} %bitcast.1._buffer), calls=%async_computation | async-start | bytes 1048576 | tf_op jit(solution)/shard_map/all_to_all | solution.py:245
  8.8 0.0 copy-start.13
  8.8 1.0 %edge.1 = (bf16[3,64,128]{2,1,0:T(8,128)(2,1)S(1)}, bf16[3,64,128]{2,1,0:T(8,128)(2,1)S(1)}) custom-call(bf16[32,64,128]{2,1,0:T(8,128)(2,1)} %convert_element_type.3.rounded), custom_call_target="tpu_custom_call" | custom-call | flops 3000000000 | bytes 200000 | tf_op jit(solution)/shard_map/edge/pallas_call | solution.py:243
  9.8 3.8 %collective-permute-start = (bf16[3,64,128]{2,1,0:T(8,128)(2,1)S(1)}, bf16[3,64,128]{2,1,0:T(8,128)(2,1)S(1)}, u32[]{:S(2)}, u32[]{:S(2)}) collective-permute-start(bf16[3,64,128]{2,1,0:T(8,128)(2,1)S(1)} %get-tuple-element.25), channel_id=1, source_target_pairs={{0,8},{8,16},{16,24},{24,32},{32,40},{40,48},{48,56},{56,64},{64,7... | collective-permute-start | bytes 147464 | tf_op jit(solution)/shard_map/ppermute | solution.py:250
  13.6 3.3 %collective-permute-start.1 = (bf16[3,64,128]{2,1,0:T(8,128)(2,1)S(1)}, bf16[3,64,128]{2,1,0:T(8,128)(2,1)S(1)}, u32[]{:S(2)}, u32[]{:S(2)}) collective-permute-start(bf16[3,64,128]{2,1,0:T(8,128)(2,1)S(1)} %get-tuple-element.26), channel_id=1, source_target_pairs={{8,0},{16,8},{24,16},{32,24},{40,32},{48,40},{56,48},{64,56},{72,6... | collective-permute-start | bytes 147464 | tf_op jit(solution)/shard_map/ppermute | solution.py:251
  17.0 0.0 copy-start.14
  17.0 0.1 collective-permute-done.low
  17.1 2.5 %collective-permute-done.1.high = bf16[3,64,128]{2,1,0:T(8,128)(2,1)S(1)} collective-permute-done((bf16[3,64,128]{2,1,0:T(8,128)(2,1)S(1)}, bf16[3,64,128]{2,1,0:T(8,128)(2,1)S(1)}, u32[]{:S(2)}, u32[]{:S(2)}) %collective-permute-start.1) | collective-permute-done | bytes 49184 | tf_op jit(solution)/shard_map/ppermute | solution.py:251
  19.6 0.0 all-to-all-done.lines
  19.6 0.0 copy-done.10
  19.7 2.0 %span.1 = bf16[8,256,128]{2,1,0:T(8,128)(2,1)} custom-call(bf16[8,256,128]{2,1,0:T(8,128)(2,1)S(1)} %all-to-all-done.lines, f32[1,1024]{1,0:T(1,128)S(1)} %copy-done.14, bf16[8,256,128]{2,1,0:T(8,128)(2,1)} %bitcast.1._buffer, bf16[1024,256]{1,0:T(8,128)(2,1)S(1)} %copy-done.10, bf16[1024,256]{1,0:T(8,128)(2,1)S(1)} %copy-done.11, ...), custom_call_target="tpu_custom_call", output_to_operand_aliasing={{}: (2, {})} | custom-call | flops 1073741824 | bytes 3200000 | tf_op jit(solution)/shard_map/span/pallas_call | solution.py:271
  21.7 0.0 copy-start.17
  21.7 4.5 %all-to-all-start.1 = ((bf16[8,256,128]{2,1,0:T(8,128)(2,1)}), bf16[8,256,128]{2,1,0:T(8,128)(2,1)S(1)}, u32[]{:S(2)}, u32[]{:S(2)}) async-start(bf16[8,256,128]{2,1,0:T(8,128)(2,1)} %span.1), calls=%async_computation.1 | async-start | bytes 1048576 | tf_op jit(solution)/shard_map/all_to_all | solution.py:286
  26.3 0.6 add_divide_fusion
  26.9 4.4 %stencil.1 = (f32[8,64,128]{2,1,0:T(8,128)}, f32[8,64,128]{2,1,0:T(8,128)}, f32[8,64,128]{2,1,0:T(8,128)}, f32[8,64,128]{2,1,0:T(8,128)}, f32[64,128]{1,0:T(8,128)}) custom-call(f32[32]{0:T(128)} %get-tuple-element.49.keep, f32[32]{0:T(128)} %get-tuple-element.48.take, f32[32,64,128]{2,1,0:T(8,128)} %velocity.1, f32[32,64,128]{2,1,0:T(8,128)} %far_register.1, ...), custom_call_target="tpu_custom_call" | custom-call | flops 8000000 | bytes 4000000 | tf_op jit(solution)/shard_map/stencil/pallas_call | solution.py:255
  31.3 0.0 copy-start
  31.3 0.0 copy-start.7
  31.3 0.8 %copy-done.7 = f32[64,128]{1,0:T(8,128)S(1)} copy-done((f32[64,128]{1,0:T(8,128)S(1)}, f32[64,128]{1,0:T(8,128)}, u32[]{:S(2)}) %copy-start.7) | copy-done | bytes 32792
  32.1 1.5 %all-to-all-done.1 = bf16[8,256,128]{2,1,0:T(8,128)(2,1)S(1)} async-done(((bf16[8,256,128]{2,1,0:T(8,128)(2,1)}), bf16[8,256,128]{2,1,0:T(8,128)(2,1)S(1)}, u32[]{:S(2)}, u32[]{:S(2)}) %all-to-all-start.1) | async-done | bytes 524320 | tf_op jit(solution)/shard_map/all_to_all | solution.py:286
  33.7 0.0 copy-done.8
  33.7 0.8 %offset.1._ = bf16[4,80,128]{2,1,0:T(8,128)(2,1)S(1)} custom-call(f32[32]{0:T(128)S(1)} %copy-done.8, f32[32]{0:T(128)S(1)} %copy-done.9, bf16[32,64,128]{2,1,0:T(8,128)(2,1)S(1)} %bitcast.5, bf16[32,64,128]{2,1,0:T(8,128)(2,1)S(1)} %copy-done.1, f32[64,128]{1,0:T(8,128)S(1)} %hold.1.base_offset), custom_call_target="tpu_custom_call" | custom-call | flops 1500000 | bytes 1100000 | tf_op jit(solution)/shard_map/offset/pallas_call | solution.py:288
  34.5 11.8 %all_to_all.25.received = bf16[4,80,128]{2,1,0:T(8,128)(2,1)S(1)} all-to-all(bf16[4,80,128]{2,1,0:T(8,128)(2,1)S(1)} %offset.1._), channel_id=1, replica_groups={{24,16,8,0},{56,48,40,32},{88,80,72,64},{120,112,104,96},{152,144,136,1..., dimensions={0} | all-to-all | bytes 163840 | tf_op jit(solution)/shard_map/all_to_all | solution.py:305
  46.4 17.4 %all_to_all.26.received = bf16[4,80,128]{2,1,0:T(8,128)(2,1)S(1)} all-to-all(bf16[4,80,128]{2,1,0:T(8,128)(2,1)S(1)} %get-tuple-element.33), channel_id=1, replica_groups={{64,96,0,32},{72,104,8,40},{80,112,16,48},{88,120,24,56},{192,224,128,1..., dimensions={0} | all-to-all | bytes 163840 | tf_op jit(solution)/shard_map/all_to_all | solution.py:305
  63.7 0.7 fold.3
  64.4 6.0 %all-to-all-start.4 = ((bf16[4,80,128]{2,1,0:T(8,128)(2,1)}), bf16[4,80,128]{2,1,0:T(8,128)(2,1)S(1)}, u32[]{:S(2)}, u32[]{:S(2)}) async-start(bf16[4,80,128]{2,1,0:T(8,128)(2,1)} %get-tuple-element.34), calls=%async_computation.4 | async-start | bytes 163840 | tf_op jit(solution)/shard_map/all_to_all | solution.py:305
  70.4 0.0 copy-done
  70.4 0.9 %copy-done.5 = f32[8,64,128]{2,1,0:T(8,128)S(1)} copy-done((f32[8,64,128]{2,1,0:T(8,128)S(1)}, f32[8,64,128]{2,1,0:T(8,128)}, u32[]{:S(2)}) %copy-start.5) | copy-done | bytes 262168
  71.4 1.6 %local.1 = (f32[32,64,128]{2,1,0:T(8,128)}, f32[8,64,128]{2,1,0:T(8,128)S(1)}, f32[8,64,128]{2,1,0:T(8,128)S(1)}, f32[8,64,128]{2,1,0:T(8,128)S(1)}, f32[8,64,128]{2,1,0:T(8,128)S(1)}) custom-call(f32[32]{0:T(128)S(1)} %copy-done.8, f32[32]{0:T(128)S(1)} %copy-done.9, ...), custom_call_target="tpu_custom_call", output_to_operand_aliasing={{1}: (6, {}), {2}: (7, {}), {3}: (8, {}), {4}: (9, {})} | custom-call | flops 3000000 | bytes 5000000 | tf_op jit(solution)/shard_map/local/pallas_call | solution.py:291
  73.0 0.9 %all-to-all-done.4.received = bf16[4,80,128]{2,1,0:T(8,128)(2,1)S(1)} async-done(((bf16[4,80,128]{2,1,0:T(8,128)(2,1)}), bf16[4,80,128]{2,1,0:T(8,128)(2,1)S(1)}, u32[]{:S(2)}, u32[]{:S(2)}) %all-to-all-start.4) | async-done | bytes 81952 | tf_op jit(solution)/shard_map/all_to_all | solution.py:305
  73.8 0.0 copy-done.6
  73.8 1.6 %final.1 = f32[32,64,128]{2,1,0:T(8,128)} custom-call(s32[1]{0:T(128)} %bitcast.place, f32[32]{0:T(128)S(1)} %copy-done.8, bf16[4,80,128]{2,1,0:T(8,128)(2,1)S(1)} %all-to-all-done.4.received, f32[64,128]{1,0:T(8,128)S(1)} %get-tuple-element.35.before1, f32[8,128]{1,0:T(8,128)S(1)} %get-tuple-element.36.gain1, f32[64,128]{1,0:T(8,128)S(1)} %get-tuple-element.37.before2, ...), custom_call_target="tpu_custom_call" | custom-call | flops 800000 | bytes 2300000 | tf_op jit(solution)/shard_map/final/pallas_call | solution.py:312
  (27 shorter events, 0.1 us)
Async XLA Ops:
  2.7 16.9 %all-to-all-start = ((bf16[8,256,128]{2,1,0:T(8,128)(2,1)}), bf16[8,256,128]{2,1,0:T(8,128)(2,1)S(1)}, u32[]{:S(2)}, u32[]{:S(2)}) async-start(bf16[8,256,128]{2,1,0:T(8,128)(2,1)} %bitcast.1._buffer), calls=%async_computation | async-start | bytes 1048576 | tf_op jit(solution)/shard_map/all_to_all | solution.py:245
  8.8 10.8 %copy-start.10 = (bf16[1024,256]{1,0:T(8,128)(2,1)S(1)}, bf16[1024,256]{1,0:T(8,128)(2,1)}, u32[]{:S(2)}) copy-start(bf16[1024,256]{1,0:T(8,128)(2,1)} %constant.58.clone.rest_0_) | copy-start | bytes 1572868
  8.8 10.8 %copy-start.11 = (bf16[1024,256]{1,0:T(8,128)(2,1)S(1)}, bf16[1024,256]{1,0:T(8,128)(2,1)}, u32[]{:S(2)}) copy-start(bf16[1024,256]{1,0:T(8,128)(2,1)} %constant.59.clone.rest_1_) | copy-start | bytes 1572868
  8.8 10.9 %copy-start.12 = (bf16[1024,256]{1,0:T(8,128)(2,1)S(1)}, bf16[1024,256]{1,0:T(8,128)(2,1)}, u32[]{:S(2)}) copy-start(bf16[1024,256]{1,0:T(8,128)(2,1)} %constant.60.clone.rest_2_) | copy-start | bytes 1572868
  8.8 10.9 %copy-start.13 = (bf16[1024,256]{1,0:T(8,128)(2,1)S(1)}, bf16[1024,256]{1,0:T(8,128)(2,1)}, u32[]{:S(2)}) copy-start(bf16[1024,256]{1,0:T(8,128)(2,1)} %constant.61.clone.rest_3_) | copy-start | bytes 1572868
  9.8 7.3 %collective-permute-start = (bf16[3,64,128]{2,1,0:T(8,128)(2,1)S(1)}, bf16[3,64,128]{2,1,0:T(8,128)(2,1)S(1)}, u32[]{:S(2)}, u32[]{:S(2)}) collective-permute-start(bf16[3,64,128]{2,1,0:T(8,128)(2,1)S(1)} %get-tuple-element.25), channel_id=1, source_target_pairs={{0,8},{8,16},{16,24},{24,32},{32,40},{40,48},{48,56},{56,64},{64,7... | collective-permute-start | bytes 147464 | tf_op jit(solution)/shard_map/ppermute | solution.py:250
  13.6 6.0 %collective-permute-start.1 = (bf16[3,64,128]{2,1,0:T(8,128)(2,1)S(1)}, bf16[3,64,128]{2,1,0:T(8,128)(2,1)S(1)}, u32[]{:S(2)}, u32[]{:S(2)}) collective-permute-start(bf16[3,64,128]{2,1,0:T(8,128)(2,1)S(1)} %get-tuple-element.26), channel_id=1, source_target_pairs={{8,0},{16,8},{24,16},{32,24},{40,32},{48,40},{56,48},{64,56},{72,6... | collective-permute-start | bytes 147464 | tf_op jit(solution)/shard_map/ppermute | solution.py:251
  17.0 2.7 %copy-start.14 = (f32[1,1024]{1,0:T(1,128)S(1)}, f32[1,1024]{1,0:T(1,128)}, u32[]{:S(2)}) copy-start(f32[1,1024]{1,0:T(1,128)} %constant.62.clone.factor) | copy-start | bytes 12292
  17.1 4.6 %copy-start.15 = (bf16[3,64,128]{2,1,0:T(8,128)(2,1)}, bf16[3,64,128]{2,1,0:T(8,128)(2,1)S(1)}, u32[]{:S(2)}) copy-start(bf16[3,64,128]{2,1,0:T(8,128)(2,1)S(1)} %collective-permute-done.low) | copy-start | bytes 147460
  19.6 2.1 %copy-start.16 = (bf16[3,64,128]{2,1,0:T(8,128)(2,1)}, bf16[3,64,128]{2,1,0:T(8,128)(2,1)S(1)}, u32[]{:S(2)}) copy-start(bf16[3,64,128]{2,1,0:T(8,128)(2,1)S(1)} %collective-permute-done.1.high) | copy-start | bytes 147460
  21.7 4.5 %copy-start.17 = (f32[32]{0:T(128)S(1)}, f32[32]{0:T(128)}, u32[]{:S(2)}) copy-start(f32[32]{0:T(128)} %param.13) | copy-start | bytes 388
  21.7 11.9 %all-to-all-start.1 = ((bf16[8,256,128]{2,1,0:T(8,128)(2,1)}), bf16[8,256,128]{2,1,0:T(8,128)(2,1)S(1)}, u32[]{:S(2)}, u32[]{:S(2)}) async-start(bf16[8,256,128]{2,1,0:T(8,128)(2,1)} %span.1), calls=%async_computation.1 | async-start | bytes 1048576 | tf_op jit(solution)/shard_map/all_to_all | solution.py:286
  26.9 6.8 %copy-start.1 = (bf16[32,64,128]{2,1,0:T(8,128)(2,1)S(1)}, bf16[32,64,128]{2,1,0:T(8,128)(2,1)}, u32[]{:S(2)}) copy-start(bf16[32,64,128]{2,1,0:T(8,128)(2,1)} %eddy.5) | copy-start | bytes 1572868
  26.9 6.8 %copy-start.8 = (f32[32]{0:T(128)S(1)}, f32[32]{0:T(128)}, u32[]{:S(2)}) copy-start(f32[32]{0:T(128)} %get-tuple-element.49.keep) | copy-start | bytes 388
  26.9 6.8 %copy-start.9 = (f32[32]{0:T(128)S(1)}, f32[32]{0:T(128)}, u32[]{:S(2)}) copy-start(f32[32]{0:T(128)} %get-tuple-element.48.take) | copy-start | bytes 388
  31.3 39.1 %copy-start = (f32[32,64,128]{2,1,0:T(8,128)S(1)}, f32[32,64,128]{2,1,0:T(8,128)}, u32[]{:S(2)}) copy-start(f32[32,64,128]{2,1,0:T(8,128)} %velocity.1) | copy-start | bytes 3145732
  31.3 0.8 %copy-start.7 = (f32[64,128]{1,0:T(8,128)S(1)}, f32[64,128]{1,0:T(8,128)}, u32[]{:S(2)}) copy-start(f32[64,128]{1,0:T(8,128)} %get-tuple-element.32.plane) | copy-start | bytes 98308
  33.7 36.7 %copy-start.4 = (f32[8,64,128]{2,1,0:T(8,128)S(1)}, f32[8,64,128]{2,1,0:T(8,128)}, u32[]{:S(2)}) copy-start(f32[8,64,128]{2,1,0:T(8,128)} %get-tuple-element.41.rest_2_) | copy-start | bytes 786436
  34.5 35.9 %copy-start.3 = (f32[8,64,128]{2,1,0:T(8,128)S(1)}, f32[8,64,128]{2,1,0:T(8,128)}, u32[]{:S(2)}) copy-start(f32[8,64,128]{2,1,0:T(8,128)} %get-tuple-element.40.rest_1_) | copy-start | bytes 786436
  46.3 24.1 %copy-start.2 = (f32[8,64,128]{2,1,0:T(8,128)S(1)}, f32[8,64,128]{2,1,0:T(8,128)}, u32[]{:S(2)}) copy-start(f32[8,64,128]{2,1,0:T(8,128)} %get-tuple-element.39.rest_0_) | copy-start | bytes 786436
  64.4 9.4 %all-to-all-start.4 = ((bf16[4,80,128]{2,1,0:T(8,128)(2,1)}), bf16[4,80,128]{2,1,0:T(8,128)(2,1)S(1)}, u32[]{:S(2)}, u32[]{:S(2)}) async-start(bf16[4,80,128]{2,1,0:T(8,128)(2,1)} %get-tuple-element.34), calls=%async_computation.4 | async-start | bytes 163840 | tf_op jit(solution)/shard_map/all_to_all | solution.py:305
  70.4 1.0 %copy-start.5 = (f32[8,64,128]{2,1,0:T(8,128)S(1)}, f32[8,64,128]{2,1,0:T(8,128)}, u32[]{:S(2)}) copy-start(f32[8,64,128]{2,1,0:T(8,128)} %get-tuple-element.42.rest_3_) | copy-start | bytes 786436
  71.4 2.5 %copy-start.6 = (f32[64,128]{1,0:T(8,128)S(1)}, f32[64,128]{1,0:T(8,128)}, u32[]{:S(2)}) copy-start(f32[64,128]{1,0:T(8,128)} %inflow.1) | copy-start | bytes 98308
